TPU v7x, 32 devices: a whole 2x2x4 slice. The times are simulated.
32 devices in a mesh: tm: 8 (over z, x), tile: 4 (over y, core).
Axes of the slice: x: 2, y: 2, z: 4, core: 2. Of those that a mesh axis runs over, the one named last changes fastest.
Arguments:
- features: bfloat16 [8, 8, 160, 512], P('tm', 'tile'), may hold values from -200 to 200, as said below
- norm_gain: float32 [512], replicated, may hold values from 0.1 to 1.9
- query_weight: bfloat16 [512, 512], replicated, may hold values from -7.9991455 to 7.9991455, as said below
- key_weight: bfloat16 [512, 512], replicated, may hold values from -0.25 to 0.25
- value_weight: bfloat16 [512, 512], replicated, may hold values from -0.25 to 0.25
- out_weight: bfloat16 [512, 512], replicated, may hold values from -0.5 to 0.5
- conv_weight: bfloat16 [3, 3, 3, 512, 256], replicated, may hold values from -0.0546875 to 0.0546875
- skip_weight: bfloat16 [512, 256], replicated, may hold values from -0.125 to 0.125
Outputs:
- decoded: bfloat16 [16, 8, 160, 256], P('tm', 'tile')
Inputs may be any that keep to these rules, and one draw needn't show every extreme that they name: Latent features whose magnitude varies from row to row and column to column. `query_weight`: A dense projection matrix.
All inputs are finite; a program needn't handle non-finite values.
Results may differ from a plain program's by a relative error of at most 0.012.
The roundings to bfloat16 on the way count: a program that leaves them out, or rounds other values in their place, can miss the bound.
Values may be sent and summed in bfloat16 or wider, within the bound.
No kernel may reach another device: no remote copies, remote signals or barrier semaphores. Data moves between devices by JAX's collectives and lax.ppermute only.
A program may use at most 128 MiB of HBM per device.

v0:
```python
import jax
import jax.numpy as jnp
from jax import lax
from jax.sharding import PartitionSpec as P

GROUPS = 32


def shifted(array, axis, by):
    devices = lax.axis_size(axis)
    pairs = [(i, i + by) for i in range(devices) if 0 <= i + by < devices]
    return lax.ppermute(array, axis, pairs)


def padded_2(block, sides, width):
    for axis, dim in sides:
        count = lax.axis_size(axis)
        forward = [(i, i + 1) for i in range(count - 1)]
        backward = [(target, source) for source, target in forward]
        low = lax.ppermute(
            lax.slice_in_dim(block, block.shape[dim] - width, None, axis=dim), axis, forward
        )
        high = lax.ppermute(lax.slice_in_dim(block, 0, width, axis=dim), axis, backward)
        block = jnp.concatenate([low, block, high], axis=dim)
    return block


def per_device(
    features,
    norm_gain,
    query_weight,
    key_weight,
    value_weight,
    out_weight,
    conv_weight,
    skip_weight,
):
    frames, tile_rows, tile_cols, channels = features.shape
    cell_count = tile_rows * tile_cols
    group_width = channels // GROUPS
    grouped = features.astype(jnp.float32).reshape(frames, cell_count, GROUPS, group_width)
    total, squared = lax.psum(
        (jnp.sum(grouped, axis=(1, 3)), jnp.sum(grouped * grouped, axis=(1, 3))), "tile"
    )
    population = lax.axis_size("tile") * cell_count * group_width
    mean = (total / population)[:, None, :, None]
    var = (squared / population)[:, None, :, None] - mean * mean
    normed = ((grouped - mean) * lax.rsqrt(var + 1e-06)).reshape(
        frames, cell_count, channels
    ) * norm_gain
    normed = normed.astype(jnp.bfloat16)
    queries = jnp.einsum(
        "fnc,cd->fnd", normed, query_weight, preferred_element_type=jnp.float32
    ).astype(jnp.bfloat16)
    key_local = jnp.einsum(
        "fnc,cd->fnd", normed, key_weight, preferred_element_type=jnp.float32
    ).astype(jnp.bfloat16)
    value_local = jnp.einsum(
        "fnc,cd->fnd", normed, value_weight, preferred_element_type=jnp.float32
    ).astype(jnp.bfloat16)
    key_rows, value_rows = (
        lax.all_gather(key_local, "tile", axis=1, tiled=True),
        lax.all_gather(value_local, "tile", axis=1, tiled=True),
    )
    scores = jnp.einsum(
        "fqc,fkc->fqk", queries, key_rows, preferred_element_type=jnp.float32
    ) * channels ** (-0.5)
    peak = jnp.max(scores, axis=2, keepdims=True)
    unnormed = jnp.exp(scores - peak)
    denominator = jnp.sum(unnormed, axis=2, keepdims=True)
    weights = unnormed.astype(jnp.bfloat16)
    attended = (
        jnp.einsum("fqk,fkc->fqc", weights, value_rows, preferred_element_type=jnp.float32)
        / denominator
    ).astype(jnp.bfloat16)
    change = jnp.einsum("fqc,cd->fqd", attended, out_weight, preferred_element_type=jnp.float32)
    mid = (features.astype(jnp.float32).reshape(frames, cell_count, channels) + change).astype(
        jnp.bfloat16
    )
    act = (
        jax.nn.silu(mid.astype(jnp.float32))
        .astype(jnp.bfloat16)
        .reshape(frames, tile_rows, tile_cols, channels)
    )
    first_span = lax.axis_index("tm") == 0
    arrived = shifted(act, "tm", 1)
    arrived = jnp.where(first_span, act, arrived)
    stacked = jnp.concatenate([arrived, act], axis=0)
    rimmed = padded_2(stacked, (("tile", 1),), 1)
    padded = jnp.pad(rimmed, ((0, 0), (0, 0), (1, 1), (0, 0)))
    pieces = [
        padded[:, offset_y : offset_y + tile_rows, offset_x : offset_x + tile_cols, :]
        for offset_y in range(3)
        for offset_x in range(3)
    ]
    patches = jnp.concatenate(pieces, axis=-1).reshape(frames + 1, cell_count, 9 * channels)
    patch_before = patches[:-1]
    patch_now = patches[1:]
    taps = conv_weight.reshape(3, 9 * channels, conv_weight.shape[-1])
    skip = jnp.einsum("fnc,cd->fnd", mid, skip_weight, preferred_element_type=jnp.float32)
    first_tap = jnp.einsum("fnc,cd->fnd", patch_before, taps[0], preferred_element_type=jnp.float32)
    even = (
        first_tap
        + jnp.einsum("fnc,cd->fnd", patch_before, taps[1], preferred_element_type=jnp.float32)
        + jnp.einsum("fnc,cd->fnd", patch_now, taps[2], preferred_element_type=jnp.float32)
        + skip
    )
    odd = (
        first_tap
        + jnp.einsum("fnc,cd->fnd", patch_now, taps[1], preferred_element_type=jnp.float32)
        + jnp.einsum("fnc,cd->fnd", patch_now, taps[2], preferred_element_type=jnp.float32)
        + skip
    )
    decoded = jnp.stack([even, odd], axis=1).astype(jnp.bfloat16)
    return decoded.reshape(2 * frames, tile_rows, tile_cols, conv_weight.shape[-1])


def solution(mesh):
    in_specs = (P("tm", "tile", None, None), P(), P(), P(), P(), P(), P(), P())
    out_specs = P("tm", "tile", None, None)
    return jax.shard_map(
        per_device, mesh=mesh, in_specs=in_specs, out_specs=out_specs, check_vma=False
    )
```

profile of v0, /device:TPU:9, one launch (start us, length us, event | category | flops | bytes accessed | tf_op | source)
XLA Modules:
  0.0 96.3 jit_solution(15848827983501576580)
XLA Ops:
  6.5 1.2 %convert_reduce_fusion = (f32[512]{0:T(512)S(1)}, f32[512]{0:T(512)S(1)}) fusion(bf16[1,2,160,512]{3,2,1,0:T(8,128)(2,1)} %param.8), kind=kLoop, calls=%fused_computation.57 | loop fusion | flops 654336 | bytes 331776 | tf_op jit(solution)/shard_map/reduce_sum | solution.py:43
  7.7 0.1 reduce_sum.34
  7.9 0.1 reduce_sum.38
  8.0 0.1 reduce_sum.51
  8.1 5.7 %all-reduce.1 = (f32[1,32]{1,0:T(1,128)S(1)}, f32[1,32]{1,0:T(1,128)S(1)}) all-reduce(f32[1,32]{1,0:T(1,128)S(1)} %bitcast.67, f32[1,32]{1,0:T(1,128)S(1)} %bitcast.66), channel_id=1, replica_groups=mesh['tm'=8,'tile'=4] {'tile'}, use_global_device_ids=true, to_apply=%region_5.0 | all-reduce | flops 64 | bytes 512 | tf_op jit(solution)/shard_map/psum | solution.py:42
  13.9 0.1 sub.40
  14.0 0.1 mul.61
  14.1 1.1 %fusion.27 = bf16[320,512]{1,0:T(8,128)(2,1)S(1)} fusion(bf16[1,2,160,512]{3,2,1,0:T(8,128)(2,1)} %param.8, f32[512]{0:T(512)} %param.9, f32[512]{0:T(512)S(1)} %mul.61, f32[512]{0:T(512)S(1)} %sub.40), kind=kLoop, calls=%fused_computation.55 | loop fusion | flops 819200 | bytes 661504 | tf_op jit(solution)/shard_map/convert_element_type | solution.py:51
  15.2 2.1 %convolution_convert_fusion.1 = bf16[320,512]{1,0:T(8,128)(2,1)} fusion(bf16[320,512]{1,0:T(8,128)(2,1)S(1)} %fusion.27, bf16[512,512]{1,0:T(8,128)(2,1)} %param.11), kind=kOutput, calls=%fused_computation.16 | convolution fusion | flops 167936000 | bytes 1179648 | tf_op jit(solution)/shard_map/fnc,cd->fnd/dot_general | solution.py:55
  17.4 1.1 %convolution_convert_fusion = bf16[320,512]{1,0:T(8,128)(2,1)} fusion(bf16[320,512]{1,0:T(8,128)(2,1)S(1)} %fusion.27, bf16[512,512]{1,0:T(8,128)(2,1)S(1)} %copy-done.2), kind=kOutput, calls=%fused_computation.15 | convolution fusion | flops 167936000 | bytes 1179648 | tf_op jit(solution)/shard_map/fnc,cd->fnd/dot_general | solution.py:58
  18.5 19.0 %all-gather.5.cloned.1.call-done = bf16[1280,512]{1,0:T(8,128)(2,1)} async-done(((bf16[320,512]{1,0:T(8,128)(2,1)}), bf16[1280,512]{1,0:T(8,128)(2,1)}) %all-gather.5.cloned.1.call-update) | async-done | bytes 1310736 | tf_op jit(solution)/shard_map/all_gather | solution.py:62
  37.5 2.3 %fusion.35 = (f32[320]{0:T(512)S(1)}, f32[320,1280]{1,0:T(8,128)S(1)}) fusion(bf16[1280,512]{1,0:T(8,128)(2,1)} %all-gather.5.cloned.1.call-done, bf16[320,512]{1,0:T(8,128)(2,1)S(1)} %fusion.27, bf16[512,512]{1,0:T(8,128)(2,1)S(1)} %copy-done), kind=kOutput, calls=%fused_computation.69 | convolution fusion | flops 588185280 | bytes 3802368 | tf_op jit(solution)/shard_map/fqc,fkc->fqk/dot_general | solution.py:65
  39.8 0.4 fusion.1
  40.2 17.1 %all-gather.7.cloned.1.call-done = bf16[1280,512]{1,0:T(8,128)(2,1)} async-done(((bf16[320,512]{1,0:T(8,128)(2,1)}), bf16[1280,512]{1,0:T(8,128)(2,1)}) %all-gather.7.cloned.1.call-update) | async-done | bytes 1310736 | tf_op jit(solution)/shard_map/all_gather | solution.py:63
  57.3 2.4 %fusion.21 = (bf16[320,512]{1,0:T(8,128)(2,1)S(1)}, bf16[320,512]{1,0:T(8,128)(2,1)S(1)}) fusion(bf16[512,512]{1,0:T(8,128)(2,1)} %param.13, bf16[1280,512]{1,0:T(8,128)(2,1)} %all-gather.7.cloned.1.call-done, f32[320,1280]{1,0:T(8,128)S(1)} %get-tuple-element.17, f32[320]{0:T(512)S(1)} %get-tuple-element.16, f32[320]{0:T(512)S(1)} %fusion.1, ...), kind=kOutput, calls=%fused_computation.38 | convolution fusion | flops 589824000 | bytes 4459008 | tf_op jit(solution)/shard_map/fqc,cd->fqd/dot_general | solution.py:76
  59.7 3.1 %collective-permute-start = (bf16[1,2,160,512]{3,2,1,0:T(8,128)(2,1)S(1)}, bf16[1,2,160,512]{3,2,1,0:T(8,128)(2,1)S(1)}, u32[]{:S(2)}, u32[]{:S(2)}) collective-permute-start(bf16[1,2,160,512]{3,2,1,0:T(8,128)(2,1)S(1)} %bitcast.54), channel_id=1, source_target_pairs={{0,4},{4,8},{8,12},{12,16},{16,20},{20,24},{24,28},{1,5},{5,9},{9,... | collective-permute-start | bytes 983048 | tf_op jit(solution)/shard_map/ppermute | solution.py:12
  62.9 8.7 %collective-permute-done = bf16[1,2,160,512]{3,2,1,0:T(8,128)(2,1)S(1)} collective-permute-done((bf16[1,2,160,512]{3,2,1,0:T(8,128)(2,1)S(1)}, bf16[1,2,160,512]{3,2,1,0:T(8,128)(2,1)S(1)}, u32[]{:S(2)}, u32[]{:S(2)}) %collective-permute-start) | collective-permute-done | bytes 327712 | tf_op jit(solution)/shard_map/ppermute | solution.py:12
  71.7 3.1 %collective-permute-start.1 = (bf16[2,1,160,512]{3,2,1,0:T(8,128)(2,1)S(1)}, bf16[2,1,160,512]{3,2,1,0:T(8,128)(2,1)S(1)}, u32[]{:S(2)}, u32[]{:S(2)}) collective-permute-start(bf16[2,1,160,512]{3,2,1,0:T(8,128)(2,1)S(1)} %get-tuple-element.14), channel_id=1, source_target_pairs={{0,1},{1,2},{2,3},{4,5},{5,6},{6,7},{8,9},{9,10},{10,11},{12,13},{... | collective-permute-start | bytes 983048 | tf_op jit(solution)/shard_map/ppermute | solution.py:20
  74.9 2.1 %collective-permute-start.2 = (bf16[2,1,160,512]{3,2,1,0:T(8,128)(2,1)S(1)}, bf16[2,1,160,512]{3,2,1,0:T(8,128)(2,1)S(1)}, u32[]{:S(2)}, u32[]{:S(2)}) collective-permute-start(bf16[2,1,160,512]{3,2,1,0:T(8,128)(2,1)S(1)} %get-tuple-element.15), channel_id=1, source_target_pairs={{1,0},{2,1},{3,2},{5,4},{6,5},{7,6},{9,8},{10,9},{11,10},{13,12},{... | collective-permute-start | bytes 983048 | tf_op jit(solution)/shard_map/ppermute | solution.py:23
  76.9 3.8 %fusion.33 = (bf16[1,3,3,512,256]{4,3,2,1,0:T(8,128)(2,1)S(1)}, bf16[1,3,3,512,256]{4,3,2,1,0:T(8,128)(2,1)S(1)}, bf16[1,3,3,512,256]{4,3,2,1,0:T(8,128)(2,1)S(1)}) fusion(bf16[3,3,3,512,256]{4,3,2,1,0:T(8,128)(2,1)} %param.14), kind=kLoop, calls=%fused_computation.67 | loop fusion | bytes 14155776 | tf_op jit(solution)/shard_map/slice | solution.py:104
  80.8 0.2 fusion.40
  81.0 2.3 %collective-permute-done.2 = bf16[2,1,160,512]{3,2,1,0:T(8,128)(2,1)S(1)} collective-permute-done((bf16[2,1,160,512]{3,2,1,0:T(8,128)(2,1)S(1)}, bf16[2,1,160,512]{3,2,1,0:T(8,128)(2,1)S(1)}, u32[]{:S(2)}, u32[]{:S(2)}) %collective-permute-start.2) | collective-permute-done | bytes 327712 | tf_op jit(solution)/shard_map/ppermute | solution.py:23
  83.4 0.4 select_maximum_fusion
  83.8 0.2 slice_dynamic-update-slice_fusion.4
  84.1 0.2 slice_dynamic-update-slice_fusion.2
  84.4 0.2 slice_dynamic-update-slice_fusion
  84.6 0.4 fusion.34
  85.0 0.9 fusion.38
  85.9 0.9 fusion.39
  86.8 0.9 fusion.13
  87.8 0.9 fusion.12
  88.7 0.8 pad_maximum_fusion.5
  (26 shorter events, 0.7 us)
Async XLA Ops:
  6.5 31.0 %copy-start = (bf16[512,512]{1,0:T(8,128)(2,1)S(1)}, bf16[512,512]{1,0:T(8,128)(2,1)}, u32[]{:S(2)}) copy-start(bf16[512,512]{1,0:T(8,128)(2,1)} %param.10) | copy-start | bytes 1572868
  6.5 10.9 %copy-start.2 = (bf16[512,512]{1,0:T(8,128)(2,1)S(1)}, bf16[512,512]{1,0:T(8,128)(2,1)}, u32[]{:S(2)}) copy-start(bf16[512,512]{1,0:T(8,128)(2,1)} %param.12) | copy-start | bytes 1572868
  6.5 31.0 %all-gather.5.cloned.1.call-start = ((), (), s32[]{:S(2)}) async-start(), calls=%async_computation | async-start | bytes 1638400 | tf_op jit(solution)/shard_map/all_gather | solution.py:62
  17.3 40.0 %all-gather.7.cloned.1.call-start = ((), (), s32[]{:S(2)}) async-start(), calls=%async_computation.1 | async-start | bytes 1638400 | tf_op jit(solution)/shard_map/all_gather | solution.py:63
  18.5 38.8 %copy-start.1 = (bf16[1,2,160,512]{3,2,1,0:T(8,128)(2,1)S(1)}, bf16[1,2,160,512]{3,2,1,0:T(8,128)(2,1)}, u32[]{:S(2)}) copy-start(bf16[1,2,160,512]{3,2,1,0:T(8,128)(2,1)} %param.8) | copy-start | bytes 983044
  59.7 11.8 %collective-permute-start = (bf16[1,2,160,512]{3,2,1,0:T(8,128)(2,1)S(1)}, bf16[1,2,160,512]{3,2,1,0:T(8,128)(2,1)S(1)}, u32[]{:S(2)}, u32[]{:S(2)}) collective-permute-start(bf16[1,2,160,512]{3,2,1,0:T(8,128)(2,1)S(1)} %bitcast.54), channel_id=1, source_target_pairs={{0,4},{4,8},{8,12},{12,16},{16,20},{20,24},{24,28},{1,5},{5,9},{9,... | collective-permute-start | bytes 983048 | tf_op jit(solution)/shard_map/ppermute | solution.py:12
  71.7 9.3 %collective-permute-start.1 = (bf16[2,1,160,512]{3,2,1,0:T(8,128)(2,1)S(1)}, bf16[2,1,160,512]{3,2,1,0:T(8,128)(2,1)S(1)}, u32[]{:S(2)}, u32[]{:S(2)}) collective-permute-start(bf16[2,1,160,512]{3,2,1,0:T(8,128)(2,1)S(1)} %get-tuple-element.14), channel_id=1, source_target_pairs={{0,1},{1,2},{2,3},{4,5},{5,6},{6,7},{8,9},{9,10},{10,11},{12,13},{... | collective-permute-start | bytes 983048 | tf_op jit(solution)/shard_map/ppermute | solution.py:20
  74.8 5.9 %copy-start.3 = (bf16[512,256]{1,0:T(8,128)(2,1)S(1)}, bf16[512,256]{1,0:T(8,128)(2,1)}, u32[]{:S(2)}) copy-start(bf16[512,256]{1,0:T(8,128)(2,1)} %param.15) | copy-start | bytes 786436
  74.9 8.5 %collective-permute-start.2 = (bf16[2,1,160,512]{3,2,1,0:T(8,128)(2,1)S(1)}, bf16[2,1,160,512]{3,2,1,0:T(8,128)(2,1)S(1)}, u32[]{:S(2)}, u32[]{:S(2)}) collective-permute-start(bf16[2,1,160,512]{3,2,1,0:T(8,128)(2,1)S(1)} %get-tuple-element.15), channel_id=1, source_target_pairs={{1,0},{2,1},{3,2},{5,4},{6,5},{7,6},{9,8},{10,9},{11,10},{13,12},{... | collective-permute-start | bytes 983048 | tf_op jit(solution)/shard_map/ppermute | solution.py:23
Sparse Core Ops, SparseCore 0:
  17.5 20.0 all-gather.4
  39.1 18.1 all-gather.6
where the time goes:
time: 96.6 us; the launch traced here: 96.3 us
  waiting for transfers between devices  47.2 us (49%)
  between operations  13.6 us (14%)
  matrix products  11.8 us (12%)
  starting transfers between devices  8.34 us (9%)
  blocking collectives  5.69 us (6%)
  local copies, waits for them, and re-layouts  5.34 us (6%)
  other arithmetic  4.26 us (4%)
    all_gather x1, waiting for transfers between devices, per_device(): lax.all_gather(key_local, 'tile', axis=1, tiled=True)  19 us
    all_gather x1, waiting for transfers between devices, per_device(): lax.all_gather(value_local, 'tile', axis=1, tiled=True)  17.1 us
    ppermute x1, waiting for transfers between devices, shifted(): return lax.ppermute(array, axis, pairs)  8.72 us
    psum x1, blocking collectives, per_device(): lax.psum((jnp.sum(grouped, axis=(1, 3)), jnp.sum(grouped * grouped, axis=...  5.69 us
    slice x1, local copies, waits for them, and re-layouts, per_device(): taps[1]  3.84 us
    ppermute x1, starting transfers between devices, padded_2(): lax.ppermute(lax.slice_in_dim(block, block.shape[dim] - width, None, axis...  3.15 us
    ppermute x1, starting transfers between devices, shifted(): return lax.ppermute(array, axis, pairs)  3.09 us
    dot_general x1, matrix products, per_device(): jnp.einsum('fqc,cd->fqd', attended, out_weight, preferred_element_type=jn...  2.43 us
  transfers between devices with their start and end apart: 5, of which 4 were waited for; matrix products, arithmetic and copies ran while one was open for 8% of the time, Pallas kernels for 0%

commit v1 on v0

v1 whole, which is shorter than its diff:
```python
import functools

import jax
import jax.numpy as jnp
from jax import lax
from jax.experimental import pallas as pl
from jax.experimental.pallas import tpu as pltpu
from jax.sharding import PartitionSpec as P

GROUPS = 32
BF = jnp.bfloat16
F32 = jnp.float32
VMEM = pltpu.VMEM
LIMIT = 48 * 1024 * 1024


def dot(left, right):
    return jnp.dot(left, right, preferred_element_type=F32)


def dot_t(left, right):
    return lax.dot_general(left, right, (((1,), (1,)), ((), ())), preferred_element_type=F32)


def spec(space=VMEM):
    return pl.BlockSpec(memory_space=space)


def call(body, outs, scratch, cost, *args, spaces=None):
    spaces = spaces or [VMEM] * len(args)
    return pl.pallas_call(
        body,
        out_shape=outs,
        in_specs=[spec(s) for s in spaces],
        out_specs=jax.tree.map(lambda _: spec(), outs),
        scratch_shapes=scratch,
        compiler_params=pltpu.CompilerParams(vmem_limit_bytes=LIMIT),
        cost_estimate=pl.CostEstimate(flops=cost, bytes_accessed=1 << 20, transcendentals=0),
    )(*args)


def stats_body(own_ref, sib_ref, out_ref):
    total = jnp.zeros((1, own_ref.shape[1]), F32)
    squared = total
    for ref in (own_ref, sib_ref):
        block = ref[...].astype(F32)
        total += jnp.sum(block, axis=0, keepdims=True)
        squared += jnp.sum(block * block, axis=0, keepdims=True)
    out_ref[...] = jnp.concatenate(
        [total, squared, jnp.zeros((6, own_ref.shape[1]), F32)], axis=0
    )


def group_sums(sums, width):
    lane = lax.broadcasted_iota(jnp.int32, sums.shape, 1)
    size = sums.shape[1]
    step = 1
    while step < width:
        low = pltpu.roll(sums, size - step, 1)
        high = pltpu.roll(sums, step, 1)
        sums = sums + jnp.where((lane & step) == 0, low, high)
        step *= 2
    return sums


def moments(sum_refs, cells):
    sums = sum_refs[0][...]
    for ref in sum_refs[1:]:
        sums = sums + ref[...]
    width = sums.shape[1] // GROUPS
    sums = group_sums(sums, width)
    population = cells * width
    mean = sums[0:1] / population
    var = sums[1:2] / population - mean * mean
    return mean, lax.rsqrt(var + 1e-06)


def normalise(block, mean, inverse, gain):
    return ((block.astype(F32) - mean) * inverse * gain).astype(BF)


def attend(queries, keys, values, state, exponent):
    scores = dot_t(queries, keys)
    peak = jnp.max(scores, axis=1, keepdims=True)
    if state is not None:
        old_peak, old_sum, old = state
        peak = jnp.maximum(peak, old_peak)
    unnormed = jnp.exp2((scores - peak) * exponent)
    total = jnp.sum(unnormed, axis=1, keepdims=True)
    mixed = dot(unnormed.astype(BF), values)
    if state is not None:
        fade = jnp.exp2((old_peak - peak) * exponent)
        total = total + old_sum * fade
        mixed = mixed + old * fade
    return peak, total, mixed


def early_body(
    cells_all, cols, exponent, n_sums,
    place_ref, own_ref, sib_ref, *refs,
):
    sum_refs, refs = refs[:n_sums], refs[n_sums:]
    gain_ref, wq_ref, wk_ref, wv_ref, q_ref, k_ref, v_ref, peak_ref, sum_ref, mix_ref = refs
    mean, inverse = moments(sum_refs, cells_all)
    gain = gain_ref[...]
    cells = own_ref.shape[0]
    core = place_ref[0]
    own = normalise(own_ref[...], mean, inverse, gain)
    sib = normalise(sib_ref[...], mean, inverse, gain)
    near = pl.multiple_of(core * (cells - cols), 16)
    halo = normalise(sib_ref[pl.ds(near, cols), :], mean, inverse, gain)
    queries = dot(jnp.concatenate([own, halo], axis=0), wq_ref[...]).astype(BF)
    both = jnp.concatenate([own, sib], axis=0)
    keys = dot(both, wk_ref[...]).astype(BF)
    values = dot(both, wv_ref[...]).astype(BF)
    q_ref[...] = queries
    k_ref[...] = keys
    v_ref[...] = values
    peak, total, mixed = attend(queries, keys, values, None, exponent)
    peak_ref[...] = jnp.broadcast_to(peak, peak_ref.shape)
    sum_ref[...] = jnp.broadcast_to(total, sum_ref.shape)
    mix_ref[...] = mixed


def spread(act, rows, cols):
    size = act.shape[0]
    col = lax.broadcasted_iota(jnp.int32, act.shape, 0) % cols
    left = jnp.where(col == 0, 0.0, pltpu.roll(act, 1, 0))
    right = jnp.where(col == cols - 1, 0.0, pltpu.roll(act, size - 1, 0))
    return jnp.concatenate([left.astype(BF), act.astype(BF), right.astype(BF)], axis=1)


def conv(wide_ref, taps, out_cells, cols):
    total = None
    for row in range(3):
        term = dot(wide_ref[row * cols : row * cols + out_cells, :], taps(row))
        total = term if total is None else total + term
    return total


def late_body(
    cells_all, cols, exponent, n_sums, n_remote,
    place_ref, own_ref, sib_ref, *refs,
):
    sum_refs, refs = refs[:n_sums], refs[n_sums:]
    recv_refs, refs = refs[:n_remote], refs[n_remote:]
    rsib_refs, refs = refs[:n_remote], refs[n_remote:]
    (gain_ref, wq_ref, wk_ref, wv_ref, wo_ref, conv_ref, q_ref, k_ref, v_ref, peak_ref, sum_ref,
     mix_ref, part_ref, act_ref, mid_ref, wide_ref, taps_ref, sem) = refs
    copy = pltpu.make_async_copy(conv_ref.at[pl.ds(0, 2)], taps_ref, sem)
    copy.start()
    mean, inverse = moments(sum_refs, cells_all)
    gain = gain_ref[...]
    cells = own_ref.shape[0]
    core = place_ref[0]
    far = pl.multiple_of((1 - core) * (cells - cols), 16)
    first = rsib_refs[0][pl.ds(far, cols), :]
    last = rsib_refs[-1][pl.ds(far, cols), :]
    far_block = first if n_remote == 1 else jnp.where(core == 0, first, last)
    far_query = dot(normalise(far_block, mean, inverse, gain), wq_ref[...]).astype(BF)
    far_state = attend(far_query, k_ref[...], v_ref[...], None, exponent)
    state = [
        jnp.concatenate([near, new], axis=0)
        for near, new in zip(
            (peak_ref[:, 0:1], sum_ref[:, 0:1], mix_ref[...]), far_state, strict=True
        )
    ]
    queries = jnp.concatenate([q_ref[...], far_query], axis=0)
    for recv_ref, rsib_ref in zip(recv_refs, rsib_refs, strict=True):
        both = normalise(
            jnp.concatenate([recv_ref[...], rsib_ref[...]], axis=0), mean, inverse, gain
        )
        keys = dot(both, wk_ref[...]).astype(BF)
        values = dot(both, wv_ref[...]).astype(BF)
        state = attend(queries, keys, values, state, exponent)
    attended = (state[2] / state[1]).astype(BF)
    change = dot(attended, wo_ref[...])
    near = pl.multiple_of(core * (cells - cols), 16)
    base = jnp.concatenate([own_ref[...], sib_ref[pl.ds(near, cols), :], far_block], axis=0)
    mid = (base.astype(F32) + change).astype(BF)
    mid_ref[...] = mid[:cells]
    act = jax.nn.silu(mid.astype(F32))
    inside = place_ref[1] != 0
    near_act = act[cells : cells + cols]
    far_act = jnp.where(inside, act[cells + cols :], 0.0)
    above = jnp.where(core == 0, far_act, near_act)
    below = jnp.where(core == 0, near_act, far_act)
    act = jnp.concatenate([above, act[:cells], below], axis=0).astype(BF)
    act_ref[...] = act
    wide_ref[...] = spread(act.astype(F32), cells // cols + 2, cols)
    copy.wait()
    first_tap = conv(wide_ref, lambda row: taps_ref[0, row], cells, cols)
    second_tap = conv(wide_ref, lambda row: taps_ref[1, row], cells, cols)
    part_ref[0] = (first_tap + second_tap).astype(BF)
    part_ref[1] = first_tap.astype(BF)


def now_body(cols, act_ref, mid_ref, conv_ref, skip_ref, out_ref, wide_ref, taps_ref, sem):
    copy = pltpu.make_async_copy(conv_ref.at[pl.ds(1, 2)], taps_ref, sem)
    copy.start()
    cells = mid_ref.shape[0]
    wide_ref[...] = spread(act_ref[...].astype(F32), cells // cols + 2, cols)
    skip = dot(mid_ref[...], skip_ref[...])
    copy.wait()
    second_tap = conv(wide_ref, lambda row: taps_ref[0, row], cells, cols)
    last_tap = conv(wide_ref, lambda row: taps_ref[1, row], cells, cols) + skip
    out_ref[0] = last_tap
    out_ref[1] = last_tap + second_tap


def per_device(
    features,
    norm_gain,
    query_weight,
    key_weight,
    value_weight,
    out_weight,
    conv_weight,
    skip_weight,
):
    _, tile_rows, cols, channels = features.shape
    out_channels = conv_weight.shape[-1]
    cells = tile_rows * cols
    devices = lax.axis_size("tile")
    chips = devices // 2
    me = lax.axis_index("tile")
    core = me % 2
    swap = [(i, i ^ 1) for i in range(devices)]
    own = features.reshape(cells, channels)

    def turned(array, by):
        return lax.ppermute(array, "tile", [(i, (i + 2 * by) % devices) for i in range(devices)])

    recv = [turned(own, by) for by in range(1, chips)]
    sib = lax.ppermute(own, "tile", swap)
    rsib = [lax.ppermute(block, "tile", swap) for block in recv]
    sums = call(
        stats_body, jax.ShapeDtypeStruct((8, channels), F32), [], 1 << 22, own, sib
    )
    sums = [sums] + [turned(sums, by) for by in range(1, chips)]

    gain = norm_gain.reshape(1, channels)
    exponent = channels ** (-0.5) * 1.4426950408889634
    outside = jnp.where(core == 0, me == 0, me == devices - 1)
    place = jnp.stack([core, 1 - outside.astype(jnp.int32)]).astype(jnp.int32)
    near = cells + cols
    shapes = [
        jax.ShapeDtypeStruct((near, channels), BF),
        jax.ShapeDtypeStruct((2 * cells, channels), BF),
        jax.ShapeDtypeStruct((2 * cells, channels), BF),
        jax.ShapeDtypeStruct((near, 128), F32),
        jax.ShapeDtypeStruct((near, 128), F32),
        jax.ShapeDtypeStruct((near, channels), F32),
    ]
    n_sums = len(sums)
    early = call(
        functools.partial(early_body, devices * cells, cols, exponent, n_sums),
        shapes,
        [],
        2 * 10**9,
        place, own, sib, *sums, gain, query_weight, key_weight, value_weight,
        spaces=[pltpu.SMEM] + [VMEM] * (6 + n_sums),
    )
    taps = conv_weight.reshape(3, 3, 3 * channels, out_channels)
    wide = VMEM((cells + 2 * cols, 3 * channels), BF)
    held = VMEM((2, 3, 3 * channels, out_channels), BF)
    part, act, mid = call(
        functools.partial(late_body, devices * cells, cols, exponent, n_sums, chips - 1),
        [
            jax.ShapeDtypeStruct((2, cells, out_channels), BF),
            jax.ShapeDtypeStruct((cells + 2 * cols, channels), BF),
            jax.ShapeDtypeStruct((cells, channels), BF),
        ],
        [wide, held, pltpu.SemaphoreType.DMA],
        4 * 10**9,
        place, own, sib, *sums, *recv, *rsib, gain, query_weight, key_weight, value_weight,
        out_weight, taps, *early,
        spaces=[pltpu.SMEM] + [VMEM] * (2 + n_sums + 2 * (chips - 1) + 5) + [pl.ANY] + [VMEM] * 6,
    )
    spans = lax.axis_size("tm")
    arrived = lax.ppermute(part, "tm", [(i, i + 1) for i in range(spans - 1)])
    now = call(
        functools.partial(now_body, cols),
        jax.ShapeDtypeStruct((2, cells, out_channels), F32),
        [wide, held, pltpu.SemaphoreType.DMA],
        2 * 10**9,
        act, mid, taps, skip_weight,
        spaces=[VMEM, VMEM, pl.ANY, VMEM],
    )
    before = jnp.where(lax.axis_index("tm") == 0, part, arrived)
    decoded = (now + before.astype(F32)).astype(BF)
    return decoded.reshape(2, tile_rows, cols, out_channels)


def solution(mesh):
    in_specs = (P("tm", "tile", None, None), P(), P(), P(), P(), P(), P(), P())
    out_specs = P("tm", "tile", None, None)
    return jax.shard_map(
        per_device, mesh=mesh, in_specs=in_specs, out_specs=out_specs, check_vma=False
    )
```

time: 96.6 us -> 46.3 us (0.48)
  the two profiles are of different devices: /device:TPU:9 before, /device:TPU:24 now
where the time goes in v1:
time: 46.3 us; the launch traced here: 45.9 us
  Pallas kernels  16.4 us (35%)
  waiting for transfers between devices  14.6 us (32%)
  local copies, waits for them, and re-layouts  7.42 us (16%)
  starting transfers between devices  6.51 us (14%)
  other arithmetic  0.9 us (2%)
    pallas_call x4, Pallas kernels, call(): pl.pallas_call(body, out_shape=outs, in_specs=[spec(s) for s in spaces],...  16.4 us
    ppermute x2, waiting for transfers between devices, turned(): lax.ppermute(array, 'tile', [(i, (i + 2 * by) % devices) for i in range(d...  10.3 us
    unnamed x20, local copies, waits for them, and re-layouts  7.42 us
    ppermute x1, waiting for transfers between devices, per_device(): arrived = lax.ppermute(part, 'tm', [(i, i + 1) for i in range(spans - 1)])  4.29 us
    ppermute x1, starting transfers between devices, per_device(): arrived = lax.ppermute(part, 'tm', [(i, i + 1) for i in range(spans - 1)])  3.4 us
    ppermute x2, starting transfers between devices, turned(): lax.ppermute(array, 'tile', [(i, (i + 2 * by) % devices) for i in range(d...  3.1 us
  transfers between devices with their start and end apart: 5, of which 3 were waited for; matrix products, arithmetic and copies ran while one was open for 0% of the time, Pallas kernels for 15%

profile of v1, /device:TPU:24, one launch (start us, length us, event | category | flops | bytes accessed | tf_op | source)
XLA Modules:
  0.0 45.9 jit_solution(17833020071842820176)
XLA Ops:
  0.0 1.5 %collective-permute-start.2 = (bf16[320,512]{1,0:T(8,128)(2,1)}, bf16[320,512]{1,0:T(8,128)(2,1)S(1)}, u32[]{:S(2)}, u32[]{:S(2)}) collective-permute-start(bf16[320,512]{1,0:T(8,128)(2,1)} %bitcast.6), channel_id=1, source_target_pairs={{0,2},{1,3},{2,0},{3,1},{4,6},{5,7},{6,4},{7,5},{8,10},{9,11},{10,... | collective-permute-start | bytes 983048 | tf_op jit(solution)/shard_map/ppermute | solution.py:232
  1.5 0.0 collective-permute-start
  1.5 8.1 %collective-permute-done.2.refs_2_ = bf16[320,512]{1,0:T(8,128)(2,1)S(1)} collective-permute-done((bf16[320,512]{1,0:T(8,128)(2,1)}, bf16[320,512]{1,0:T(8,128)(2,1)S(1)}, u32[]{:S(2)}, u32[]{:S(2)}) %collective-permute-start.2) | collective-permute-done | bytes 327712 | tf_op jit(solution)/shard_map/ppermute | solution.py:232
  9.7 0.0 collective-permute-start.3
  9.7 0.0 collective-permute-done.sib_ref
  9.7 0.0 copy-start
  9.7 1.0 %copy-done = bf16[1,2,160,512]{3,2,1,0:T(8,128)(2,1)S(1)} copy-done((bf16[1,2,160,512]{3,2,1,0:T(8,128)(2,1)S(1)}, bf16[1,2,160,512]{3,2,1,0:T(8,128)(2,1)}, u32[]{:S(2)}) %copy-start) | copy-done | bytes 327704
  10.6 0.0 copy-start.5
  10.6 0.1 shard_map.82.refs_0_
  10.8 1.6 %collective-permute-start.1 = (f32[8,512]{1,0:T(8,128)S(1)}, f32[8,512]{1,0:T(8,128)S(1)}, u32[]{:S(2)}, u32[]{:S(2)}) collective-permute-start(f32[8,512]{1,0:T(8,128)S(1)} %shard_map.82.refs_0_), channel_id=1, source_target_pairs={{0,2},{1,3},{2,0},{3,1},{4,6},{5,7},{6,4},{7,5},{8,10},{9,11},{10,... | collective-permute-start | bytes 49160 | tf_op jit(solution)/shard_map/ppermute | solution.py:232
  12.4 0.1 pad_add_fusion.place_ref
  12.4 2.1 %collective-permute-done.1.refs_1_ = f32[8,512]{1,0:T(8,128)S(1)} collective-permute-done((f32[8,512]{1,0:T(8,128)S(1)}, f32[8,512]{1,0:T(8,128)S(1)}, u32[]{:S(2)}, u32[]{:S(2)}) %collective-permute-start.1) | collective-permute-done | bytes 16416 | tf_op jit(solution)/shard_map/ppermute | solution.py:232
  14.6 0.0 copy-start.2
  14.6 1.0 %copy-done.2 = bf16[512,512]{1,0:T(8,128)(2,1)S(1)} copy-done((bf16[512,512]{1,0:T(8,128)(2,1)S(1)}, bf16[512,512]{1,0:T(8,128)(2,1)}, u32[]{:S(2)}) %copy-start.2) | copy-done | bytes 524312
  15.6 0.0 copy-start.3
  15.6 1.0 %copy-done.3 = bf16[512,512]{1,0:T(8,128)(2,1)S(1)} copy-done((bf16[512,512]{1,0:T(8,128)(2,1)S(1)}, bf16[512,512]{1,0:T(8,128)(2,1)}, u32[]{:S(2)}) %copy-start.3) | copy-done | bytes 524312
  16.7 0.0 copy-start.4
  16.7 1.0 %copy-done.4 = bf16[512,512]{1,0:T(8,128)(2,1)S(1)} copy-done((bf16[512,512]{1,0:T(8,128)(2,1)S(1)}, bf16[512,512]{1,0:T(8,128)(2,1)}, u32[]{:S(2)}) %copy-start.4) | copy-done | bytes 524312
  17.7 0.7 %copy-done.6 = f32[512]{0:T(512)S(1)} copy-done((f32[512]{0:T(512)S(1)}, f32[512]{0:T(512)}, u32[]{:S(2)}) %copy-start.6) | copy-done | bytes 2072
  18.4 2.9 %shard_map.83 = (bf16[480,512]{1,0:T(8,128)(2,1)S(1)}, bf16[640,512]{1,0:T(8,128)(2,1)S(1)}, bf16[640,512]{1,0:T(8,128)(2,1)S(1)}, f32[480,128]{1,0:T(8,128)S(1)...) custom-call(s32[2]{0:T(128)S(1)} %pad_add_fusion.place_ref, bf16[320,512]{1,0:T(8,128)(2,1)S(1)} %bitcast.9, ...), custom_call_target="tpu_custom_call" | custom-call | flops 2000000000 | bytes 1048576 | tf_op jit(solution)/shard_map/pallas_call | solution.py:31
  21.3 0.0 copy-start.7
  21.3 0.9 %copy-done.7 = f32[480,512]{1,0:T(8,128)} copy-done((f32[480,512]{1,0:T(8,128)}, f32[480,512]{1,0:T(8,128)S(1)}, u32[]{:S(2)}) %copy-start.7) | copy-done | bytes 983064
  22.2 0.9 %copy-done.8 = bf16[640,512]{1,0:T(8,128)(2,1)} copy-done((bf16[640,512]{1,0:T(8,128)(2,1)}, bf16[640,512]{1,0:T(8,128)(2,1)S(1)}, u32[]{:S(2)}) %copy-start.8) | copy-done | bytes 655384
  23.1 0.8 %copy-done.9 = bf16[640,512]{1,0:T(8,128)(2,1)} copy-done((bf16[640,512]{1,0:T(8,128)(2,1)}, bf16[640,512]{1,0:T(8,128)(2,1)S(1)}, u32[]{:S(2)}) %copy-start.9) | copy-done | bytes 655384
  23.9 0.0 collective-permute-done.3.refs_3_
  23.9 0.0 copy-done.5
  23.9 9.4 %shard_map.84 = (bf16[2,320,256]{2,1,0:T(8,128)(2,1)S(1)}, bf16[640,512]{1,0:T(8,128)(2,1)S(1)}, bf16[320,512]{1,0:T(8,128)(2,1)S(1)}) custom-call(s32[2]{0:T(128)S(1)} %pad_add_fusion.place_ref, bf16[320,512]{1,0:T(8,128)(2,1)S(1)} %bitcast.10, bf16[320,512]{1,0:T(8,128)(2,1)S(1)} %collective-permute-done.sib_ref, f32[8,512]{1,0:T(8,128)S(1)} %shard_map.82.refs_0_, ...), custom_call_target="tpu_custom_call" | custom-call | flops 4000000000 | bytes 1048576 | tf_op jit(solution)/shard_map/pallas_call | solution.py:31
  33.3 3.4 %collective-permute-start.4 = (bf16[2,320,256]{2,1,0:T(8,128)(2,1)S(1)}, bf16[2,320,256]{2,1,0:T(8,128)(2,1)S(1)}, u32[]{:S(2)}, u32[]{:S(2)}) collective-permute-start(bf16[2,320,256]{2,1,0:T(8,128)(2,1)S(1)} %get-tuple-element.22), channel_id=1, source_target_pairs={{0,4},{4,8},{8,12},{12,16},{16,20},{20,24},{24,28},{1,5},{5,9},{9,... | collective-permute-start | bytes 983048 | tf_op jit(solution)/shard_map/ppermute | solution.py:281
  36.7 0.0 copy-done.1
  36.7 4.0 %shard_map.85 = f32[2,320,256]{2,1,0:T(8,128)S(1)} custom-call(bf16[640,512]{1,0:T(8,128)(2,1)S(1)} %get-tuple-element.20.act_ref, bf16[320,512]{1,0:T(8,128)(2,1)S(1)} %get-tuple-element.21.mid_ref, bf16[3,3,1536,256]{3,2,1,0:T(8,128)(2,1)} %bitcast.14, bf16[512,256]{1,0:T(8,128)(2,1)S(1)} %copy-done.1), custom_call_target="tpu_custom_call" | custom-call | flops 2000000000 | bytes 1048576 | tf_op jit(solution)/shard_map/pallas_call | solution.py:31
  40.8 4.3 %collective-permute-done.4 = bf16[2,320,256]{2,1,0:T(8,128)(2,1)S(1)} collective-permute-done((bf16[2,320,256]{2,1,0:T(8,128)(2,1)S(1)}, bf16[2,320,256]{2,1,0:T(8,128)(2,1)S(1)}, u32[]{:S(2)}, u32[]{:S(2)}) %collective-permute-start.4) | collective-permute-done | bytes 327712 | tf_op jit(solution)/shard_map/ppermute | solution.py:281
  45.0 0.8 %add_convert_fusion = bf16[2,320,256]{2,1,0:T(8,128)(2,1)} fusion(f32[2,320,256]{2,1,0:T(8,128)S(1)} %shard_map.85, bf16[2,320,256]{2,1,0:T(8,128)(2,1)S(1)} %get-tuple-element.22, bf16[2,320,256]{2,1,0:T(8,128)(2,1)S(1)} %collective-permute-done.4, pred[]{:T(512)S(6)} %eq.17), kind=kLoop, calls=%fused_computation | loop fusion | flops 655360 | bytes 1638401 | tf_op jit(solution)/shard_map/convert_element_type | solution.py:291
  (4 shorter events, 0.0 us)
Async XLA Ops:
  0.0 9.7 %collective-permute-start.2 = (bf16[320,512]{1,0:T(8,128)(2,1)}, bf16[320,512]{1,0:T(8,128)(2,1)S(1)}, u32[]{:S(2)}, u32[]{:S(2)}) collective-permute-start(bf16[320,512]{1,0:T(8,128)(2,1)} %bitcast.6), channel_id=1, source_target_pairs={{0,2},{1,3},{2,0},{3,1},{4,6},{5,7},{6,4},{7,5},{8,10},{9,11},{10,... | collective-permute-start | bytes 983048 | tf_op jit(solution)/shard_map/ppermute | solution.py:232
  1.5 8.1 %collective-permute-start = (bf16[320,512]{1,0:T(8,128)(2,1)}, bf16[320,512]{1,0:T(8,128)(2,1)S(1)}, u32[]{:S(2)}, u32[]{:S(2)}) collective-permute-start(bf16[320,512]{1,0:T(8,128)(2,1)} %bitcast.7), channel_id=1, source_target_pairs={{0,1},{1,0},{2,3},{3,2},{4,5},{5,4},{6,7},{7,6},{8,9},{9,8},{10,11... | collective-permute-start | bytes 983048 | tf_op jit(solution)/shard_map/ppermute | solution.py:235
  9.7 14.3 %collective-permute-start.3 = (bf16[320,512]{1,0:T(8,128)(2,1)S(1)}, bf16[320,512]{1,0:T(8,128)(2,1)S(1)}, u32[]{:S(2)}, u32[]{:S(2)}) collective-permute-start(bf16[320,512]{1,0:T(8,128)(2,1)S(1)} %collective-permute-done.2.refs_2_), channel_id=1, source_target_pairs={{0,1},{1,0},{2,3},{3,2},{4,5},{5,4},{6,7},{7,6},{8,9},{9,8},{10,11... | collective-permute-start | bytes 983048 | tf_op jit(solution)/shard_map/ppermute | solution.py:236
  9.7 1.0 %copy-start = (bf16[1,2,160,512]{3,2,1,0:T(8,128)(2,1)S(1)}, bf16[1,2,160,512]{3,2,1,0:T(8,128)(2,1)}, u32[]{:S(2)}) copy-start(bf16[1,2,160,512]{3,2,1,0:T(8,128)(2,1)} %param.8) | copy-start | bytes 983044
  10.6 13.3 %copy-start.5 = (bf16[512,512]{1,0:T(8,128)(2,1)S(1)}, bf16[512,512]{1,0:T(8,128)(2,1)}, u32[]{:S(2)}) copy-start(bf16[512,512]{1,0:T(8,128)(2,1)} %refs_8_.1) | copy-start | bytes 1572868
  10.8 3.8 %collective-permute-start.1 = (f32[8,512]{1,0:T(8,128)S(1)}, f32[8,512]{1,0:T(8,128)S(1)}, u32[]{:S(2)}, u32[]{:S(2)}) collective-permute-start(f32[8,512]{1,0:T(8,128)S(1)} %shard_map.82.refs_0_), channel_id=1, source_target_pairs={{0,2},{1,3},{2,0},{3,1},{4,6},{5,7},{6,4},{7,5},{8,10},{9,11},{10,... | collective-permute-start | bytes 49160 | tf_op jit(solution)/shard_map/ppermute | solution.py:232
  14.6 1.0 %copy-start.2 = (bf16[512,512]{1,0:T(8,128)(2,1)S(1)}, bf16[512,512]{1,0:T(8,128)(2,1)}, u32[]{:S(2)}) copy-start(bf16[512,512]{1,0:T(8,128)(2,1)} %refs_5_.3) | copy-start | bytes 1572868
  15.6 1.0 %copy-start.3 = (bf16[512,512]{1,0:T(8,128)(2,1)S(1)}, bf16[512,512]{1,0:T(8,128)(2,1)}, u32[]{:S(2)}) copy-start(bf16[512,512]{1,0:T(8,128)(2,1)} %refs_6_.1) | copy-start | bytes 1572868
  16.7 1.0 %copy-start.4 = (bf16[512,512]{1,0:T(8,128)(2,1)S(1)}, bf16[512,512]{1,0:T(8,128)(2,1)}, u32[]{:S(2)}) copy-start(bf16[512,512]{1,0:T(8,128)(2,1)} %refs_7_.1) | copy-start | bytes 1572868
  17.7 0.7 %copy-start.6 = (f32[512]{0:T(512)S(1)}, f32[512]{0:T(512)}, u32[]{:S(2)}) copy-start(f32[512]{0:T(512)} %param.9) | copy-start | bytes 6148
  21.3 1.0 %copy-start.7 = (f32[480,512]{1,0:T(8,128)}, f32[480,512]{1,0:T(8,128)S(1)}, u32[]{:S(2)}) copy-start(f32[480,512]{1,0:T(8,128)S(1)} %get-tuple-element.19.refs_15_) | copy-start | bytes 2949124
  22.2 0.9 %copy-start.8 = (bf16[640,512]{1,0:T(8,128)(2,1)}, bf16[640,512]{1,0:T(8,128)(2,1)S(1)}, u32[]{:S(2)}) copy-start(bf16[640,512]{1,0:T(8,128)(2,1)S(1)} %get-tuple-element.15.refs_11_) | copy-start | bytes 1966084
  23.1 0.8 %copy-start.9 = (bf16[640,512]{1,0:T(8,128)(2,1)}, bf16[640,512]{1,0:T(8,128)(2,1)S(1)}, u32[]{:S(2)}) copy-start(bf16[640,512]{1,0:T(8,128)(2,1)S(1)} %get-tuple-element.16.refs_12_) | copy-start | bytes 1966084
  23.9 12.8 %copy-start.1 = (bf16[512,256]{1,0:T(8,128)(2,1)S(1)}, bf16[512,256]{1,0:T(8,128)(2,1)}, u32[]{:S(2)}) copy-start(bf16[512,256]{1,0:T(8,128)(2,1)} %skip_ref.1) | copy-start | bytes 786436
  33.3 11.8 %collective-permute-start.4 = (bf16[2,320,256]{2,1,0:T(8,128)(2,1)S(1)}, bf16[2,320,256]{2,1,0:T(8,128)(2,1)S(1)}, u32[]{:S(2)}, u32[]{:S(2)}) collective-permute-start(bf16[2,320,256]{2,1,0:T(8,128)(2,1)S(1)} %get-tuple-element.22), channel_id=1, source_target_pairs={{0,4},{4,8},{8,12},{12,16},{16,20},{20,24},{24,28},{1,5},{5,9},{9,... | collective-permute-start | bytes 983048 | tf_op jit(solution)/shard_map/ppermute | solution.py:281

commit v2 on v1

v2 whole, which is shorter than its diff:
```python
import functools

import jax
import jax.numpy as jnp
from jax import lax
from jax.experimental import pallas as pl
from jax.experimental.pallas import tpu as pltpu
from jax.sharding import PartitionSpec as P

GROUPS = 32
BF = jnp.bfloat16
F32 = jnp.float32
VMEM = pltpu.VMEM
LIMIT = 20 * 1024 * 1024


def dot(left, right):
    return jnp.dot(left, right, preferred_element_type=F32)


def dot_t(left, right):
    return lax.dot_general(left, right, (((1,), (1,)), ((), ())), preferred_element_type=F32)


def spec(space=VMEM):
    return pl.BlockSpec(memory_space=space)


def call(body, outs, scratch, cost, *args, spaces=None):
    spaces = spaces or [VMEM] * len(args)
    return pl.pallas_call(
        body,
        out_shape=outs,
        in_specs=[spec(s) for s in spaces],
        out_specs=jax.tree.map(lambda _: spec(), outs),
        scratch_shapes=scratch,
        compiler_params=pltpu.CompilerParams(vmem_limit_bytes=LIMIT),
        cost_estimate=pl.CostEstimate(flops=cost, bytes_accessed=1 << 20, transcendentals=0),
    )(*args)


def stats_body(own_ref, sib_ref, out_ref):
    total = jnp.zeros((1, own_ref.shape[1]), F32)
    squared = total
    for ref in (own_ref, sib_ref):
        block = ref[...].astype(F32)
        total += jnp.sum(block, axis=0, keepdims=True)
        squared += jnp.sum(block * block, axis=0, keepdims=True)
    out_ref[...] = jnp.concatenate(
        [total, squared, jnp.zeros((6, own_ref.shape[1]), F32)], axis=0
    )


def group_sums(sums, width):
    lane = lax.broadcasted_iota(jnp.int32, sums.shape, 1)
    size = sums.shape[1]
    step = 1
    while step < width:
        low = pltpu.roll(sums, size - step, 1)
        high = pltpu.roll(sums, step, 1)
        sums = sums + jnp.where((lane & step) == 0, low, high)
        step *= 2
    return sums


def moments(sum_refs, cells):
    sums = sum_refs[0][...]
    for ref in sum_refs[1:]:
        sums = sums + ref[...]
    width = sums.shape[1] // GROUPS
    sums = group_sums(sums, width)
    population = cells * width
    mean = sums[0:1] / population
    var = sums[1:2] / population - mean * mean
    return mean, lax.rsqrt(var + 1e-06)


def normalise(block, mean, inverse, gain):
    return ((block.astype(F32) - mean) * inverse * gain).astype(BF)


def attend(queries, keys, values, state, exponent):
    scores = dot_t(queries, keys)
    peak = jnp.max(scores, axis=1, keepdims=True)
    if state is not None:
        old_peak, old_sum, old = state
        peak = jnp.maximum(peak, old_peak)
    unnormed = jnp.exp2((scores - peak) * exponent)
    total = jnp.sum(unnormed, axis=1, keepdims=True)
    mixed = dot(unnormed.astype(BF), values)
    if state is not None:
        fade = jnp.exp2((old_peak - peak) * exponent)
        total = total + old_sum * fade
        mixed = mixed + old * fade
    return peak, total, mixed


def save_state(state, peak_ref, sum_ref, mix_ref):
    peak, total, mixed = state
    peak_ref[...] = jnp.broadcast_to(peak, peak_ref.shape)
    sum_ref[...] = jnp.broadcast_to(total, sum_ref.shape)
    mix_ref[...] = mixed


def load_state(peak_ref, sum_ref, mix_ref):
    return peak_ref[:, 0:1], sum_ref[:, 0:1], mix_ref[...]


def early_body(
    cells_all, cols, exponent, n_sums,
    place_ref, own_ref, sib_ref, *refs,
):
    sum_refs, refs = refs[:n_sums], refs[n_sums:]
    gain_ref, refs = refs[0], refs[1:]
    hbm_refs, refs = refs[:6], refs[6:]
    norm_ref, q_ref, k_ref, v_ref, peak_ref, sum_ref, mix_ref, refs = *refs[:7], refs[7:]
    held_refs, sems = refs[:6], refs[6]
    copies = [
        pltpu.make_async_copy(source, target, sems.at[i])
        for i, (source, target) in enumerate(zip(hbm_refs, held_refs, strict=True))
    ]
    for copy in copies:
        copy.start()
    wq_ref, wk_ref, wv_ref = held_refs[:3]
    mean, inverse = moments(sum_refs, cells_all)
    gain = gain_ref[...]
    norm_ref[...] = jnp.concatenate(
        [mean, inverse, gain, jnp.zeros((5, mean.shape[1]), F32)], axis=0
    )
    cells = own_ref.shape[0]
    core = place_ref[0]
    own = normalise(own_ref[...], mean, inverse, gain)
    sib = normalise(sib_ref[...], mean, inverse, gain)
    near = pl.multiple_of(core * (cells - cols), 16)
    halo = normalise(sib_ref[pl.ds(near, cols), :], mean, inverse, gain)
    both = jnp.concatenate([own, sib], axis=0)
    copies[0].wait()
    q_ref[...] = dot(jnp.concatenate([own, halo], axis=0), wq_ref[...]).astype(BF)
    copies[1].wait()
    k_ref[...] = dot(both, wk_ref[...]).astype(BF)
    copies[2].wait()
    v_ref[...] = dot(both, wv_ref[...]).astype(BF)
    state = attend(q_ref[...], k_ref[...], v_ref[...], None, exponent)
    save_state(state, peak_ref, sum_ref, mix_ref)
    for copy in copies[3:]:
        copy.wait()


def normal_of(norm_ref):
    return norm_ref[0:1], norm_ref[1:2], norm_ref[2:3]


def keys_body(block_ref, norm_ref, wk_ref, wv_ref, kv_ref):
    cells = block_ref.shape[0]
    normed = normalise(block_ref[...], *normal_of(norm_ref))
    kv_ref[:cells] = dot(normed, wk_ref[...]).astype(BF)
    kv_ref[cells:] = dot(normed, wv_ref[...]).astype(BF)


def join_body(
    cols, exponent,
    place_ref, first_ref, last_ref, norm_ref, wq_ref, q_ref, k_ref, v_ref, peak_ref, sum_ref,
    mix_ref, kv_ref, all_q_ref, all_peak_ref, all_sum_ref, all_mix_ref,
):
    cells = first_ref.shape[0]
    core = place_ref[0]
    far = pl.multiple_of((1 - core) * (cells - cols), 16)
    block = jnp.where(core == 0, first_ref[pl.ds(far, cols), :], last_ref[pl.ds(far, cols), :])
    near = q_ref.shape[0]
    far_q = dot(normalise(block, *normal_of(norm_ref)), wq_ref[...]).astype(BF)
    all_q_ref[:near] = q_ref[...]
    all_q_ref[near:] = far_q
    far_state = attend(far_q, k_ref[...], v_ref[...], None, exponent)
    state = [
        jnp.concatenate([old, new], axis=0)
        for old, new in zip(load_state(peak_ref, sum_ref, mix_ref), far_state, strict=True)
    ]
    state = attend(all_q_ref[...], kv_ref[:cells], kv_ref[cells:], state, exponent)
    save_state(state, all_peak_ref, all_sum_ref, all_mix_ref)


def more_body(
    exponent, q_ref, peak_ref, sum_ref, mix_ref, kv_ref, new_peak_ref, new_sum_ref, new_mix_ref
):
    cells = kv_ref.shape[0] // 2
    state = load_state(peak_ref, sum_ref, mix_ref)
    state = attend(q_ref[...], kv_ref[:cells], kv_ref[cells:], state, exponent)
    save_state(state, new_peak_ref, new_sum_ref, new_mix_ref)


def spread(act, cols):
    size = act.shape[0]
    col = lax.broadcasted_iota(jnp.int32, act.shape, 0) % cols
    left = jnp.where(col == 0, 0.0, pltpu.roll(act, 1, 0))
    right = jnp.where(col == cols - 1, 0.0, pltpu.roll(act, size - 1, 0))
    return jnp.concatenate([left.astype(BF), act.astype(BF), right.astype(BF)], axis=1)


def conv(wide_ref, taps, out_cells, cols):
    total = None
    for row in range(3):
        term = dot(wide_ref[row * cols : row * cols + out_cells, :], taps(row))
        total = term if total is None else total + term
    return total


def late_body(
    cols, exponent,
    place_ref, own_ref, sib_ref, first_ref, last_ref, q_ref, peak_ref, sum_ref, mix_ref, kv_ref,
    wo_ref, taps_ref, part_ref, wide_ref, mid_ref,
):
    cells = own_ref.shape[0]
    core = place_ref[0]
    state = load_state(peak_ref, sum_ref, mix_ref)
    _, total, mixed = attend(q_ref[...], kv_ref[:cells], kv_ref[cells:], state, exponent)
    change = dot((mixed / total).astype(BF), wo_ref[...])
    near = pl.multiple_of(core * (cells - cols), 16)
    far = pl.multiple_of((1 - core) * (cells - cols), 16)
    far_block = jnp.where(core == 0, first_ref[pl.ds(far, cols), :], last_ref[pl.ds(far, cols), :])
    base = jnp.concatenate([own_ref[...], sib_ref[pl.ds(near, cols), :], far_block], axis=0)
    mid = (base.astype(F32) + change).astype(BF)
    mid_ref[...] = mid[:cells]
    act = jax.nn.silu(mid.astype(F32)).astype(BF).astype(F32)
    near_act = act[cells : cells + cols]
    far_act = jnp.where(place_ref[1] != 0, act[cells + cols :], 0.0)
    above = jnp.where(core == 0, far_act, near_act)
    below = jnp.where(core == 0, near_act, far_act)
    wide_ref[...] = spread(jnp.concatenate([above, act[:cells], below], axis=0), cols)
    first_tap = conv(wide_ref, lambda row: taps_ref[0, row], cells, cols)
    second_tap = conv(wide_ref, lambda row: taps_ref[1, row], cells, cols)
    part_ref[0] = (first_tap + second_tap).astype(BF)
    part_ref[1] = first_tap.astype(BF)


def now_body(cols, wide_ref, mid_ref, taps_ref, skip_ref, out_ref):
    cells = mid_ref.shape[0]
    skip = dot(mid_ref[...], skip_ref[...])
    second_tap = conv(wide_ref, lambda row: taps_ref[1, row], cells, cols)
    last_tap = conv(wide_ref, lambda row: taps_ref[2, row], cells, cols) + skip
    out_ref[0] = last_tap
    out_ref[1] = last_tap + second_tap


def per_device(
    features,
    norm_gain,
    query_weight,
    key_weight,
    value_weight,
    out_weight,
    conv_weight,
    skip_weight,
):
    _, tile_rows, cols, channels = features.shape
    out_channels = conv_weight.shape[-1]
    cells = tile_rows * cols
    devices = lax.axis_size("tile")
    chips = devices // 2
    me = lax.axis_index("tile")
    core = me % 2
    swap = [(i, i ^ 1) for i in range(devices)]
    own = features.reshape(cells, channels)

    def turned(array, by, flip):
        pairs = [(i, ((i + 2 * by) % devices) ^ flip) for i in range(devices)]
        return lax.ppermute(array, "tile", pairs)

    recv = [turned(own, by, 1) for by in range(1, chips)]
    sib = lax.ppermute(own, "tile", swap)
    sums = call(
        stats_body, jax.ShapeDtypeStruct((8, channels), F32), [], 1 << 22, own, sib
    )
    sums = [sums] + [turned(sums, by, 0) for by in range(1, chips)]

    gain = norm_gain.reshape(1, channels)
    exponent = channels ** (-0.5) * 1.4426950408889634
    outside = jnp.where(core == 0, me == 0, me == devices - 1)
    place = jnp.stack([core, 1 - outside.astype(jnp.int32)]).astype(jnp.int32)
    near = cells + cols
    every = near + cols
    taps = conv_weight.reshape(3, 3, 3 * channels, out_channels)
    weights = [query_weight, key_weight, value_weight, out_weight, taps, skip_weight]

    def state_shapes(rows):
        return [
            jax.ShapeDtypeStruct((rows, 128), F32),
            jax.ShapeDtypeStruct((rows, 128), F32),
            jax.ShapeDtypeStruct((rows, channels), F32),
        ]

    n_sums = len(sums)
    norm, q, k, v, *rest = call(
        functools.partial(early_body, devices * cells, cols, exponent, n_sums),
        [
            jax.ShapeDtypeStruct((8, channels), F32),
            jax.ShapeDtypeStruct((near, channels), BF),
            jax.ShapeDtypeStruct((2 * cells, channels), BF),
            jax.ShapeDtypeStruct((2 * cells, channels), BF),
            *state_shapes(near),
            *[jax.ShapeDtypeStruct(w.shape, w.dtype) for w in weights],
        ],
        [pltpu.SemaphoreType.DMA((len(weights),))],
        2 * 10**9,
        place, own, sib, *sums, gain, *[pltpu.with_memory_space_constraint(w, pltpu.HBM) for w in weights],
        spaces=[pltpu.SMEM] + [VMEM] * (3 + n_sums) + [pltpu.HBM] * len(weights),
    )
    state, (wq, wk, wv, wo, taps, ws) = rest[:3], rest[3:]

    kv = [
        call(
            keys_body, jax.ShapeDtypeStruct((2 * cells, channels), BF), [], 10**9,
            block, norm, wk, wv,
        )
        for block in recv
    ]
    rkv = [lax.ppermute(block, "tile", swap) for block in kv]
    q, *state = call(
        functools.partial(join_body, cols, exponent),
        [jax.ShapeDtypeStruct((every, channels), BF), *state_shapes(every)],
        [],
        2 * 10**9,
        place, recv[0], recv[-1], norm, wq, q, k, v, *state, kv[0],
        spaces=[pltpu.SMEM] + [VMEM] * 11,
    )
    for block in kv[1:] + rkv[:-1]:
        state = call(
            functools.partial(more_body, exponent), state_shapes(every), [], 10**9,
            q, *state, block,
        )
    part, wide, mid = call(
        functools.partial(late_body, cols, exponent),
        [
            jax.ShapeDtypeStruct((2, cells, out_channels), BF),
            jax.ShapeDtypeStruct((every, 3 * channels), BF),
            jax.ShapeDtypeStruct((cells, channels), BF),
        ],
        [],
        4 * 10**9,
        place, own, sib, recv[0], recv[-1], q, *state, rkv[-1], wo, taps,
        spaces=[pltpu.SMEM] + [VMEM] * 11,
    )
    spans = lax.axis_size("tm")
    arrived = lax.ppermute(part, "tm", [(i, i + 1) for i in range(spans - 1)])
    now = call(
        functools.partial(now_body, cols),
        jax.ShapeDtypeStruct((2, cells, out_channels), F32),
        [],
        2 * 10**9,
        wide, mid, taps, ws,
    )
    before = jnp.where(lax.axis_index("tm") == 0, part, arrived)
    decoded = (now + before.astype(F32)).astype(BF)
    return decoded.reshape(2, tile_rows, cols, out_channels)


def solution(mesh):
    in_specs = (P("tm", "tile", None, None), P(), P(), P(), P(), P(), P(), P())
    out_specs = P("tm", "tile", None, None)
    return jax.shard_map(
        per_device, mesh=mesh, in_specs=in_specs, out_specs=out_specs, check_vma=False
    )
```

time: 46.3 us -> 39.3 us (0.85)
  waiting for transfers between devices: 14.6 us -> 10.9 us
  local copies, waits for them, and re-layouts: 7.42 us -> 4.67 us
  Pallas kernels: 16.4 us -> 15.8 us
    ppermute x3, waiting for transfers between devices: 10.3 us -> 5.98 us  [the longest x2 5.97 us: turned(): return lax.ppermute(array, 'tile', pairs)]
    unnamed x20 -> x10, local copies, waits for them, and re-layouts: 7.42 us -> 4.67 us
    pallas_call x4 -> x6, Pallas kernels: 16.4 us -> 15.8 us  [call(): pl.pallas_call(body, out_shape=outs, in_specs=[spec(s) for s in spaces],...]
  transfers between devices with their start and end apart: 5 -> 5, of which waited for: 3 -> 3; matrix products, arithmetic and copies ran while one was open for 0% -> 0% of each run, Pallas kernels for 15% -> 26%
where the time goes in v2:
time: 39.3 us; the launch traced here: 39.1 us
  Pallas kernels  15.8 us (40%)
  waiting for transfers between devices  10.9 us (28%)
  starting transfers between devices  6.69 us (17%)
  local copies, waits for them, and re-layouts  4.67 us (12%)
  other arithmetic  0.9 us (2%)
    pallas_call x6, Pallas kernels, call(): pl.pallas_call(body, out_shape=outs, in_specs=[spec(s) for s in spaces],...  15.8 us
    ppermute x2, waiting for transfers between devices, turned(): return lax.ppermute(array, 'tile', pairs)  5.97 us
    ppermute x1, waiting for transfers between devices, per_device(): arrived = lax.ppermute(part, 'tm', [(i, i + 1) for i in range(spans - 1)])  4.7 us
    unnamed x10, local copies, waits for them, and re-layouts  4.67 us
    ppermute x1, starting transfers between devices, per_device(): arrived = lax.ppermute(part, 'tm', [(i, i + 1) for i in range(spans - 1)])  3.4 us
    ppermute x2, starting transfers between devices, turned(): return lax.ppermute(array, 'tile', pairs)  3.22 us
    convert_element_type x1, other arithmetic, per_device(): decoded = (now + before.astype(F32)).astype(BF)  0.82 us
  transfers between devices with their start and end apart: 5, of which 3 were waited for; matrix products, arithmetic and copies ran while one was open for 0% of the time, Pallas kernels for 26%

profile of v2, /device:TPU:24, one launch (start us, length us, event | category | flops | bytes accessed | tf_op | source)
XLA Modules:
  0.0 39.1 jit_solution(612597538947257180)
XLA Ops:
  0.0 0.0 collective-permute-start
  0.0 1.6 %collective-permute-start.1 = (bf16[320,512]{1,0:T(8,128)(2,1)}, bf16[320,512]{1,0:T(8,128)(2,1)S(1)}, u32[]{:S(2)}, u32[]{:S(2)}) collective-permute-start(bf16[320,512]{1,0:T(8,128)(2,1)} %bitcast.7), channel_id=1, source_target_pairs={{0,3},{1,2},{2,1},{3,0},{4,7},{5,6},{6,5},{7,4},{8,11},{9,10},{10,... | collective-permute-start | bytes 983048 | tf_op jit(solution)/shard_map/ppermute | solution.py:266
  1.6 0.2 collective-permute-done.sib_ref
  1.8 0.0 copy-start.2
  1.8 1.0 %copy-done.2 = bf16[1,2,160,512]{3,2,1,0:T(8,128)(2,1)S(1)} copy-done((bf16[1,2,160,512]{3,2,1,0:T(8,128)(2,1)S(1)}, bf16[1,2,160,512]{3,2,1,0:T(8,128)(2,1)}, u32[]{:S(2)}) %copy-start.2) | copy-done | bytes 327704
  2.8 0.1 shard_map.82.refs_0_
  2.9 1.6 %collective-permute-start.2 = (f32[8,512]{1,0:T(8,128)S(1)}, f32[8,512]{1,0:T(8,128)S(1)}, u32[]{:S(2)}, u32[]{:S(2)}) collective-permute-start(f32[8,512]{1,0:T(8,128)S(1)} %shard_map.82.refs_0_), channel_id=1, source_target_pairs={{0,2},{1,3},{2,0},{3,1},{4,6},{5,7},{6,4},{7,5},{8,10},{9,11},{10,... | collective-permute-start | bytes 49160 | tf_op jit(solution)/shard_map/ppermute | solution.py:266
  4.5 0.1 pad_add_fusion.place_ref
  4.6 6.0 %collective-permute-done.2.refs_1_ = f32[8,512]{1,0:T(8,128)S(1)} collective-permute-done((f32[8,512]{1,0:T(8,128)S(1)}, f32[8,512]{1,0:T(8,128)S(1)}, u32[]{:S(2)}, u32[]{:S(2)}) %collective-permute-start.2) | collective-permute-done | bytes 16416 | tf_op jit(solution)/shard_map/ppermute | solution.py:266
  10.6 0.0 copy-start.4
  10.6 0.7 %copy-done.4 = f32[512]{0:T(512)S(1)} copy-done((f32[512]{0:T(512)S(1)}, f32[512]{0:T(512)}, u32[]{:S(2)}) %copy-start.4) | copy-done | bytes 2072
  11.3 4.7 %shard_map.83 = (f32[8,512]{1,0:T(8,128)S(1)}, bf16[480,512]{1,0:T(8,128)(2,1)S(1)}, bf16[640,512]{1,0:T(8,128)(2,1)S(1)}, bf16[640,512]{1,0:T(8,128)(2,1)S(1)},...) custom-call(s32[2]{0:T(128)S(1)} %pad_add_fusion.place_ref, ...), custom_call_target="tpu_custom_call" | custom-call | flops 2000000000 | bytes 1048576 | tf_op jit(solution)/shard_map/pallas_call | solution.py:31
  16.0 0.0 copy-start
  16.0 0.0 copy-start.3
  16.0 0.0 collective-permute-done.1.block_ref.first_ref.last_ref
  16.0 0.5 %shard_map.84.kv_ref = bf16[640,512]{1,0:T(8,128)(2,1)S(1)} custom-call(bf16[320,512]{1,0:T(8,128)(2,1)S(1)} %collective-permute-done.1.block_ref.first_ref.last_ref, f32[8,512]{1,0:T(8,128)S(1)} %get-tuple-element.25.norm_ref, bf16[512,512]{1,0:T(8,128)(2,1)S(1)} %get-tuple-element.33.wk_ref, bf16[512,512]{1,0:T(8,128)(2,1)S(1)} %get-tuple-element.34.wv_ref), custom_call_target="tpu_custom_call" | custom-call | flops 1000000000 | bytes 1048576 | tf_op jit(solution)/shard_map/pallas_call | solution.py:31
  16.5 0.1 collective-permute-start.3
  16.6 3.6 %shard_map.85 = (bf16[640,512]{1,0:T(8,128)(2,1)S(1)}, f32[640,128]{1,0:T(8,128)S(1)}, f32[640,128]{1,0:T(8,128)S(1)}, f32[640,512]{1,0:T(8,128)S(1)}) custom-call(s32[2]{0:T(128)S(1)} %pad_add_fusion.place_ref, bf16[320,512]{1,0:T(8,128)(2,1)S(1)} %collective-permute-done.1.block_ref.first_ref.last_ref, ...), custom_call_target="tpu_custom_call" | custom-call | flops 2000000000 | bytes 1048576 | tf_op jit(solution)/shard_map/pallas_call | solution.py:31
  20.2 0.0 collective-permute-done.3.kv_ref
  20.3 0.0 copy-done.3
  20.3 5.1 %shard_map.86 = (bf16[2,320,256]{2,1,0:T(8,128)(2,1)S(1)}, bf16[640,1536]{1,0:T(8,128)(2,1)S(1)}, bf16[320,512]{1,0:T(8,128)(2,1)S(1)}) custom-call(s32[2]{0:T(128)S(1)} %pad_add_fusion.place_ref, bf16[320,512]{1,0:T(8,128)(2,1)S(1)} %bitcast.10, bf16[320,512]{1,0:T(8,128)(2,1)S(1)} %collective-permute-done.sib_ref, ...), custom_call_target="tpu_custom_call" | custom-call | flops 4000000000 | bytes 1048576 | tf_op jit(solution)/shard_map/pallas_call | solution.py:31
  25.3 0.0 copy-done
  25.3 3.4 %collective-permute-start.4 = (bf16[2,320,256]{2,1,0:T(8,128)(2,1)S(1)}, bf16[2,320,256]{2,1,0:T(8,128)(2,1)S(1)}, u32[]{:S(2)}, u32[]{:S(2)}) collective-permute-start(bf16[2,320,256]{2,1,0:T(8,128)(2,1)S(1)} %get-tuple-element.44), channel_id=1, source_target_pairs={{0,4},{4,8},{8,12},{12,16},{16,20},{20,24},{24,28},{1,5},{5,9},{9,... | collective-permute-start | bytes 983048 | tf_op jit(solution)/shard_map/ppermute | solution.py:343
  28.8 0.0 copy-start.1
  28.8 3.0 %copy-done.1 = bf16[3,3,1536,256]{3,2,1,0:T(8,128)(2,1)S(1)} copy-done((bf16[3,3,1536,256]{3,2,1,0:T(8,128)(2,1)S(1)}, bf16[3,3,1536,256]{3,2,1,0:T(8,128)(2,1)}, u32[]{:S(2)}) %copy-start.1) | copy-done | bytes 7077912
  31.8 1.8 %shard_map.87 = f32[2,320,256]{2,1,0:T(8,128)S(1)} custom-call(bf16[640,1536]{1,0:T(8,128)(2,1)S(1)} %get-tuple-element.41.wide_ref, bf16[320,512]{1,0:T(8,128)(2,1)S(1)} %get-tuple-element.42.mid_ref, bf16[3,3,1536,256]{3,2,1,0:T(8,128)(2,1)S(1)} %copy-done.1, bf16[512,256]{1,0:T(8,128)(2,1)S(1)} %get-tuple-element.43.skip_ref), custom_call_target="tpu_custom_call" | custom-call | flops 2000000000 | bytes 1048576 | tf_op jit(solution)/shard_map/pallas_call | solution.py:31
  33.5 4.7 %collective-permute-done.4 = bf16[2,320,256]{2,1,0:T(8,128)(2,1)S(1)} collective-permute-done((bf16[2,320,256]{2,1,0:T(8,128)(2,1)S(1)}, bf16[2,320,256]{2,1,0:T(8,128)(2,1)S(1)}, u32[]{:S(2)}, u32[]{:S(2)}) %collective-permute-start.4) | collective-permute-done | bytes 327712 | tf_op jit(solution)/shard_map/ppermute | solution.py:343
  38.2 0.8 %add_convert_fusion = bf16[2,320,256]{2,1,0:T(8,128)(2,1)} fusion(f32[2,320,256]{2,1,0:T(8,128)S(1)} %shard_map.87, bf16[2,320,256]{2,1,0:T(8,128)(2,1)S(1)} %get-tuple-element.44, bf16[2,320,256]{2,1,0:T(8,128)(2,1)S(1)} %collective-permute-done.4, pred[]{:T(512)S(6)} %eq.17), kind=kLoop, calls=%fused_computation | loop fusion | flops 655360 | bytes 1638401 | tf_op jit(solution)/shard_map/convert_element_type | solution.py:352
Async XLA Ops:
  0.0 1.8 %collective-permute-start = (bf16[320,512]{1,0:T(8,128)(2,1)}, bf16[320,512]{1,0:T(8,128)(2,1)S(1)}, u32[]{:S(2)}, u32[]{:S(2)}) collective-permute-start(bf16[320,512]{1,0:T(8,128)(2,1)} %bitcast.6), channel_id=1, source_target_pairs={{0,1},{1,0},{2,3},{3,2},{4,5},{5,4},{6,7},{7,6},{8,9},{9,8},{10,11... | collective-permute-start | bytes 983048 | tf_op jit(solution)/shard_map/ppermute | solution.py:269
  0.0 16.0 %collective-permute-start.1 = (bf16[320,512]{1,0:T(8,128)(2,1)}, bf16[320,512]{1,0:T(8,128)(2,1)S(1)}, u32[]{:S(2)}, u32[]{:S(2)}) collective-permute-start(bf16[320,512]{1,0:T(8,128)(2,1)} %bitcast.7), channel_id=1, source_target_pairs={{0,3},{1,2},{2,1},{3,0},{4,7},{5,6},{6,5},{7,4},{8,11},{9,10},{10,... | collective-permute-start | bytes 983048 | tf_op jit(solution)/shard_map/ppermute | solution.py:266
  1.8 1.0 %copy-start.2 = (bf16[1,2,160,512]{3,2,1,0:T(8,128)(2,1)S(1)}, bf16[1,2,160,512]{3,2,1,0:T(8,128)(2,1)}, u32[]{:S(2)}) copy-start(bf16[1,2,160,512]{3,2,1,0:T(8,128)(2,1)} %param.8) | copy-start | bytes 983044
  2.9 7.6 %collective-permute-start.2 = (f32[8,512]{1,0:T(8,128)S(1)}, f32[8,512]{1,0:T(8,128)S(1)}, u32[]{:S(2)}, u32[]{:S(2)}) collective-permute-start(f32[8,512]{1,0:T(8,128)S(1)} %shard_map.82.refs_0_), channel_id=1, source_target_pairs={{0,2},{1,3},{2,0},{3,1},{4,6},{5,7},{6,4},{7,5},{8,10},{9,11},{10,... | collective-permute-start | bytes 49160 | tf_op jit(solution)/shard_map/ppermute | solution.py:266
  10.6 0.7 %copy-start.4 = (f32[512]{0:T(512)S(1)}, f32[512]{0:T(512)}, u32[]{:S(2)}) copy-start(f32[512]{0:T(512)} %param.9) | copy-start | bytes 6148
  16.0 9.3 %copy-start = (bf16[3,3,1536,256]{3,2,1,0:T(8,128)(2,1)}, bf16[3,3,1536,256]{3,2,1,0:T(8,128)(2,1)S(1)}, u32[]{:S(2)}) copy-start(bf16[3,3,1536,256]{3,2,1,0:T(8,128)(2,1)S(1)} %get-tuple-element.40.taps_ref) | copy-start | bytes 21233668
  16.0 4.2 %copy-start.3 = (bf16[1,2,160,512]{3,2,1,0:T(8,128)(2,1)S(1)}, bf16[1,2,160,512]{3,2,1,0:T(8,128)(2,1)}, u32[]{:S(2)}) copy-start(bf16[1,2,160,512]{3,2,1,0:T(8,128)(2,1)} %param.8) | copy-start | bytes 983044
  16.5 3.7 %collective-permute-start.3 = (bf16[640,512]{1,0:T(8,128)(2,1)S(1)}, bf16[640,512]{1,0:T(8,128)(2,1)S(1)}, u32[]{:S(2)}, u32[]{:S(2)}) collective-permute-start(bf16[640,512]{1,0:T(8,128)(2,1)S(1)} %shard_map.84.kv_ref), channel_id=1, source_target_pairs={{0,1},{1,0},{2,3},{3,2},{4,5},{5,4},{6,7},{7,6},{8,9},{9,8},{10,11... | collective-permute-start | bytes 1966088 | tf_op jit(solution)/shard_map/ppermute | solution.py:316
  25.3 12.9 %collective-permute-start.4 = (bf16[2,320,256]{2,1,0:T(8,128)(2,1)S(1)}, bf16[2,320,256]{2,1,0:T(8,128)(2,1)S(1)}, u32[]{:S(2)}, u32[]{:S(2)}) collective-permute-start(bf16[2,320,256]{2,1,0:T(8,128)(2,1)S(1)} %get-tuple-element.44), channel_id=1, source_target_pairs={{0,4},{4,8},{8,12},{12,16},{16,20},{20,24},{24,28},{1,5},{5,9},{9,... | collective-permute-start | bytes 983048 | tf_op jit(solution)/shard_map/ppermute | solution.py:343
  28.8 3.0 %copy-start.1 = (bf16[3,3,1536,256]{3,2,1,0:T(8,128)(2,1)S(1)}, bf16[3,3,1536,256]{3,2,1,0:T(8,128)(2,1)}, u32[]{:S(2)}) copy-start(bf16[3,3,1536,256]{3,2,1,0:T(8,128)(2,1)} %copy-done) | copy-start | bytes 21233668

commit v3 on v2

v3 whole, which is shorter than its diff:
```python
import functools

import jax
import jax.numpy as jnp
from jax import lax
from jax.experimental import pallas as pl
from jax.experimental.pallas import tpu as pltpu
from jax.sharding import PartitionSpec as P

GROUPS = 32
BF = jnp.bfloat16
F32 = jnp.float32
VMEM = pltpu.VMEM
LIMIT = 20 * 1024 * 1024
PIECES = 4


def dot(left, right):
    return jnp.dot(left, right, preferred_element_type=F32)


def dot_t(left, right):
    return lax.dot_general(left, right, (((1,), (1,)), ((), ())), preferred_element_type=F32)


def spec(space=VMEM):
    return pl.BlockSpec(memory_space=space)


def hbm(array):
    return pltpu.with_memory_space_constraint(array, pltpu.HBM)


def call(body, outs, scratch, cost, *args, spaces=None):
    spaces = spaces or [VMEM] * len(args)
    return pl.pallas_call(
        body,
        out_shape=outs,
        in_specs=[spec(s) for s in spaces],
        out_specs=jax.tree.map(lambda _: spec(), outs),
        scratch_shapes=scratch,
        compiler_params=pltpu.CompilerParams(vmem_limit_bytes=LIMIT),
        cost_estimate=pl.CostEstimate(flops=cost, bytes_accessed=1 << 20, transcendentals=0),
    )(*args)


def stats_body(features_ref, sums_ref, own_ref, sems):
    rows = own_ref.shape[0] // PIECES
    copies = []
    for i in range(PIECES):
        piece = pl.ds(i * rows, rows)
        copies.append(
            pltpu.make_async_copy(features_ref.at[piece], own_ref.at[piece], sems.at[i])
        )
        copies[-1].start()
    total = jnp.zeros((1, own_ref.shape[1]), F32)
    squared = total
    for i in range(PIECES):
        copies[i].wait()
        block = own_ref[i * rows : (i + 1) * rows].astype(F32)
        total += jnp.sum(block, axis=0, keepdims=True)
        squared += jnp.sum(block * block, axis=0, keepdims=True)
    sums_ref[...] = jnp.concatenate(
        [total, squared, jnp.zeros((6, own_ref.shape[1]), F32)], axis=0
    )


def group_sums(sums, width):
    lane = lax.broadcasted_iota(jnp.int32, sums.shape, 1)
    size = sums.shape[1]
    step = 1
    while step < width:
        low = pltpu.roll(sums, size - step, 1)
        high = pltpu.roll(sums, step, 1)
        sums = sums + jnp.where((lane & step) == 0, low, high)
        step *= 2
    return sums


def moments(sum_refs, cells):
    sums = 0.0
    for ref in sum_refs:
        for first in range(0, ref.shape[0], 8):
            sums = sums + ref[first : first + 8]
    width = sums.shape[1] // GROUPS
    sums = group_sums(sums, width)
    population = cells * width
    mean = sums[0:1] / population
    var = sums[1:2] / population - mean * mean
    return mean, lax.rsqrt(var + 1e-06)


def normalise(block, mean, inverse, gain):
    return ((block.astype(F32) - mean) * inverse * gain).astype(BF)


def attend(queries, keys, values, exponent, peak_ref, sum_ref, mix_ref):
    scores = dot_t(queries, keys)
    peak = jnp.max(scores, axis=1, keepdims=True)
    unnormed = jnp.exp2((scores - peak) * exponent)
    peak_ref[...] = jnp.broadcast_to(peak, peak_ref.shape)
    sum_ref[...] = jnp.broadcast_to(jnp.sum(unnormed, axis=1, keepdims=True), sum_ref.shape)
    mix_ref[...] = dot(unnormed.astype(BF), values)


def merge(old, new, out_refs, exponent, last):
    peak = jnp.maximum(old[0][...], new[0][...])
    fade_old = jnp.exp2((old[0][...] - peak) * exponent)
    fade_new = jnp.exp2((new[0][...] - peak) * exponent)
    total = old[1][...] * fade_old + new[1][...] * fade_new
    if last:
        scale = 1.0 / total
        fade_old = fade_old * scale
        fade_new = fade_new * scale
    else:
        out_refs[0][...] = peak
        out_refs[1][...] = total
    width = peak.shape[1]
    for first in range(0, old[2].shape[1], width):
        lanes = slice(first, first + width)
        mixed = old[2][:, lanes] * fade_old + new[2][:, lanes] * fade_new
        out_refs[-1][:, lanes] = mixed.astype(out_refs[-1].dtype)


def early_body(
    cells_all, cols, exponent, n_sums,
    place_ref, own_ref, sib_ref, *refs,
):
    sum_refs, refs = refs[:n_sums], refs[n_sums:]
    hbm_refs, refs = refs[:6], refs[6:]
    norm_ref, q_ref, k_ref, v_ref, *state_refs = refs[:7]
    held_refs, gain_ref, sems = refs[7:12], refs[12], refs[13]
    sources = (*hbm_refs[:5], hbm_refs[5].at[pl.ds(0, 2)])
    copies = [
        pltpu.make_async_copy(source, target, sems.at[i])
        for i, (source, target) in enumerate(zip(sources, (gain_ref, *held_refs), strict=True))
    ]
    for copy in copies[:4]:
        copy.start()
    wq_ref, wk_ref, wv_ref = held_refs[:3]
    mean, inverse = moments(sum_refs, cells_all)
    copies[0].wait()
    gain = gain_ref[...]
    norm_ref[...] = jnp.concatenate(
        [mean, inverse, gain, jnp.zeros((5, mean.shape[1]), F32)], axis=0
    )
    cells = own_ref.shape[0]
    core = place_ref[0]
    own = normalise(own_ref[...], mean, inverse, gain)
    sib = normalise(sib_ref[...], mean, inverse, gain)
    near = pl.multiple_of(core * (cells - cols), 16)
    halo = normalise(sib_ref[pl.ds(near, cols), :], mean, inverse, gain)
    both = jnp.concatenate([own, sib], axis=0)
    for copy in copies[1:4]:
        copy.wait()
    for copy in copies[4:]:
        copy.start()
    q_ref[...] = dot(jnp.concatenate([own, halo], axis=0), wq_ref[...]).astype(BF)
    k_ref[...] = dot(both, wk_ref[...]).astype(BF)
    v_ref[...] = dot(both, wv_ref[...]).astype(BF)
    attend(q_ref[...], k_ref[...], v_ref[...], exponent, *state_refs)
    for copy in copies[4:]:
        copy.wait()


def normal_of(norm_ref):
    return norm_ref[0:1], norm_ref[1:2], norm_ref[2:3]


def far_rows(place_ref, first_ref, last_ref, cols):
    core = place_ref[0]
    far = pl.multiple_of((1 - core) * (first_ref.shape[0] - cols), 16)
    first = first_ref[pl.ds(far, cols), :]
    if last_ref is None:
        return first
    return jnp.where(core == 0, first, last_ref[pl.ds(far, cols), :])


def project(block_ref, norm_ref, wk_ref, wv_ref, k_ref, v_ref):
    normed = normalise(block_ref[...], *normal_of(norm_ref))
    k_ref[...] = dot(normed, wk_ref[...]).astype(BF)
    v_ref[...] = dot(normed, wv_ref[...]).astype(BF)


def join_body(cols, exponent, single, place_ref, *refs):
    first_ref, refs = refs[0], refs[1:]
    last_ref, refs = (None, refs) if single else (refs[0], refs[1:])
    (norm_ref, wq_ref, wk_ref, wv_ref, q_ref, k_ref, v_ref, peak_ref, sum_ref, mix_ref,
     all_q_ref, all_peak_ref, all_sum_ref, all_mix_ref, new_k_ref, new_v_ref) = refs
    near = q_ref.shape[0]
    far_q = dot(
        normalise(far_rows(place_ref, first_ref, last_ref, cols), *normal_of(norm_ref)),
        wq_ref[...],
    ).astype(BF)
    project(first_ref, norm_ref, wk_ref, wv_ref, new_k_ref, new_v_ref)
    all_q_ref[:near] = q_ref[...]
    all_q_ref[near:] = far_q
    every = (all_peak_ref, all_sum_ref, all_mix_ref)
    for old, new in zip((peak_ref, sum_ref, mix_ref), every, strict=True):
        new[:near] = old[...]
    attend(
        far_q, k_ref[...], v_ref[...], exponent, *[ref.at[pl.ds(near, cols)] for ref in every]
    )


def more_body(exponent, block_ref, norm_ref, wk_ref, wv_ref, q_ref, *refs):
    old, out, new = refs[:3], refs[3:6], refs[6:9]
    k_ref, v_ref = refs[9:]
    project(block_ref, norm_ref, wk_ref, wv_ref, k_ref, v_ref)
    attend(q_ref[...], k_ref[...], v_ref[...], exponent, *new)
    merge(old, new, out, exponent, False)


def spread(act, cols):
    size = act.shape[0]
    col = lax.broadcasted_iota(jnp.int32, act.shape, 0) % cols
    left = jnp.where(col == 0, 0.0, pltpu.roll(act, 1, 0))
    right = jnp.where(col == cols - 1, 0.0, pltpu.roll(act, size - 1, 0))
    return jnp.concatenate([left.astype(BF), act.astype(BF), right.astype(BF)], axis=1)


def conv(wide_ref, taps, out_cells, cols):
    total = None
    for row in range(3):
        term = dot(wide_ref[row * cols : row * cols + out_cells, :], taps(row))
        total = term if total is None else total + term
    return total


def late_body(cols, exponent, single, place_ref, own_ref, sib_ref, *refs):
    first_ref, refs = refs[0], refs[1:]
    last_ref, refs = (None, refs) if single else (refs[0], refs[1:])
    (block_ref, norm_ref, q_ref, peak_ref, sum_ref, mix_ref, k_ref, v_ref, wk_ref, wv_ref, wo_ref,
     taps_ref, part_ref, wide_ref, mid_ref, keys_ref, values_ref, *new, attended_ref) = refs
    cells = own_ref.shape[0]
    core = place_ref[0]
    keys_ref[:cells] = k_ref[...]
    values_ref[:cells] = v_ref[...]
    rest = pl.ds(cells, cells)
    project(block_ref, norm_ref, wk_ref, wv_ref, keys_ref.at[rest], values_ref.at[rest])
    attend(q_ref[...], keys_ref[...], values_ref[...], exponent, *new)
    merge((peak_ref, sum_ref, mix_ref), new, (attended_ref,), exponent, True)
    change = dot(attended_ref[...], wo_ref[...])
    near = pl.multiple_of(core * (cells - cols), 16)
    far_block = far_rows(place_ref, first_ref, last_ref, cols)
    base = jnp.concatenate([own_ref[...], sib_ref[pl.ds(near, cols), :], far_block], axis=0)
    mid = (base.astype(F32) + change).astype(BF)
    mid_ref[...] = mid[:cells]
    act = jax.nn.silu(mid.astype(F32)).astype(BF).astype(F32)
    near_act = act[cells : cells + cols]
    far_act = jnp.where(place_ref[1] != 0, act[cells + cols :], 0.0)
    above = jnp.where(core == 0, far_act, near_act)
    below = jnp.where(core == 0, near_act, far_act)
    wide_ref[...] = spread(jnp.concatenate([above, act[:cells], below], axis=0), cols)
    first_tap = conv(wide_ref, lambda row: taps_ref[0, row], cells, cols)
    second_tap = conv(wide_ref, lambda row: taps_ref[1, row], cells, cols)
    part_ref[0] = (first_tap + second_tap).astype(BF)
    part_ref[1] = first_tap.astype(BF)


def now_body(cols, wide_ref, mid_ref, conv_ref, skip_ref, out_ref, taps_ref, skip_held_ref, sems):
    copies = [
        pltpu.make_async_copy(skip_ref, skip_held_ref, sems.at[0]),
        pltpu.make_async_copy(conv_ref.at[pl.ds(1, 2)], taps_ref, sems.at[1]),
    ]
    for copy in copies:
        copy.start()
    cells = mid_ref.shape[0]
    copies[0].wait()
    skip = dot(mid_ref[...], skip_held_ref[...])
    copies[1].wait()
    second_tap = conv(wide_ref, lambda row: taps_ref[0, row], cells, cols)
    last_tap = conv(wide_ref, lambda row: taps_ref[1, row], cells, cols) + skip
    out_ref[0] = last_tap
    out_ref[1] = last_tap + second_tap


def per_device(
    features,
    norm_gain,
    query_weight,
    key_weight,
    value_weight,
    out_weight,
    conv_weight,
    skip_weight,
):
    _, tile_rows, cols, channels = features.shape
    out_channels = conv_weight.shape[-1]
    cells = tile_rows * cols
    devices = lax.axis_size("tile")
    chips = devices // 2
    me = lax.axis_index("tile")
    core = me % 2
    swap = [(i, i ^ 1) for i in range(devices)]
    own = features.reshape(cells, channels)

    def turned(array, by, flip):
        pairs = [(i, ((i + 2 * by) % devices) ^ flip) for i in range(devices)]
        return lax.ppermute(array, "tile", pairs)

    sib = lax.ppermute(own, "tile", swap)
    sums, own = call(
        stats_body,
        [jax.ShapeDtypeStruct((8, channels), F32), jax.ShapeDtypeStruct(own.shape, BF)],
        [pltpu.SemaphoreType.DMA((PIECES,))],
        1 << 22,
        hbm(own),
        spaces=[pltpu.HBM],
    )
    sums = [sums] + [turned(sums, by, 1) for by in range(1, chips)]
    recv = [turned(own, by, 1) for by in range(1, chips)]
    sums = jnp.concatenate(sums, axis=0)
    sums = [sums, lax.ppermute(sums, "tile", swap)]

    exponent = channels ** (-0.5) * 1.4426950408889634
    outside = jnp.where(core == 0, me == 0, me == devices - 1)
    place = jnp.stack([core, 1 - outside.astype(jnp.int32)]).astype(jnp.int32)
    near = cells + cols
    every = near + cols
    taps = conv_weight.reshape(3, 3, 3 * channels, out_channels)
    weights = [norm_gain.reshape(1, channels), query_weight, key_weight, value_weight, out_weight]
    first_taps = (2, *taps.shape[1:])

    def rows_of(rows, kind=BF, width=channels):
        return jax.ShapeDtypeStruct((rows, width), kind)

    def state_of(rows):
        return [rows_of(rows, F32, 128), rows_of(rows, F32, 128), rows_of(rows, F32)]

    def scratch_of(shapes):
        return [VMEM(shape.shape, shape.dtype) for shape in shapes]

    n_sums = len(sums)
    norm, q, k, v, *rest = call(
        functools.partial(early_body, devices * cells, cols, exponent, n_sums),
        [
            rows_of(8, F32),
            rows_of(near),
            rows_of(2 * cells),
            rows_of(2 * cells),
            *state_of(near),
            *[jax.ShapeDtypeStruct(w.shape, w.dtype) for w in weights[1:]],
            jax.ShapeDtypeStruct(first_taps, BF),
        ],
        [VMEM((1, channels), F32), pltpu.SemaphoreType.DMA((len(weights) + 1,))],
        2 * 10**9,
        place, own, sib, *sums, *[hbm(w) for w in weights], hbm(taps),
        spaces=[pltpu.SMEM] + [VMEM] * (2 + n_sums) + [pltpu.HBM] * (len(weights) + 1),
    )
    state, (wq, wk, wv, wo, held_taps) = rest[:3], rest[3:]

    *recv, norm = lax.optimization_barrier((*recv, norm))
    rsib = [lax.ppermute(block, "tile", swap) for block in recv]
    ends = recv[:1] if chips == 2 else [recv[0], recv[-1]]
    q, *state, new_k, new_v = call(
        functools.partial(join_body, cols, exponent, chips == 2),
        [rows_of(every), *state_of(every), rows_of(cells), rows_of(cells)],
        [],
        2 * 10**9,
        place, *ends, norm, wq, wk, wv, q, k, v, *state,
        spaces=[pltpu.SMEM] + [VMEM] * (10 + len(ends)),
    )
    for block in recv[1:] + rsib[:-1]:
        state = call(
            functools.partial(more_body, exponent),
            state_of(every),
            scratch_of([*state_of(every), rows_of(cells), rows_of(cells)]),
            10**9,
            block, norm, wk, wv, q, *state,
        )
    part, wide, mid = call(
        functools.partial(late_body, cols, exponent, chips == 2),
        [
            jax.ShapeDtypeStruct((2, cells, out_channels), BF),
            rows_of(every, BF, 3 * channels),
            rows_of(cells),
        ],
        scratch_of([rows_of(2 * cells), rows_of(2 * cells), *state_of(every), rows_of(every)]),
        4 * 10**9,
        place, own, sib, *ends, rsib[-1], norm, q, *state, new_k, new_v, wk, wv, wo, held_taps,
        spaces=[pltpu.SMEM] + [VMEM] * (14 + len(ends)),
    )
    spans = lax.axis_size("tm")
    arrived = lax.ppermute(part, "tm", [(i, i + 1) for i in range(spans - 1)])
    now = call(
        functools.partial(now_body, cols),
        jax.ShapeDtypeStruct((2, cells, out_channels), F32),
        [VMEM(first_taps, BF), VMEM(skip_weight.shape, BF), pltpu.SemaphoreType.DMA((2,))],
        2 * 10**9,
        wide, mid, hbm(taps), hbm(skip_weight),
        spaces=[VMEM, VMEM, pltpu.HBM, pltpu.HBM],
    )
    before = jnp.where(lax.axis_index("tm") == 0, part, arrived)
    decoded = (now + before.astype(F32)).astype(BF)
    return decoded.reshape(2, tile_rows, cols, out_channels)


def solution(mesh):
    in_specs = (P("tm", "tile", None, None), P(), P(), P(), P(), P(), P(), P())
    out_specs = P("tm", "tile", None, None)
    return jax.shard_map(
        per_device, mesh=mesh, in_specs=in_specs, out_specs=out_specs, check_vma=False
    )
```

time: 39.3 us -> 34.4 us (0.88)
  local copies, waits for them, and re-layouts: 4.67 us -> 0.98 us
  waiting for transfers between devices: 10.9 us -> 9.53 us
  Pallas kernels: 15.8 us -> 16.8 us
  starting transfers between devices: 6.69 us -> 5.86 us
    unnamed x10 -> x5, local copies, waits for them, and re-layouts: 4.67 us -> 0.97 us
    ppermute x2, waiting for transfers between devices: 5.97 us -> 3.53 us  [turned(): return lax.ppermute(array, 'tile', pairs)]
    ppermute x2, starting transfers between devices: 3.22 us -> 1.81 us  [turned(): return lax.ppermute(array, 'tile', pairs)]
    pallas_call x6 -> x5, Pallas kernels: 15.8 us -> 16.8 us  [call(): pl.pallas_call(body, out_shape=outs, in_specs=[spec(s) for s in spaces],...]
    ppermute x1 -> x2, waiting for transfers between devices: 0.01 us -> 0.79 us  [the longest x1 0.78 us: per_device(): sums = [sums, lax.ppermute(sums, 'tile', swap)]]
    ppermute x1 -> x2, starting transfers between devices: 0.07 us -> 0.62 us  [the longest x1 0.51 us: per_device(): sums = [sums, lax.ppermute(sums, 'tile', swap)]]
    ppermute x1, waiting for transfers between devices: 4.7 us -> 5.21 us  [per_device(): arrived = lax.ppermute(part, 'tm', [(i, i + 1) for i in range(spans - 1)])]
  transfers between devices with their start and end apart: 5 -> 6, of which waited for: 3 -> 4; matrix products, arithmetic and copies ran while one was open for 0% -> 0% of each run, Pallas kernels for 26% -> 34%
where the time goes in v3:
time: 34.4 us; the launch traced here: 34.1 us
  Pallas kernels  16.8 us (49%)
  waiting for transfers between devices  9.53 us (28%)
  starting transfers between devices  5.86 us (17%)
  local copies, waits for them, and re-layouts  0.98 us (3%)
  other arithmetic  0.9 us (3%)
    pallas_call x5, Pallas kernels, call(): pl.pallas_call(body, out_shape=outs, in_specs=[spec(s) for s in spaces],...  16.8 us
    ppermute x1, waiting for transfers between devices, per_device(): arrived = lax.ppermute(part, 'tm', [(i, i + 1) for i in range(spans - 1)])  5.21 us
    ppermute x2, waiting for transfers between devices, turned(): return lax.ppermute(array, 'tile', pairs)  3.53 us
    ppermute x1, starting transfers between devices, per_device(): arrived = lax.ppermute(part, 'tm', [(i, i + 1) for i in range(spans - 1)])  3.43 us
    ppermute x2, starting transfers between devices, turned(): return lax.ppermute(array, 'tile', pairs)  1.81 us
    unnamed x5, local copies, waits for them, and re-layouts  0.97 us
    convert_element_type x1, other arithmetic, per_device(): decoded = (now + before.astype(F32)).astype(BF)  0.82 us
    ppermute x1, waiting for transfers between devices, per_device(): sums = [sums, lax.ppermute(sums, 'tile', swap)]  0.78 us
  transfers between devices with their start and end apart: 6, of which 4 were waited for; matrix products, arithmetic and copies ran while one was open for 0% of the time, Pallas kernels for 34%

profile of v3, /device:TPU:24, one launch (start us, length us, event | category | flops | bytes accessed | tf_op | source)
XLA Modules:
  0.0 34.1 jit_solution(962492502534917829)
XLA Ops:
  0.0 0.0 collective-permute-start
  0.0 1.1 %shard_map.82 = (f32[8,512]{1,0:T(8,128)S(1)}, bf16[320,512]{1,0:T(8,128)(2,1)S(1)}) custom-call(bf16[320,512]{1,0:T(8,128)(2,1)} %bitcast.9), custom_call_target="tpu_custom_call" | custom-call | flops 4194304 | bytes 1048576 | tf_op jit(solution)/shard_map/pallas_call | solution.py:36
  1.1 1.7 %collective-permute-start.2 = (f32[8,512]{1,0:T(8,128)S(1)}, f32[8,512]{1,0:T(8,128)S(1)}, u32[]{:S(2)}, u32[]{:S(2)}) collective-permute-start(f32[8,512]{1,0:T(8,128)S(1)} %get-tuple-element.31), channel_id=1, source_target_pairs={{0,3},{1,2},{2,1},{3,0},{4,7},{5,6},{6,5},{7,4},{8,11},{9,10},{10,... | collective-permute-start | bytes 49160 | tf_op jit(solution)/shard_map/ppermute | solution.py:300
  2.8 0.1 collective-permute-start.1
  2.9 1.4 %collective-permute-done.2 = f32[8,512]{1,0:T(8,128)S(1)} collective-permute-done((f32[8,512]{1,0:T(8,128)S(1)}, f32[8,512]{1,0:T(8,128)S(1)}, u32[]{:S(2)}, u32[]{:S(2)}) %collective-permute-start.2) | collective-permute-done | bytes 16416 | tf_op jit(solution)/shard_map/ppermute | solution.py:300
  4.3 0.5 %collective-permute-start.3 = (f32[16,512]{1,0:T(8,128)S(1)}, f32[16,512]{1,0:T(8,128)S(1)}, u32[]{:S(2)}, u32[]{:S(2)}) collective-permute-start(f32[16,512]{1,0:T(8,128)S(1)} %constant_dynamic-update-slice_fusion.refs_0_), channel_id=1, source_target_pairs={{0,1},{1,0},{2,3},{3,2},{4,5},{5,4},{6,7},{7,6},{8,9},{9,8},{10,11... | collective-permute-start | bytes 98312 | tf_op jit(solution)/shard_map/ppermute | solution.py:314
  4.8 0.1 pad_add_fusion.place_ref
  4.9 0.8 %collective-permute-done.3.refs_1_ = f32[16,512]{1,0:T(8,128)S(1)} collective-permute-done((f32[16,512]{1,0:T(8,128)S(1)}, f32[16,512]{1,0:T(8,128)S(1)}, u32[]{:S(2)}, u32[]{:S(2)}) %collective-permute-start.3) | collective-permute-done | bytes 32800 | tf_op jit(solution)/shard_map/ppermute | solution.py:314
  5.7 0.0 collective-permute-done.sib_ref
  5.7 4.8 %shard_map.83 = (f32[8,512]{1,0:T(8,128)S(1)}, bf16[480,512]{1,0:T(8,128)(2,1)S(1)}, bf16[640,512]{1,0:T(8,128)(2,1)S(1)}, bf16[640,512]{1,0:T(8,128)(2,1)S(1)},...) custom-call(s32[2]{0:T(128)S(1)} %pad_add_fusion.place_ref, ...), custom_call_target="tpu_custom_call" | custom-call | flops 2000000000 | bytes 1048576 | tf_op jit(solution)/shard_map/pallas_call | solution.py:36
  10.5 2.1 %collective-permute-done.1.refs_0_ = bf16[320,512]{1,0:T(8,128)(2,1)S(1)} collective-permute-done((bf16[320,512]{1,0:T(8,128)(2,1)S(1)}, bf16[320,512]{1,0:T(8,128)(2,1)S(1)}, u32[]{:S(2)}, u32[]{:S(2)}) %collective-permute-start.1) | collective-permute-done | bytes 327712 | tf_op jit(solution)/shard_map/ppermute | solution.py:300
  12.6 0.0 copy-start
  12.6 0.1 collective-permute-start.4
  12.7 1.7 %shard_map.84 = (bf16[640,512]{1,0:T(8,128)(2,1)S(1)}, f32[640,128]{1,0:T(8,128)S(1)}, f32[640,128]{1,0:T(8,128)S(1)}, f32[640,512]{1,0:T(8,128)S(1)}, bf16[320,...) custom-call(s32[2]{0:T(128)S(1)} %pad_add_fusion.place_ref, bf16[320,512]{1,0:T(8,128)(2,1)S(1)} %collective-permute-done.1.refs_0_, ...), custom_call_target="tpu_custom_call" | custom-call | flops 2000000000 | bytes 1048576 | tf_op jit(solution)/shard_map/pallas_call | solution.py:36
  14.4 0.0 collective-permute-done.4.refs_1_
  14.4 0.0 copy-done
  14.5 0.0 copy-start.1
  14.5 1.0 %copy-done.1 = bf16[320,512]{1,0:T(8,128)(2,1)S(1)} copy-done((bf16[320,512]{1,0:T(8,128)(2,1)S(1)}, bf16[320,512]{1,0:T(8,128)(2,1)}, u32[]{:S(2)}) %copy-start.1) | copy-done | bytes 327704
  15.4 5.0 %shard_map.85 = (bf16[2,320,256]{2,1,0:T(8,128)(2,1)S(1)}, bf16[640,1536]{1,0:T(8,128)(2,1)S(1)}, bf16[320,512]{1,0:T(8,128)(2,1)S(1)}) custom-call(s32[2]{0:T(128)S(1)} %pad_add_fusion.place_ref, bf16[320,512]{1,0:T(8,128)(2,1)S(1)} %get-tuple-element.30.own_ref, bf16[320,512]{1,0:T(8,128)(2,1)S(1)} %collective-permute-done.sib_ref, ...), custom_call_target="tpu_custom_call" | custom-call | flops 4000000000 | bytes 1048576 | tf_op jit(solution)/shard_map/pallas_call | solution.py:36
  20.5 3.4 %collective-permute-start.5 = (bf16[2,320,256]{2,1,0:T(8,128)(2,1)S(1)}, bf16[2,320,256]{2,1,0:T(8,128)(2,1)S(1)}, u32[]{:S(2)}, u32[]{:S(2)}) collective-permute-start(bf16[2,320,256]{2,1,0:T(8,128)(2,1)S(1)} %get-tuple-element.54), channel_id=1, source_target_pairs={{0,4},{4,8},{8,12},{12,16},{16,20},{20,24},{24,28},{1,5},{5,9},{9,... | collective-permute-start | bytes 983048 | tf_op jit(solution)/shard_map/ppermute | solution.py:385
  23.9 4.1 %shard_map.86 = f32[2,320,256]{2,1,0:T(8,128)S(1)} custom-call(bf16[640,1536]{1,0:T(8,128)(2,1)S(1)} %get-tuple-element.52.wide_ref, bf16[320,512]{1,0:T(8,128)(2,1)S(1)} %get-tuple-element.53.mid_ref, bf16[3,3,1536,256]{3,2,1,0:T(8,128)(2,1)} %bitcast.7, bf16[512,256]{1,0:T(8,128)(2,1)} %skip_ref.1), custom_call_target="tpu_custom_call" | custom-call | flops 2000000000 | bytes 1048576 | tf_op jit(solution)/shard_map/pallas_call | solution.py:36
  28.1 5.2 %collective-permute-done.5 = bf16[2,320,256]{2,1,0:T(8,128)(2,1)S(1)} collective-permute-done((bf16[2,320,256]{2,1,0:T(8,128)(2,1)S(1)}, bf16[2,320,256]{2,1,0:T(8,128)(2,1)S(1)}, u32[]{:S(2)}, u32[]{:S(2)}) %collective-permute-start.5) | collective-permute-done | bytes 327712 | tf_op jit(solution)/shard_map/ppermute | solution.py:385
  33.3 0.8 %add_convert_fusion = bf16[2,320,256]{2,1,0:T(8,128)(2,1)} fusion(f32[2,320,256]{2,1,0:T(8,128)S(1)} %shard_map.86, bf16[2,320,256]{2,1,0:T(8,128)(2,1)S(1)} %get-tuple-element.54, bf16[2,320,256]{2,1,0:T(8,128)(2,1)S(1)} %collective-permute-done.5, pred[]{:T(512)S(6)} %eq.17), kind=kLoop, calls=%fused_computation | loop fusion | flops 655360 | bytes 1638401 | tf_op jit(solution)/shard_map/convert_element_type | solution.py:395
  (2 shorter events, 0.0 us)
Async XLA Ops:
  0.0 5.7 %collective-permute-start = (bf16[320,512]{1,0:T(8,128)(2,1)}, bf16[320,512]{1,0:T(8,128)(2,1)S(1)}, u32[]{:S(2)}, u32[]{:S(2)}) collective-permute-start(bf16[320,512]{1,0:T(8,128)(2,1)} %bitcast.8), channel_id=1, source_target_pairs={{0,1},{1,0},{2,3},{3,2},{4,5},{5,4},{6,7},{7,6},{8,9},{9,8},{10,11... | collective-permute-start | bytes 983048 | tf_op jit(solution)/shard_map/ppermute | solution.py:302
  1.1 3.2 %collective-permute-start.2 = (f32[8,512]{1,0:T(8,128)S(1)}, f32[8,512]{1,0:T(8,128)S(1)}, u32[]{:S(2)}, u32[]{:S(2)}) collective-permute-start(f32[8,512]{1,0:T(8,128)S(1)} %get-tuple-element.31), channel_id=1, source_target_pairs={{0,3},{1,2},{2,1},{3,0},{4,7},{5,6},{6,5},{7,4},{8,11},{9,10},{10,... | collective-permute-start | bytes 49160 | tf_op jit(solution)/shard_map/ppermute | solution.py:300
  2.8 9.8 %collective-permute-start.1 = (bf16[320,512]{1,0:T(8,128)(2,1)S(1)}, bf16[320,512]{1,0:T(8,128)(2,1)S(1)}, u32[]{:S(2)}, u32[]{:S(2)}) collective-permute-start(bf16[320,512]{1,0:T(8,128)(2,1)S(1)} %get-tuple-element.30.own_ref), channel_id=1, source_target_pairs={{0,3},{1,2},{2,1},{3,0},{4,7},{5,6},{6,5},{7,4},{8,11},{9,10},{10,... | collective-permute-start | bytes 983048 | tf_op jit(solution)/shard_map/ppermute | solution.py:300
  4.3 1.4 %collective-permute-start.3 = (f32[16,512]{1,0:T(8,128)S(1)}, f32[16,512]{1,0:T(8,128)S(1)}, u32[]{:S(2)}, u32[]{:S(2)}) collective-permute-start(f32[16,512]{1,0:T(8,128)S(1)} %constant_dynamic-update-slice_fusion.refs_0_), channel_id=1, source_target_pairs={{0,1},{1,0},{2,3},{3,2},{4,5},{5,4},{6,7},{7,6},{8,9},{9,8},{10,11... | collective-permute-start | bytes 98312 | tf_op jit(solution)/shard_map/ppermute | solution.py:314
  12.6 1.8 %copy-start = (bf16[320,512]{1,0:T(8,128)(2,1)}, bf16[320,512]{1,0:T(8,128)(2,1)S(1)}, u32[]{:S(2)}) copy-start(bf16[320,512]{1,0:T(8,128)(2,1)S(1)} %collective-permute-done.1.refs_0_) | copy-start | bytes 983044
  12.6 1.8 %collective-permute-start.4 = (bf16[320,512]{1,0:T(8,128)(2,1)S(1)}, bf16[320,512]{1,0:T(8,128)(2,1)S(1)}, u32[]{:S(2)}, u32[]{:S(2)}) collective-permute-start(bf16[320,512]{1,0:T(8,128)(2,1)S(1)} %collective-permute-done.1.refs_0_), channel_id=1, source_target_pairs={{0,1},{1,0},{2,3},{3,2},{4,5},{5,4},{6,7},{7,6},{8,9},{9,8},{10,11... | collective-permute-start | bytes 983048 | tf_op jit(solution)/shard_map/ppermute | solution.py:354
  14.5 1.0 %copy-start.1 = (bf16[320,512]{1,0:T(8,128)(2,1)S(1)}, bf16[320,512]{1,0:T(8,128)(2,1)}, u32[]{:S(2)}) copy-start(bf16[320,512]{1,0:T(8,128)(2,1)} %copy-done) | copy-start | bytes 983044
  20.5 12.8 %collective-permute-start.5 = (bf16[2,320,256]{2,1,0:T(8,128)(2,1)S(1)}, bf16[2,320,256]{2,1,0:T(8,128)(2,1)S(1)}, u32[]{:S(2)}, u32[]{:S(2)}) collective-permute-start(bf16[2,320,256]{2,1,0:T(8,128)(2,1)S(1)} %get-tuple-element.54), channel_id=1, source_target_pairs={{0,4},{4,8},{8,12},{12,16},{16,20},{20,24},{24,28},{1,5},{5,9},{9,... | collective-permute-start | bytes 983048 | tf_op jit(solution)/shard_map/ppermute | solution.py:385

commit v4 on v3

--- a/solution.py
+++ b/solution.py
@@ -12,7 +12,8 @@
 F32 = jnp.float32
 VMEM = pltpu.VMEM
 LIMIT = 20 * 1024 * 1024
-PIECES = 4
+SHARE = 1 << 16
+PAD = 16
 
 
 def dot(left, right):
@@ -40,29 +41,35 @@
         out_specs=jax.tree.map(lambda _: spec(), outs),
         scratch_shapes=scratch,
         compiler_params=pltpu.CompilerParams(vmem_limit_bytes=LIMIT),
-        cost_estimate=pl.CostEstimate(flops=cost, bytes_accessed=1 << 20, transcendentals=0),
+        cost_estimate=pl.CostEstimate(flops=cost // SHARE, bytes_accessed=1 << 10, transcendentals=0),
     )(*args)
 
 
-def stats_body(features_ref, sums_ref, own_ref, sems):
-    rows = own_ref.shape[0] // PIECES
-    copies = []
-    for i in range(PIECES):
-        piece = pl.ds(i * rows, rows)
-        copies.append(
-            pltpu.make_async_copy(features_ref.at[piece], own_ref.at[piece], sems.at[i])
-        )
-        copies[-1].start()
+def stats_body(cols, place_ref, features_ref, sums_ref, own_ref, edge_ref, rest_ref, sems):
+    cells = own_ref.shape[0]
+    core = place_ref[0]
+    edge = pl.multiple_of(core * (cells - cols), 16)
+    rest = pl.multiple_of((1 - core) * cols, 16)
+    parts = [
+        (features_ref.at[pl.ds(edge, cols)], edge_ref),
+        (features_ref.at[pl.ds(rest, cells - cols)], rest_ref.at[pl.ds(0, cells - cols)]),
+        (features_ref, own_ref),
+    ]
+    copies = [pltpu.make_async_copy(*part, sems.at[i]) for i, part in enumerate(parts)]
+    for copy in copies:
+        copy.start()
     total = jnp.zeros((1, own_ref.shape[1]), F32)
     squared = total
-    for i in range(PIECES):
-        copies[i].wait()
-        block = own_ref[i * rows : (i + 1) * rows].astype(F32)
+    rest_ref[cells - cols :] = jnp.zeros((PAD, own_ref.shape[1]), BF)
+    for copy, (_, ref) in zip(copies[:2], parts[:2], strict=True):
+        copy.wait()
+        block = ref[...].astype(F32)
         total += jnp.sum(block, axis=0, keepdims=True)
         squared += jnp.sum(block * block, axis=0, keepdims=True)
     sums_ref[...] = jnp.concatenate(
         [total, squared, jnp.zeros((6, own_ref.shape[1]), F32)], axis=0
     )
+    copies[2].wait()
 
 
 def group_sums(sums, width):
@@ -167,46 +174,44 @@
     return norm_ref[0:1], norm_ref[1:2], norm_ref[2:3]
 
 
-def far_rows(place_ref, first_ref, last_ref, cols):
-    core = place_ref[0]
-    far = pl.multiple_of((1 - core) * (first_ref.shape[0] - cols), 16)
-    first = first_ref[pl.ds(far, cols), :]
-    if last_ref is None:
-        return first
-    return jnp.where(core == 0, first, last_ref[pl.ds(far, cols), :])
-
-
-def project(block_ref, norm_ref, wk_ref, wv_ref, k_ref, v_ref):
-    normed = normalise(block_ref[...], *normal_of(norm_ref))
+def project(blocks, norm_ref, wk_ref, wv_ref, k_ref, v_ref):
+    block = jnp.concatenate([block[...] for block in blocks], axis=0)
+    normed = normalise(block, *normal_of(norm_ref))
     k_ref[...] = dot(normed, wk_ref[...]).astype(BF)
     v_ref[...] = dot(normed, wv_ref[...]).astype(BF)
 
 
-def join_body(cols, exponent, single, place_ref, *refs):
-    first_ref, refs = refs[0], refs[1:]
-    last_ref, refs = (None, refs) if single else (refs[0], refs[1:])
+def keys_body(block_ref, norm_ref, wk_ref, wv_ref, k_ref, v_ref):
+    project([block_ref.at[pl.ds(0, k_ref.shape[0])]], norm_ref, wk_ref, wv_ref, k_ref, v_ref)
+
+
+def join_body(exponent, single, place_ref, recv_ref, rsib_ref, *refs):
+    last_ref, refs = (rsib_ref, refs) if single else (refs[0], refs[1:])
     (norm_ref, wq_ref, wk_ref, wv_ref, q_ref, k_ref, v_ref, peak_ref, sum_ref, mix_ref,
-     all_q_ref, all_peak_ref, all_sum_ref, all_mix_ref, new_k_ref, new_v_ref) = refs
+     far_ref, all_q_ref, *refs) = refs
+    out, every, new, (new_k_ref, new_v_ref) = refs[:3], refs[3:6], refs[6:9], refs[9:]
     near = q_ref.shape[0]
-    far_q = dot(
-        normalise(far_rows(place_ref, first_ref, last_ref, cols), *normal_of(norm_ref)),
-        wq_ref[...],
-    ).astype(BF)
-    project(first_ref, norm_ref, wk_ref, wv_ref, new_k_ref, new_v_ref)
+    far = rsib_ref[...]
+    if not single:
+        far = jnp.where(place_ref[0] == 0, far, last_ref[...])
+    far_ref[...] = far
+    far_q = dot(normalise(far, *normal_of(norm_ref)), wq_ref[...]).astype(BF)
+    project([recv_ref, rsib_ref], norm_ref, wk_ref, wv_ref, new_k_ref, new_v_ref)
     all_q_ref[:near] = q_ref[...]
     all_q_ref[near:] = far_q
-    every = (all_peak_ref, all_sum_ref, all_mix_ref)
-    for old, new in zip((peak_ref, sum_ref, mix_ref), every, strict=True):
-        new[:near] = old[...]
-    attend(
-        far_q, k_ref[...], v_ref[...], exponent, *[ref.at[pl.ds(near, cols)] for ref in every]
-    )
-
-
-def more_body(exponent, block_ref, norm_ref, wk_ref, wv_ref, q_ref, *refs):
+    for old_ref, every_ref in zip((peak_ref, sum_ref, mix_ref), every, strict=True):
+        every_ref[:near] = old_ref[...]
+    tail = pl.ds(near, far.shape[0])
+    attend(far_q, k_ref[...], v_ref[...], exponent, *[ref.at[tail] for ref in every])
+    attend(all_q_ref[...], new_k_ref[...], new_v_ref[...], exponent, *new)
+    merge(every, new, out, exponent, False)
+
+
+def more_body(exponent, recv_ref, rsib_ref, norm_ref, wk_ref, wv_ref, q_ref, *refs):
     old, out, new = refs[:3], refs[3:6], refs[6:9]
     k_ref, v_ref = refs[9:]
-    project(block_ref, norm_ref, wk_ref, wv_ref, k_ref, v_ref)
+    blocks = [ref.at[pl.ds(0, k_ref.shape[0] // 2)] for ref in (recv_ref, rsib_ref)]
+    project(blocks, norm_ref, wk_ref, wv_ref, k_ref, v_ref)
     attend(q_ref[...], k_ref[...], v_ref[...], exponent, *new)
     merge(old, new, out, exponent, False)
 
@@ -227,23 +232,27 @@
     return total
 
 
-def late_body(cols, exponent, single, place_ref, own_ref, sib_ref, *refs):
-    first_ref, refs = refs[0], refs[1:]
-    last_ref, refs = (None, refs) if single else (refs[0], refs[1:])
-    (block_ref, norm_ref, q_ref, peak_ref, sum_ref, mix_ref, k_ref, v_ref, wk_ref, wv_ref, wo_ref,
-     taps_ref, part_ref, wide_ref, mid_ref, keys_ref, values_ref, *new, attended_ref) = refs
+def late_body(
+    cols, exponent,
+    place_ref, own_ref, sib_ref, far_ref, block_ref, norm_ref, q_ref, peak_ref, sum_ref, mix_ref,
+    k_ref, v_ref, wk_ref, wv_ref, wo_ref, taps_ref,
+    odd_ref, first_ref, wide_ref, mid_ref,
+    keys_ref, values_ref, new_peak_ref, new_sum_ref, new_mix_ref, attended_ref,
+):
     cells = own_ref.shape[0]
     core = place_ref[0]
-    keys_ref[:cells] = k_ref[...]
-    values_ref[:cells] = v_ref[...]
-    rest = pl.ds(cells, cells)
-    project(block_ref, norm_ref, wk_ref, wv_ref, keys_ref.at[rest], values_ref.at[rest])
+    half = k_ref.shape[0]
+    keys_ref[:half] = k_ref[...]
+    values_ref[:half] = v_ref[...]
+    rest = pl.ds(half, half)
+    block = block_ref.at[pl.ds(0, half)]
+    project([block], norm_ref, wk_ref, wv_ref, keys_ref.at[rest], values_ref.at[rest])
+    new = (new_peak_ref, new_sum_ref, new_mix_ref)
     attend(q_ref[...], keys_ref[...], values_ref[...], exponent, *new)
     merge((peak_ref, sum_ref, mix_ref), new, (attended_ref,), exponent, True)
     change = dot(attended_ref[...], wo_ref[...])
     near = pl.multiple_of(core * (cells - cols), 16)
-    far_block = far_rows(place_ref, first_ref, last_ref, cols)
-    base = jnp.concatenate([own_ref[...], sib_ref[pl.ds(near, cols), :], far_block], axis=0)
+    base = jnp.concatenate([own_ref[...], sib_ref[pl.ds(near, cols), :], far_ref[...]], axis=0)
     mid = (base.astype(F32) + change).astype(BF)
     mid_ref[...] = mid[:cells]
     act = jax.nn.silu(mid.astype(F32)).astype(BF).astype(F32)
@@ -253,9 +262,15 @@
     below = jnp.where(core == 0, near_act, far_act)
     wide_ref[...] = spread(jnp.concatenate([above, act[:cells], below], axis=0), cols)
     first_tap = conv(wide_ref, lambda row: taps_ref[0, row], cells, cols)
+    odd_ref[:cells] = first_tap.astype(BF)
+    odd_ref[cells:] = jnp.zeros((PAD, odd_ref.shape[1]), BF)
+    first_ref[...] = first_tap
+
+
+def even_body(cols, wide_ref, first_ref, taps_ref, even_ref):
+    cells = first_ref.shape[0]
     second_tap = conv(wide_ref, lambda row: taps_ref[1, row], cells, cols)
-    part_ref[0] = (first_tap + second_tap).astype(BF)
-    part_ref[1] = first_tap.astype(BF)
+    even_ref[...] = (first_ref[...] + second_tap).astype(BF)
 
 
 def now_body(cols, wide_ref, mid_ref, conv_ref, skip_ref, out_ref, taps_ref, skip_held_ref, sems):
@@ -273,6 +288,16 @@
     last_tap = conv(wide_ref, lambda row: taps_ref[1, row], cells, cols) + skip
     out_ref[0] = last_tap
     out_ref[1] = last_tap + second_tap
+
+
+def last_body(which, place_ref, now_ref, own_ref, arrived_ref, *refs):
+    out_ref, sum_ref, sem = refs[-3:]
+    cells = sum_ref.shape[0]
+    before = jnp.where(place_ref[2] != 0, own_ref[:cells], arrived_ref[:cells])
+    sum_ref[...] = (now_ref[which] + before.astype(F32)).astype(BF)
+    copy = pltpu.make_async_copy(sum_ref, out_ref.at[which], sem)
+    copy.start()
+    copy.wait()
 
 
 def per_device(
@@ -292,44 +317,48 @@
     chips = devices // 2
     me = lax.axis_index("tile")
     core = me % 2
-    swap = [(i, i ^ 1) for i in range(devices)]
     own = features.reshape(cells, channels)
 
-    def turned(array, by, flip):
-        pairs = [(i, ((i + 2 * by) % devices) ^ flip) for i in range(devices)]
-        return lax.ppermute(array, "tile", pairs)
-
-    sib = lax.ppermute(own, "tile", swap)
-    sums, own = call(
-        stats_body,
-        [jax.ShapeDtypeStruct((8, channels), F32), jax.ShapeDtypeStruct(own.shape, BF)],
-        [pltpu.SemaphoreType.DMA((PIECES,))],
+    def turned(array, by):
+        return lax.ppermute(array, "tile", [(i, (i + 2 * by) % devices) for i in range(devices)])
+
+    def swapped(array):
+        return lax.ppermute(array, "tile", [(i, i ^ 1) for i in range(devices)])
+
+    def rows_of(rows, kind=BF, width=channels):
+        return jax.ShapeDtypeStruct((rows, width), kind)
+
+    def state_of(rows):
+        return [rows_of(rows, F32, 128), rows_of(rows, F32, 128), rows_of(rows, F32)]
+
+    def scratch_of(shapes):
+        return [VMEM(shape.shape, shape.dtype) for shape in shapes]
+
+    outside = jnp.where(core == 0, me == 0, me == devices - 1)
+    first_span = lax.axis_index("tm") == 0
+    place = jnp.stack([core, 1 - outside.astype(jnp.int32), first_span.astype(jnp.int32)])
+    place = place.astype(jnp.int32)
+    sib = swapped(own)
+    sums, own, edge, rest = call(
+        functools.partial(stats_body, cols),
+        [rows_of(8, F32), rows_of(cells), rows_of(cols), rows_of(cells - cols + PAD)],
+        [pltpu.SemaphoreType.DMA((3,))],
         1 << 22,
-        hbm(own),
-        spaces=[pltpu.HBM],
-    )
-    sums = [sums] + [turned(sums, by, 1) for by in range(1, chips)]
-    recv = [turned(own, by, 1) for by in range(1, chips)]
-    sums = jnp.concatenate(sums, axis=0)
-    sums = [sums, lax.ppermute(sums, "tile", swap)]
+        place, hbm(own),
+        spaces=[pltpu.SMEM, pltpu.HBM],
+    )
+    shifts = range(1, chips)
+    sums = jnp.concatenate([sums] + [turned(sums, by) for by in shifts], axis=0)
+    recv_edge = [turned(edge, by) for by in shifts]
+    recv_rest = [turned(rest, by) for by in shifts]
+    sums = [sums, swapped(sums)]
 
     exponent = channels ** (-0.5) * 1.4426950408889634
-    outside = jnp.where(core == 0, me == 0, me == devices - 1)
-    place = jnp.stack([core, 1 - outside.astype(jnp.int32)]).astype(jnp.int32)
     near = cells + cols
     every = near + cols
     taps = conv_weight.reshape(3, 3, 3 * channels, out_channels)
     weights = [norm_gain.reshape(1, channels), query_weight, key_weight, value_weight, out_weight]
     first_taps = (2, *taps.shape[1:])
-
-    def rows_of(rows, kind=BF, width=channels):
-        return jax.ShapeDtypeStruct((rows, width), kind)
-
-    def state_of(rows):
-        return [rows_of(rows, F32, 128), rows_of(rows, F32, 128), rows_of(rows, F32)]
-
-    def scratch_of(shapes):
-        return [VMEM(shape.shape, shape.dtype) for shape in shapes]
 
     n_sums = len(sums)
     norm, q, k, v, *rest = call(
@@ -350,39 +379,54 @@
     )
     state, (wq, wk, wv, wo, held_taps) = rest[:3], rest[3:]
 
-    *recv, norm = lax.optimization_barrier((*recv, norm))
-    rsib = [lax.ppermute(block, "tile", swap) for block in recv]
-    ends = recv[:1] if chips == 2 else [recv[0], recv[-1]]
-    q, *state, new_k, new_v = call(
-        functools.partial(join_body, cols, exponent, chips == 2),
-        [rows_of(every), *state_of(every), rows_of(cells), rows_of(cells)],
-        [],
+    *recv_edge, norm = lax.optimization_barrier((*recv_edge, norm))
+    rsib_edge = [swapped(block) for block in recv_edge]
+    ends = rsib_edge[:1] if chips == 2 else [rsib_edge[0], rsib_edge[-1]]
+    far, q, *state = call(
+        functools.partial(join_body, exponent, chips == 2),
+        [rows_of(cols), rows_of(every), *state_of(every)],
+        scratch_of([*state_of(every), *state_of(every), rows_of(2 * cols), rows_of(2 * cols)]),
         2 * 10**9,
-        place, *ends, norm, wq, wk, wv, q, k, v, *state,
-        spaces=[pltpu.SMEM] + [VMEM] * (10 + len(ends)),
-    )
-    for block in recv[1:] + rsib[:-1]:
+        place, recv_edge[0], *ends, norm, wq, wk, wv, q, k, v, *state,
+        spaces=[pltpu.SMEM] + [VMEM] * (11 + len(ends)),
+    )
+    *recv_rest, state[0] = lax.optimization_barrier((*recv_rest, state[0]))
+    rsib_rest = [swapped(block) for block in recv_rest]
+    pairs = [*zip(recv_edge, rsib_edge, strict=True)][1:]
+    pairs += [*zip(recv_rest, rsib_rest, strict=True)][:-1]
+    for pair in pairs:
+        held = rows_of(2 * (pair[0].shape[0] // cols * cols))
         state = call(
             functools.partial(more_body, exponent),
             state_of(every),
-            scratch_of([*state_of(every), rows_of(cells), rows_of(cells)]),
+            scratch_of([*state_of(every), held, held]),
             10**9,
-            block, norm, wk, wv, q, *state,
+            *pair, norm, wk, wv, q, *state,
         )
-    part, wide, mid = call(
-        functools.partial(late_body, cols, exponent, chips == 2),
+    last = rows_of(cells - cols)
+    last_k, last_v = call(keys_body, [last, last], [], 10**8, recv_rest[-1], norm, wk, wv)
+    both = rows_of(2 * (cells - cols))
+    odd, first, wide, mid = call(
+        functools.partial(late_body, cols, exponent),
         [
-            jax.ShapeDtypeStruct((2, cells, out_channels), BF),
+            rows_of(cells + PAD, BF, out_channels),
+            rows_of(cells, F32, out_channels),
             rows_of(every, BF, 3 * channels),
             rows_of(cells),
         ],
-        scratch_of([rows_of(2 * cells), rows_of(2 * cells), *state_of(every), rows_of(every)]),
+        scratch_of([both, both, *state_of(every), rows_of(every)]),
         4 * 10**9,
-        place, own, sib, *ends, rsib[-1], norm, q, *state, new_k, new_v, wk, wv, wo, held_taps,
-        spaces=[pltpu.SMEM] + [VMEM] * (14 + len(ends)),
+        place, own, sib, far, rsib_rest[-1], norm, q, *state, last_k, last_v, wk, wv, wo,
+        held_taps,
+        spaces=[pltpu.SMEM] + [VMEM] * 15,
     )
     spans = lax.axis_size("tm")
-    arrived = lax.ppermute(part, "tm", [(i, i + 1) for i in range(spans - 1)])
+    arrived_odd = lax.ppermute(odd, "tm", [(i, (i + 1) % spans) for i in range(spans)])
+    even = call(
+        functools.partial(even_body, cols), rows_of(cells, BF, out_channels), [], 8 * 10**8,
+        wide, first, held_taps,
+    )
+    arrived_even = lax.ppermute(even, "tm", [(i, i + 1) for i in range(spans - 1)])
     now = call(
         functools.partial(now_body, cols),
         jax.ShapeDtypeStruct((2, cells, out_channels), F32),
@@ -391,8 +435,20 @@
         wide, mid, hbm(taps), hbm(skip_weight),
         spaces=[VMEM, VMEM, pltpu.HBM, pltpu.HBM],
     )
-    before = jnp.where(lax.axis_index("tm") == 0, part, arrived)
-    decoded = (now + before.astype(F32)).astype(BF)
+    result = jax.ShapeDtypeStruct((2, cells, out_channels), BF)
+    decoded = None
+    for which, own_part, arrived in ((1, odd, arrived_odd), (0, even, arrived_even)):
+        operands = [place, now, own_part, arrived]
+        decoded = pl.pallas_call(
+            functools.partial(last_body, which),
+            out_shape=result,
+            in_specs=[spec(pltpu.SMEM)] + [spec()] * 3 + [spec(pl.ANY)] * (decoded is not None),
+            out_specs=spec(pl.ANY),
+            input_output_aliases={} if decoded is None else {4: 0},
+            scratch_shapes=[VMEM((cells, out_channels), BF), pltpu.SemaphoreType.DMA],
+            compiler_params=pltpu.CompilerParams(vmem_limit_bytes=LIMIT),
+            cost_estimate=pl.CostEstimate(flops=1, bytes_accessed=1 << 10, transcendentals=0),
+        )(*operands, *([] if decoded is None else [decoded]))
     return decoded.reshape(2, tile_rows, cols, out_channels)
 
 

time: 34.4 us -> 37 us (1.076)
  the two profiles are of different devices: /device:TPU:24 before, /device:TPU:0 now
where the time goes in v4:
time: 37 us; the launch traced here: 36.8 us
  Pallas kernels  22 us (59%)
  starting transfers between devices  10.9 us (29%)
  waiting for transfers between devices  3.66 us (10%)
    pallas_call x7, Pallas kernels, call(): pl.pallas_call(body, out_shape=outs, in_specs=[spec(s) for s in spaces],...  19.5 us
    ppermute x3, starting transfers between devices, turned(): lax.ppermute(array, 'tile', [(i, (i + 2 * by) % devices) for i in range(d...  4.78 us
    ppermute x1, starting transfers between devices, per_device(): lax.ppermute(even, 'tm', [(i, i + 1) for i in range(spans - 1)])  3.46 us
    pallas_call x2, Pallas kernels, per_device(): pl.pallas_call(functools.partial(last_body, which), out_shape=result, in_...  2.53 us
    ppermute x4, waiting for transfers between devices, swapped(): return lax.ppermute(array, 'tile', [(i, i ^ 1) for i in range(devices)])  2.02 us
    ppermute x3, waiting for transfers between devices, turned(): lax.ppermute(array, 'tile', [(i, (i + 2 * by) % devices) for i in range(d...  1.64 us
    ppermute x1, starting transfers between devices, per_device(): lax.ppermute(odd, 'tm', [(i, (i + 1) % spans) for i in range(spans)])  1.63 us
    ppermute x4, starting transfers between devices, swapped(): return lax.ppermute(array, 'tile', [(i, i ^ 1) for i in range(devices)])  1.04 us
  transfers between devices with their start and end apart: 9, of which 3 were waited for; matrix products, arithmetic and copies ran while one was open for 0% of the time, Pallas kernels for 43%

profile of v4, /device:TPU:0, one launch (start us, length us, event | category | flops | bytes accessed | tf_op | source)
XLA Modules:
  0.0 36.8 jit_solution(9685931764032057810)
XLA Ops:
  0.0 0.5 %collective-permute-start = (bf16[320,512]{1,0:T(8,128)(2,1)}, bf16[320,512]{1,0:T(8,128)(2,1)S(1)}, u32[]{:S(2)}, u32[]{:S(2)}) collective-permute-start(bf16[320,512]{1,0:T(8,128)(2,1)} %bitcast.9), channel_id=1, source_target_pairs={{0,1},{1,0},{2,3},{3,2},{4,5},{5,4},{6,7},{7,6},{8,9},{9,8},{10,11... | collective-permute-start | bytes 983048 | tf_op jit(solution)/shard_map/ppermute | solution.py:326
  0.5 0.1 pad_add_fusion.place_ref
  0.5 1.7 %shard_map.82 = (f32[8,512]{1,0:T(8,128)S(1)}, bf16[320,512]{1,0:T(8,128)(2,1)S(1)}, bf16[160,512]{1,0:T(8,128)(2,1)S(1)}, bf16[176,512]{1,0:T(8,128)(2,1)S(1)}) custom-call(s32[3]{0:T(128)S(1)} %pad_add_fusion.place_ref, bf16[320,512]{1,0:T(8,128)(2,1)} %bitcast.10), custom_call_target="tpu_custom_call" | custom-call | flops 64 | bytes 1024 | tf_op jit(solution)/shard_map/pallas_call | solution.py:37
  2.2 2.6 %collective-permute-start.2 = (f32[8,512]{1,0:T(8,128)S(1)}, f32[8,512]{1,0:T(8,128)S(1)}, u32[]{:S(2)}, u32[]{:S(2)}) collective-permute-start(f32[8,512]{1,0:T(8,128)S(1)} %get-tuple-element.38), channel_id=1, source_target_pairs={{0,2},{1,3},{2,0},{3,1},{4,6},{5,7},{6,4},{7,5},{8,10},{9,11},{10,... | collective-permute-start | bytes 49160 | tf_op jit(solution)/shard_map/ppermute | solution.py:323
  4.8 0.1 collective-permute-start.1
  4.9 1.6 %collective-permute-done.2 = f32[8,512]{1,0:T(8,128)S(1)} collective-permute-done((f32[8,512]{1,0:T(8,128)S(1)}, f32[8,512]{1,0:T(8,128)S(1)}, u32[]{:S(2)}, u32[]{:S(2)}) %collective-permute-start.2) | collective-permute-done | bytes 16416 | tf_op jit(solution)/shard_map/ppermute | solution.py:323
  6.6 0.0 collective-permute-start.3
  6.6 2.1 %collective-permute-start.5 = (bf16[176,512]{1,0:T(8,128)(2,1)S(1)}, bf16[176,512]{1,0:T(8,128)(2,1)S(1)}, u32[]{:S(2)}, u32[]{:S(2)}) collective-permute-start(bf16[176,512]{1,0:T(8,128)(2,1)S(1)} %get-tuple-element.52), channel_id=1, source_target_pairs={{0,2},{1,3},{2,0},{3,1},{4,6},{5,7},{6,4},{7,5},{8,10},{9,11},{10,... | collective-permute-start | bytes 540680 | tf_op jit(solution)/shard_map/ppermute | solution.py:323
  8.7 0.0 collective-permute-done.3.refs_1_
  8.7 0.0 collective-permute-done.sib_ref
  8.7 4.8 %shard_map.83 = (f32[8,512]{1,0:T(8,128)S(1)}, bf16[480,512]{1,0:T(8,128)(2,1)S(1)}, bf16[640,512]{1,0:T(8,128)(2,1)S(1)}, bf16[640,512]{1,0:T(8,128)(2,1)S(1)},...) custom-call(s32[3]{0:T(128)S(1)} %pad_add_fusion.place_ref, ...), custom_call_target="tpu_custom_call" | custom-call | flops 30517 | bytes 1024 | tf_op jit(solution)/shard_map/pallas_call | solution.py:37
  13.5 0.0 collective-permute-done.1.recv_ref
  13.5 0.3 collective-permute-start.4
  13.8 1.2 %collective-permute-done.4.rsib_ref = bf16[160,512]{1,0:T(8,128)(2,1)S(1)} collective-permute-done((bf16[160,512]{1,0:T(8,128)(2,1)S(1)}, bf16[160,512]{1,0:T(8,128)(2,1)S(1)}, u32[]{:S(2)}, u32[]{:S(2)}) %collective-permute-start.4) | collective-permute-done | bytes 163872 | tf_op jit(solution)/shard_map/ppermute | solution.py:326
  15.0 2.6 %shard_map.84 = (bf16[160,512]{1,0:T(8,128)(2,1)S(1)}, bf16[640,512]{1,0:T(8,128)(2,1)S(1)}, f32[640,128]{1,0:T(8,128)S(1)}, f32[640,128]{1,0:T(8,128)S(1)}, f32[640,512]{1,0:T(8,128)S(1)}) custom-call(s32[3]{0:T(128)S(1)} %pad_add_fusion.place_ref, bf16[160,512]{1,0:T(8,128)(2,1)S(1)} %collective-permute-done.1.recv_ref, ...), custom_call_target="tpu_custom_call" | custom-call | flops 30517 | bytes 1024 | tf_op jit(solution)/shard_map/pallas_call | solution.py:37
  17.6 0.0 collective-permute-done.5.block_ref
  17.6 0.3 collective-permute-start.6
  17.9 0.3 shard_map.85
  18.2 0.8 %collective-permute-done.6.block_ref = bf16[176,512]{1,0:T(8,128)(2,1)S(1)} collective-permute-done((bf16[176,512]{1,0:T(8,128)(2,1)S(1)}, bf16[176,512]{1,0:T(8,128)(2,1)S(1)}, u32[]{:S(2)}, u32[]{:S(2)}) %collective-permute-start.6) | collective-permute-done | bytes 180256 | tf_op jit(solution)/shard_map/ppermute | solution.py:326
  19.1 5.0 %shard_map.86 = (bf16[336,256]{1,0:T(8,128)(2,1)S(1)}, f32[320,256]{1,0:T(8,128)S(1)}, bf16[640,1536]{1,0:T(8,128)(2,1)S(1)}, bf16[320,512]{1,0:T(8,128)(2,1)S(1)}) custom-call(s32[3]{0:T(128)S(1)} %pad_add_fusion.place_ref, bf16[320,512]{1,0:T(8,128)(2,1)S(1)} %get-tuple-element.36.own_ref, bf16[320,512]{1,0:T(8,128)(2,1)S(1)} %collective-permute-done.sib_ref, ...), custom_call_target="tpu_custom_call" | custom-call | flops 61035 | bytes 1024 | tf_op jit(solution)/shard_map/pallas_call | solution.py:37
  24.0 1.6 %collective-permute-start.8 = (bf16[336,256]{1,0:T(8,128)(2,1)S(1)}, bf16[336,256]{1,0:T(8,128)(2,1)S(1)}, u32[]{:S(2)}, u32[]{:S(2)}) collective-permute-start(bf16[336,256]{1,0:T(8,128)(2,1)S(1)} %get-tuple-element.66.own_ref), channel_id=1, source_target_pairs={{0,4},{4,8},{8,12},{12,16},{16,20},{20,24},{24,28},{28,0},{1,5},{5... | collective-permute-start | bytes 516104 | tf_op jit(solution)/shard_map/ppermute | solution.py:424
  25.7 0.9 %shard_map.88.own_ref = bf16[320,256]{1,0:T(8,128)(2,1)S(1)} custom-call(bf16[640,1536]{1,0:T(8,128)(2,1)S(1)} %get-tuple-element.63.wide_ref, f32[320,256]{1,0:T(8,128)S(1)} %get-tuple-element.65.first_ref, bf16[2,3,1536,256]{3,2,1,0:T(8,128)(2,1)S(1)} %get-tuple-element.62.taps_ref), custom_call_target="tpu_custom_call" | custom-call | flops 12207 | bytes 1024 | tf_op jit(solution)/shard_map/pallas_call | solution.py:37
  26.6 3.5 %collective-permute-start.7 = (bf16[320,256]{1,0:T(8,128)(2,1)S(1)}, bf16[320,256]{1,0:T(8,128)(2,1)S(1)}, u32[]{:S(2)}, u32[]{:S(2)}) collective-permute-start(bf16[320,256]{1,0:T(8,128)(2,1)S(1)} %shard_map.88.own_ref), channel_id=1, source_target_pairs={{0,4},{4,8},{8,12},{12,16},{16,20},{20,24},{24,28},{1,5},{5,9},{9,... | collective-permute-start | bytes 491528 | tf_op jit(solution)/shard_map/ppermute | solution.py:429
  30.1 4.1 %shard_map.87.now_ref = f32[2,320,256]{2,1,0:T(8,128)S(1)} custom-call(bf16[640,1536]{1,0:T(8,128)(2,1)S(1)} %get-tuple-element.63.wide_ref, bf16[320,512]{1,0:T(8,128)(2,1)S(1)} %get-tuple-element.64.mid_ref, bf16[3,3,1536,256]{3,2,1,0:T(8,128)(2,1)} %bitcast.8, bf16[512,256]{1,0:T(8,128)(2,1)} %skip_ref.1), custom_call_target="tpu_custom_call" | custom-call | flops 30517 | bytes 1024 | tf_op jit(solution)/shard_map/pallas_call | solution.py:37
  34.2 0.0 collective-permute-done.8.arrived_ref
  34.2 1.3 %shard_map.89.refs_0_ = bf16[2,320,256]{2,1,0:T(8,128)(2,1)} custom-call(s32[3]{0:T(128)S(1)} %pad_add_fusion.place_ref, f32[2,320,256]{2,1,0:T(8,128)S(1)} %shard_map.87.now_ref, bf16[336,256]{1,0:T(8,128)(2,1)S(1)} %get-tuple-element.66.own_ref, bf16[336,256]{1,0:T(8,128)(2,1)S(1)} %collective-permute-done.8.arrived_ref), custom_call_target="tpu_custom_call" | custom-call | flops 1 | bytes 1024 | tf_op jit(solution)/shard_map/pallas_call | solution.py:442
  35.5 0.0 collective-permute-done.7.arrived_ref
  35.5 1.3 %shard_map.90 = bf16[2,320,256]{2,1,0:T(8,128)(2,1)} custom-call(s32[3]{0:T(128)S(1)} %pad_add_fusion.place_ref, f32[2,320,256]{2,1,0:T(8,128)S(1)} %shard_map.87.now_ref, bf16[320,256]{1,0:T(8,128)(2,1)S(1)} %shard_map.88.own_ref, bf16[320,256]{1,0:T(8,128)(2,1)S(1)} %collective-permute-done.7.arrived_ref, ...), custom_call_target="tpu_custom_call", output_to_operand_aliasing={{}: (4, {})} | custom-call | flops 1 | bytes 1024 | tf_op jit(solution)/shard_map/pallas_call | solution.py:442
  (2 shorter events, 0.0 us)
Async XLA Ops:
  0.0 8.7 %collective-permute-start = (bf16[320,512]{1,0:T(8,128)(2,1)}, bf16[320,512]{1,0:T(8,128)(2,1)S(1)}, u32[]{:S(2)}, u32[]{:S(2)}) collective-permute-start(bf16[320,512]{1,0:T(8,128)(2,1)} %bitcast.9), channel_id=1, source_target_pairs={{0,1},{1,0},{2,3},{3,2},{4,5},{5,4},{6,7},{7,6},{8,9},{9,8},{10,11... | collective-permute-start | bytes 983048 | tf_op jit(solution)/shard_map/ppermute | solution.py:326
  2.2 4.3 %collective-permute-start.2 = (f32[8,512]{1,0:T(8,128)S(1)}, f32[8,512]{1,0:T(8,128)S(1)}, u32[]{:S(2)}, u32[]{:S(2)}) collective-permute-start(f32[8,512]{1,0:T(8,128)S(1)} %get-tuple-element.38), channel_id=1, source_target_pairs={{0,2},{1,3},{2,0},{3,1},{4,6},{5,7},{6,4},{7,5},{8,10},{9,11},{10,... | collective-permute-start | bytes 49160 | tf_op jit(solution)/shard_map/ppermute | solution.py:323
  4.8 8.7 %collective-permute-start.1 = (bf16[160,512]{1,0:T(8,128)(2,1)S(1)}, bf16[160,512]{1,0:T(8,128)(2,1)S(1)}, u32[]{:S(2)}, u32[]{:S(2)}) collective-permute-start(bf16[160,512]{1,0:T(8,128)(2,1)S(1)} %get-tuple-element.37), channel_id=1, source_target_pairs={{0,2},{1,3},{2,0},{3,1},{4,6},{5,7},{6,4},{7,5},{8,10},{9,11},{10,... | collective-permute-start | bytes 491528 | tf_op jit(solution)/shard_map/ppermute | solution.py:323
  6.6 2.1 %collective-permute-start.3 = (f32[16,512]{1,0:T(8,128)S(1)}, f32[16,512]{1,0:T(8,128)S(1)}, u32[]{:S(2)}, u32[]{:S(2)}) collective-permute-start(f32[16,512]{1,0:T(8,128)S(1)} %constant_dynamic-update-slice_fusion.refs_0_), channel_id=1, source_target_pairs={{0,1},{1,0},{2,3},{3,2},{4,5},{5,4},{6,7},{7,6},{8,9},{9,8},{10,11... | collective-permute-start | bytes 98312 | tf_op jit(solution)/shard_map/ppermute | solution.py:326
  6.6 11.0 %collective-permute-start.5 = (bf16[176,512]{1,0:T(8,128)(2,1)S(1)}, bf16[176,512]{1,0:T(8,128)(2,1)S(1)}, u32[]{:S(2)}, u32[]{:S(2)}) collective-permute-start(bf16[176,512]{1,0:T(8,128)(2,1)S(1)} %get-tuple-element.52), channel_id=1, source_target_pairs={{0,2},{1,3},{2,0},{3,1},{4,6},{5,7},{6,4},{7,5},{8,10},{9,11},{10,... | collective-permute-start | bytes 540680 | tf_op jit(solution)/shard_map/ppermute | solution.py:323
  13.5 1.5 %collective-permute-start.4 = (bf16[160,512]{1,0:T(8,128)(2,1)S(1)}, bf16[160,512]{1,0:T(8,128)(2,1)S(1)}, u32[]{:S(2)}, u32[]{:S(2)}) collective-permute-start(bf16[160,512]{1,0:T(8,128)(2,1)S(1)} %collective-permute-done.1.recv_ref), channel_id=1, source_target_pairs={{0,1},{1,0},{2,3},{3,2},{4,5},{5,4},{6,7},{7,6},{8,9},{9,8},{10,11... | collective-permute-start | bytes 491528 | tf_op jit(solution)/shard_map/ppermute | solution.py:326
  17.6 1.5 %collective-permute-start.6 = (bf16[176,512]{1,0:T(8,128)(2,1)S(1)}, bf16[176,512]{1,0:T(8,128)(2,1)S(1)}, u32[]{:S(2)}, u32[]{:S(2)}) collective-permute-start(bf16[176,512]{1,0:T(8,128)(2,1)S(1)} %collective-permute-done.5.block_ref), channel_id=1, source_target_pairs={{0,1},{1,0},{2,3},{3,2},{4,5},{5,4},{6,7},{7,6},{8,9},{9,8},{10,11... | collective-permute-start | bytes 540680 | tf_op jit(solution)/shard_map/ppermute | solution.py:326
  24.0 10.2 %collective-permute-start.8 = (bf16[336,256]{1,0:T(8,128)(2,1)S(1)}, bf16[336,256]{1,0:T(8,128)(2,1)S(1)}, u32[]{:S(2)}, u32[]{:S(2)}) collective-permute-start(bf16[336,256]{1,0:T(8,128)(2,1)S(1)} %get-tuple-element.66.own_ref), channel_id=1, source_target_pairs={{0,4},{4,8},{8,12},{12,16},{16,20},{20,24},{24,28},{28,0},{1,5},{5... | collective-permute-start | bytes 516104 | tf_op jit(solution)/shard_map/ppermute | solution.py:424
  26.6 8.9 %collective-permute-start.7 = (bf16[320,256]{1,0:T(8,128)(2,1)S(1)}, bf16[320,256]{1,0:T(8,128)(2,1)S(1)}, u32[]{:S(2)}, u32[]{:S(2)}) collective-permute-start(bf16[320,256]{1,0:T(8,128)(2,1)S(1)} %shard_map.88.own_ref), channel_id=1, source_target_pairs={{0,4},{4,8},{8,12},{12,16},{16,20},{20,24},{24,28},{1,5},{5,9},{9,... | collective-permute-start | bytes 491528 | tf_op jit(solution)/shard_map/ppermute | solution.py:429

commit v5 on v3

--- a/solution.py
+++ b/solution.py
@@ -11,8 +11,10 @@
 BF = jnp.bfloat16
 F32 = jnp.float32
 VMEM = pltpu.VMEM
-LIMIT = 20 * 1024 * 1024
+LIMIT = 12 * 1024 * 1024
 PIECES = 4
+PAD = 16
+SHARE = 1 << 16
 
 
 def dot(left, right):
@@ -40,7 +42,7 @@
         out_specs=jax.tree.map(lambda _: spec(), outs),
         scratch_shapes=scratch,
         compiler_params=pltpu.CompilerParams(vmem_limit_bytes=LIMIT),
-        cost_estimate=pl.CostEstimate(flops=cost, bytes_accessed=1 << 20, transcendentals=0),
+        cost_estimate=pl.CostEstimate(flops=cost // SHARE, bytes_accessed=1 << 10, transcendentals=0),
     )(*args)
 
 
@@ -122,24 +124,33 @@
         out_refs[-1][:, lanes] = mixed.astype(out_refs[-1].dtype)
 
 
+def stage_body(*refs):
+    refs, sems = refs[1:-1], refs[-1]
+    count = len(refs) // 2
+    copies = [
+        pltpu.make_async_copy(refs[i], refs[count + i], sems.at[i]) for i in range(count)
+    ]
+    for copy in copies:
+        copy.start()
+    for copy in copies:
+        copy.wait()
+
+
 def early_body(
     cells_all, cols, exponent, n_sums,
     place_ref, own_ref, sib_ref, *refs,
 ):
     sum_refs, refs = refs[:n_sums], refs[n_sums:]
-    hbm_refs, refs = refs[:6], refs[6:]
+    gain_ref, wq_ref, wk_ref, wv_ref, wo_hbm_ref, taps_hbm_ref, refs = *refs[:6], refs[6:]
     norm_ref, q_ref, k_ref, v_ref, *state_refs = refs[:7]
-    held_refs, gain_ref, sems = refs[7:12], refs[12], refs[13]
-    sources = (*hbm_refs[:5], hbm_refs[5].at[pl.ds(0, 2)])
+    wo_ref, taps_ref, sems = refs[7:]
     copies = [
-        pltpu.make_async_copy(source, target, sems.at[i])
-        for i, (source, target) in enumerate(zip(sources, (gain_ref, *held_refs), strict=True))
+        pltpu.make_async_copy(wo_hbm_ref, wo_ref, sems.at[0]),
+        pltpu.make_async_copy(taps_hbm_ref, taps_ref, sems.at[1]),
     ]
-    for copy in copies[:4]:
+    for copy in copies:
         copy.start()
-    wq_ref, wk_ref, wv_ref = held_refs[:3]
     mean, inverse = moments(sum_refs, cells_all)
-    copies[0].wait()
     gain = gain_ref[...]
     norm_ref[...] = jnp.concatenate(
         [mean, inverse, gain, jnp.zeros((5, mean.shape[1]), F32)], axis=0
@@ -151,15 +162,11 @@
     near = pl.multiple_of(core * (cells - cols), 16)
     halo = normalise(sib_ref[pl.ds(near, cols), :], mean, inverse, gain)
     both = jnp.concatenate([own, sib], axis=0)
-    for copy in copies[1:4]:
-        copy.wait()
-    for copy in copies[4:]:
-        copy.start()
     q_ref[...] = dot(jnp.concatenate([own, halo], axis=0), wq_ref[...]).astype(BF)
     k_ref[...] = dot(both, wk_ref[...]).astype(BF)
     v_ref[...] = dot(both, wv_ref[...]).astype(BF)
     attend(q_ref[...], k_ref[...], v_ref[...], exponent, *state_refs)
-    for copy in copies[4:]:
+    for copy in copies:
         copy.wait()
 
 
@@ -186,12 +193,11 @@
     first_ref, refs = refs[0], refs[1:]
     last_ref, refs = (None, refs) if single else (refs[0], refs[1:])
     (norm_ref, wq_ref, wk_ref, wv_ref, q_ref, k_ref, v_ref, peak_ref, sum_ref, mix_ref,
-     all_q_ref, all_peak_ref, all_sum_ref, all_mix_ref, new_k_ref, new_v_ref) = refs
+     far_ref, all_q_ref, all_peak_ref, all_sum_ref, all_mix_ref, new_k_ref, new_v_ref) = refs
     near = q_ref.shape[0]
-    far_q = dot(
-        normalise(far_rows(place_ref, first_ref, last_ref, cols), *normal_of(norm_ref)),
-        wq_ref[...],
-    ).astype(BF)
+    far = far_rows(place_ref, first_ref, last_ref, cols)
+    far_ref[...] = far
+    far_q = dot(normalise(far, *normal_of(norm_ref)), wq_ref[...]).astype(BF)
     project(first_ref, norm_ref, wk_ref, wv_ref, new_k_ref, new_v_ref)
     all_q_ref[:near] = q_ref[...]
     all_q_ref[near:] = far_q
@@ -227,52 +233,58 @@
     return total
 
 
-def late_body(cols, exponent, single, place_ref, own_ref, sib_ref, *refs):
-    first_ref, refs = refs[0], refs[1:]
-    last_ref, refs = (None, refs) if single else (refs[0], refs[1:])
-    (block_ref, norm_ref, q_ref, peak_ref, sum_ref, mix_ref, k_ref, v_ref, wk_ref, wv_ref, wo_ref,
-     taps_ref, part_ref, wide_ref, mid_ref, keys_ref, values_ref, *new, attended_ref) = refs
+def late_body(
+    cols, exponent,
+    place_ref, own_ref, sib_ref, far_ref, block_ref, norm_ref, q_ref, peak_ref, sum_ref, mix_ref,
+    k_ref, v_ref, wk_ref, wv_ref, wo_ref, taps_ref,
+    even_ref, odd_ref, wide_ref, mid_ref,
+    keys_ref, values_ref, new_peak_ref, new_sum_ref, new_mix_ref, attended_ref,
+):
     cells = own_ref.shape[0]
     core = place_ref[0]
     keys_ref[:cells] = k_ref[...]
     values_ref[:cells] = v_ref[...]
     rest = pl.ds(cells, cells)
     project(block_ref, norm_ref, wk_ref, wv_ref, keys_ref.at[rest], values_ref.at[rest])
+    new = (new_peak_ref, new_sum_ref, new_mix_ref)
     attend(q_ref[...], keys_ref[...], values_ref[...], exponent, *new)
     merge((peak_ref, sum_ref, mix_ref), new, (attended_ref,), exponent, True)
     change = dot(attended_ref[...], wo_ref[...])
     near = pl.multiple_of(core * (cells - cols), 16)
-    far_block = far_rows(place_ref, first_ref, last_ref, cols)
-    base = jnp.concatenate([own_ref[...], sib_ref[pl.ds(near, cols), :], far_block], axis=0)
+    base = jnp.concatenate([own_ref[...], sib_ref[pl.ds(near, cols), :], far_ref[...]], axis=0)
     mid = (base.astype(F32) + change).astype(BF)
     mid_ref[...] = mid[:cells]
     act = jax.nn.silu(mid.astype(F32)).astype(BF).astype(F32)
-    near_act = act[cells : cells + cols]
     far_act = jnp.where(place_ref[1] != 0, act[cells + cols :], 0.0)
-    above = jnp.where(core == 0, far_act, near_act)
-    below = jnp.where(core == 0, near_act, far_act)
-    wide_ref[...] = spread(jnp.concatenate([above, act[:cells], below], axis=0), cols)
+    above = pl.multiple_of(core * (cells + cols), 16)
+    below = pl.multiple_of((1 - core) * (cells + cols), 16)
+    wide_ref[cols : cols + cells] = spread(act[:cells], cols)
+    wide_ref[pl.ds(below, cols), :] = spread(act[cells : cells + cols], cols)
+    wide_ref[pl.ds(above, cols), :] = spread(far_act, cols)
     first_tap = conv(wide_ref, lambda row: taps_ref[0, row], cells, cols)
     second_tap = conv(wide_ref, lambda row: taps_ref[1, row], cells, cols)
-    part_ref[0] = (first_tap + second_tap).astype(BF)
-    part_ref[1] = first_tap.astype(BF)
-
-
-def now_body(cols, wide_ref, mid_ref, conv_ref, skip_ref, out_ref, taps_ref, skip_held_ref, sems):
-    copies = [
-        pltpu.make_async_copy(skip_ref, skip_held_ref, sems.at[0]),
-        pltpu.make_async_copy(conv_ref.at[pl.ds(1, 2)], taps_ref, sems.at[1]),
-    ]
-    for copy in copies:
-        copy.start()
+    even_ref[...] = (first_tap + second_tap).astype(BF)
+    odd_ref[:cells] = first_tap.astype(BF)
+    odd_ref[cells:] = jnp.zeros((PAD, odd_ref.shape[1]), BF)
+
+
+def now_body(cols, wide_ref, mid_ref, taps_ref, skip_hbm_ref, out_ref, skip_ref, sem):
+    copy = pltpu.make_async_copy(skip_hbm_ref, skip_ref, sem)
+    copy.start()
     cells = mid_ref.shape[0]
-    copies[0].wait()
-    skip = dot(mid_ref[...], skip_held_ref[...])
-    copies[1].wait()
-    second_tap = conv(wide_ref, lambda row: taps_ref[0, row], cells, cols)
-    last_tap = conv(wide_ref, lambda row: taps_ref[1, row], cells, cols) + skip
+    second_tap = conv(wide_ref, lambda row: taps_ref[1, row], cells, cols)
+    last_tap = conv(wide_ref, lambda row: taps_ref[2, row], cells, cols)
+    copy.wait()
+    last_tap = last_tap + dot(mid_ref[...], skip_ref[...])
     out_ref[0] = last_tap
     out_ref[1] = last_tap + second_tap
+
+
+def odd_body(place_ref, now_ref, own_ref, arrived_ref, sum_ref):
+    cells = now_ref.shape[1]
+    before = jnp.where(place_ref[2] != 0, own_ref[:cells], arrived_ref[:cells])
+    sum_ref[0] = now_ref[0]
+    sum_ref[1] = now_ref[1] + before.astype(F32)
 
 
 def per_device(
@@ -315,12 +327,22 @@
 
     exponent = channels ** (-0.5) * 1.4426950408889634
     outside = jnp.where(core == 0, me == 0, me == devices - 1)
-    place = jnp.stack([core, 1 - outside.astype(jnp.int32)]).astype(jnp.int32)
+    first_span = lax.axis_index("tm") == 0
+    place = jnp.stack([core, 1 - outside.astype(jnp.int32), first_span.astype(jnp.int32)])
+    place = place.astype(jnp.int32)
     near = cells + cols
     every = near + cols
     taps = conv_weight.reshape(3, 3, 3 * channels, out_channels)
-    weights = [norm_gain.reshape(1, channels), query_weight, key_weight, value_weight, out_weight]
-    first_taps = (2, *taps.shape[1:])
+    weights = [norm_gain.reshape(1, channels), query_weight, key_weight, value_weight]
+    held = call(
+        stage_body,
+        [jax.ShapeDtypeStruct(w.shape, w.dtype) for w in weights],
+        [pltpu.SemaphoreType.DMA((len(weights),))],
+        1 << 20,
+        sums[0], *[hbm(w) for w in weights],
+        spaces=[VMEM] + [pltpu.HBM] * len(weights),
+    )
+    _, wq, wk, wv = held
 
     def rows_of(rows, kind=BF, width=channels):
         return jax.ShapeDtypeStruct((rows, width), kind)
@@ -340,22 +362,21 @@
             rows_of(2 * cells),
             rows_of(2 * cells),
             *state_of(near),
-            *[jax.ShapeDtypeStruct(w.shape, w.dtype) for w in weights[1:]],
-            jax.ShapeDtypeStruct(first_taps, BF),
+            *[jax.ShapeDtypeStruct(w.shape, w.dtype) for w in (out_weight, taps)],
         ],
-        [VMEM((1, channels), F32), pltpu.SemaphoreType.DMA((len(weights) + 1,))],
+        [pltpu.SemaphoreType.DMA((2,))],
         2 * 10**9,
-        place, own, sib, *sums, *[hbm(w) for w in weights], hbm(taps),
-        spaces=[pltpu.SMEM] + [VMEM] * (2 + n_sums) + [pltpu.HBM] * (len(weights) + 1),
-    )
-    state, (wq, wk, wv, wo, held_taps) = rest[:3], rest[3:]
+        place, own, sib, *sums, *held, hbm(out_weight), hbm(taps),
+        spaces=[pltpu.SMEM] + [VMEM] * (6 + n_sums) + [pltpu.HBM] * 2,
+    )
+    state, (wo, held_taps) = rest[:3], rest[3:]
 
     *recv, norm = lax.optimization_barrier((*recv, norm))
     rsib = [lax.ppermute(block, "tile", swap) for block in recv]
     ends = recv[:1] if chips == 2 else [recv[0], recv[-1]]
-    q, *state, new_k, new_v = call(
+    far, q, *state, new_k, new_v = call(
         functools.partial(join_body, cols, exponent, chips == 2),
-        [rows_of(every), *state_of(every), rows_of(cells), rows_of(cells)],
+        [rows_of(cols), rows_of(every), *state_of(every), rows_of(cells), rows_of(cells)],
         [],
         2 * 10**9,
         place, *ends, norm, wq, wk, wv, q, k, v, *state,
@@ -369,30 +390,38 @@
             10**9,
             block, norm, wk, wv, q, *state,
         )
-    part, wide, mid = call(
-        functools.partial(late_body, cols, exponent, chips == 2),
+    even, odd, wide, mid = call(
+        functools.partial(late_body, cols, exponent),
         [
-            jax.ShapeDtypeStruct((2, cells, out_channels), BF),
+            rows_of(cells, BF, out_channels),
+            rows_of(cells + PAD, BF, out_channels),
             rows_of(every, BF, 3 * channels),
             rows_of(cells),
         ],
         scratch_of([rows_of(2 * cells), rows_of(2 * cells), *state_of(every), rows_of(every)]),
         4 * 10**9,
-        place, own, sib, *ends, rsib[-1], norm, q, *state, new_k, new_v, wk, wv, wo, held_taps,
-        spaces=[pltpu.SMEM] + [VMEM] * (14 + len(ends)),
+        place, own, sib, far, rsib[-1], norm, q, *state, new_k, new_v, wk, wv, wo, held_taps,
+        spaces=[pltpu.SMEM] + [VMEM] * 15,
     )
     spans = lax.axis_size("tm")
-    arrived = lax.ppermute(part, "tm", [(i, i + 1) for i in range(spans - 1)])
+    arrived_odd = lax.ppermute(odd, "tm", [(i, (i + 1) % spans) for i in range(spans)])
+    arrived_even = lax.ppermute(even, "tm", [(i, i + 1) for i in range(spans - 1)])
+    both = jax.ShapeDtypeStruct((2, cells, out_channels), F32)
     now = call(
         functools.partial(now_body, cols),
-        jax.ShapeDtypeStruct((2, cells, out_channels), F32),
-        [VMEM(first_taps, BF), VMEM(skip_weight.shape, BF), pltpu.SemaphoreType.DMA((2,))],
+        both,
+        [VMEM(skip_weight.shape, BF), pltpu.SemaphoreType.DMA],
         2 * 10**9,
-        wide, mid, hbm(taps), hbm(skip_weight),
-        spaces=[VMEM, VMEM, pltpu.HBM, pltpu.HBM],
-    )
-    before = jnp.where(lax.axis_index("tm") == 0, part, arrived)
-    decoded = (now + before.astype(F32)).astype(BF)
+        wide, mid, held_taps, hbm(skip_weight),
+        spaces=[VMEM, VMEM, VMEM, pltpu.HBM],
+    )
+    total = call(
+        odd_body, both, [], 1, place, now, odd, arrived_odd, spaces=[pltpu.SMEM] + [VMEM] * 3
+    )
+    total, arrived_even = lax.optimization_barrier((total, arrived_even))
+    before = jnp.where(first_span, even, arrived_even).astype(F32)
+    is_even = lax.broadcasted_iota(jnp.int32, both.shape, 0) == 0
+    decoded = (total + jnp.where(is_even, before, 0.0)).astype(BF)
     return decoded.reshape(2, tile_rows, cols, out_channels)
 
 

time: 34.4 us -> 32.2 us (0.936)
  the two profiles are of different devices: /device:TPU:24 before, /device:TPU:0 now
where the time goes in v5:
time: 32.2 us; the launch traced here: 31.9 us
  Pallas kernels  16.7 us (52%)
  starting transfers between devices  8.41 us (26%)
  waiting for transfers between devices  5.78 us (18%)
  other arithmetic  0.97 us (3%)
    pallas_call x7, Pallas kernels, call(): pl.pallas_call(body, out_shape=outs, in_specs=[spec(s) for s in spaces],...  16.7 us
    ppermute x2, waiting for transfers between devices, turned(): return lax.ppermute(array, 'tile', pairs)  4.22 us
    ppermute x1, starting transfers between devices, per_device(): lax.ppermute(even, 'tm', [(i, i + 1) for i in range(spans - 1)])  3.48 us
    ppermute x2, starting transfers between devices, turned(): return lax.ppermute(array, 'tile', pairs)  2.77 us
    ppermute x1, waiting for transfers between devices, per_device(): lax.ppermute(odd, 'tm', [(i, (i + 1) % spans) for i in range(spans)])  1.55 us
    ppermute x1, starting transfers between devices, per_device(): lax.ppermute(odd, 'tm', [(i, (i + 1) % spans) for i in range(spans)])  1.51 us
    convert_element_type x1, other arithmetic, per_device(): decoded = (total + jnp.where(is_even, before, 0.0)).astype(BF)  0.86 us
  transfers between devices with their start and end apart: 7, of which 3 were waited for; matrix products, arithmetic and copies ran while one was open for 0% of the time, Pallas kernels for 37%

profile of v5, /device:TPU:0, one launch (start us, length us, event | category | flops | bytes accessed | tf_op | source)
XLA Modules:
  0.0 31.9 jit_solution(11559343208836670576)
XLA Ops:
  0.0 0.5 %collective-permute-start = (bf16[320,512]{1,0:T(8,128)(2,1)}, bf16[320,512]{1,0:T(8,128)(2,1)S(1)}, u32[]{:S(2)}, u32[]{:S(2)}) collective-permute-start(bf16[320,512]{1,0:T(8,128)(2,1)} %bitcast.8), channel_id=1, source_target_pairs={{0,1},{1,0},{2,3},{3,2},{4,5},{5,4},{6,7},{7,6},{8,9},{9,8},{10,11... | collective-permute-start | bytes 983048 | tf_op jit(solution)/shard_map/ppermute | solution.py:314
  0.5 1.1 %shard_map.82 = (f32[8,512]{1,0:T(8,128)S(1)}, bf16[320,512]{1,0:T(8,128)(2,1)S(1)}) custom-call(bf16[320,512]{1,0:T(8,128)(2,1)} %bitcast.9), custom_call_target="tpu_custom_call" | custom-call | flops 64 | bytes 1024 | tf_op jit(solution)/shard_map/pallas_call | solution.py:38
  1.5 2.7 %collective-permute-start.2 = (f32[8,512]{1,0:T(8,128)S(1)}, f32[8,512]{1,0:T(8,128)S(1)}, u32[]{:S(2)}, u32[]{:S(2)}) collective-permute-start(f32[8,512]{1,0:T(8,128)S(1)} %get-tuple-element.36), channel_id=1, source_target_pairs={{0,3},{1,2},{2,1},{3,0},{4,7},{5,6},{6,5},{7,4},{8,11},{9,10},{10,... | collective-permute-start | bytes 49160 | tf_op jit(solution)/shard_map/ppermute | solution.py:312
  4.2 0.1 collective-permute-start.1
  4.3 1.4 %collective-permute-done.2 = f32[8,512]{1,0:T(8,128)S(1)} collective-permute-done((f32[8,512]{1,0:T(8,128)S(1)}, f32[8,512]{1,0:T(8,128)S(1)}, u32[]{:S(2)}, u32[]{:S(2)}) %collective-permute-start.2) | collective-permute-done | bytes 16416 | tf_op jit(solution)/shard_map/ppermute | solution.py:312
  5.7 0.1 collective-permute-start.3
  5.8 0.1 pad_add_fusion.place_ref
  5.8 1.4 %shard_map.83 = (f32[1,512]{1,0:T(1,128)S(1)}, bf16[512,512]{1,0:T(8,128)(2,1)S(1)}, bf16[512,512]{1,0:T(8,128)(2,1)S(1)}, bf16[512,512]{1,0:T(8,128)(2,1)S(1)}) custom-call(f32[16,512]{1,0:T(8,128)S(1)} %constant_dynamic-update-slice_fusion.refs_0_, f32[1,512]{1,0:T(1,128)} %bitcast.10, bf16[512,512]{1,0:T(8,128)(2,1)} %refs_2_.1, ...), custom_call_target="tpu_custom_call" | custom-call | flops 16 | bytes 1024 | tf_op jit(solution)/shard_map/pallas_call | solution.py:38
  7.3 0.0 collective-permute-done.3.refs_1_
  7.3 0.0 collective-permute-done.sib_ref
  7.3 3.9 %shard_map.84 = (f32[8,512]{1,0:T(8,128)S(1)}, bf16[480,512]{1,0:T(8,128)(2,1)S(1)}, bf16[640,512]{1,0:T(8,128)(2,1)S(1)}, bf16[640,512]{1,0:T(8,128)(2,1)S(1)},...) custom-call(s32[3]{0:T(128)S(1)} %pad_add_fusion.place_ref, ...), custom_call_target="tpu_custom_call" | custom-call | flops 30517 | bytes 1024 | tf_op jit(solution)/shard_map/pallas_call | solution.py:38
  11.2 2.8 %collective-permute-done.1.refs_0_ = bf16[320,512]{1,0:T(8,128)(2,1)S(1)} collective-permute-done((bf16[320,512]{1,0:T(8,128)(2,1)S(1)}, bf16[320,512]{1,0:T(8,128)(2,1)S(1)}, u32[]{:S(2)}, u32[]{:S(2)}) %collective-permute-start.1) | collective-permute-done | bytes 327712 | tf_op jit(solution)/shard_map/ppermute | solution.py:312
  14.1 0.1 collective-permute-start.4
  14.2 1.7 %shard_map.85 = (bf16[160,512]{1,0:T(8,128)(2,1)S(1)}, bf16[640,512]{1,0:T(8,128)(2,1)S(1)}, f32[640,128]{1,0:T(8,128)S(1)}, f32[640,128]{1,0:T(8,128)S(1)}, f32...) custom-call(s32[3]{0:T(128)S(1)} %pad_add_fusion.place_ref, ...), custom_call_target="tpu_custom_call" | custom-call | flops 30517 | bytes 1024 | tf_op jit(solution)/shard_map/pallas_call | solution.py:38
  15.9 0.0 collective-permute-done.4.block_ref
  15.9 5.0 %shard_map.86 = (bf16[320,256]{1,0:T(8,128)(2,1)S(1)}, bf16[336,256]{1,0:T(8,128)(2,1)S(1)}, bf16[640,1536]{1,0:T(8,128)(2,1)S(1)}, bf16[320,512]{1,0:T(8,128)(2,1)S(1)}) custom-call(s32[3]{0:T(128)S(1)} %pad_add_fusion.place_ref, bf16[320,512]{1,0:T(8,128)(2,1)S(1)} %get-tuple-element.35.own_ref, bf16[320,512]{1,0:T(8,128)(2,1)S(1)} %collective-permute-done.sib_ref, ...), custom_call_target="tpu_custom_call" | custom-call | flops 61035 | bytes 1024 | tf_op jit(solution)/shard_map/pallas_call | solution.py:38
  20.9 1.5 %collective-permute-start.5 = (bf16[336,256]{1,0:T(8,128)(2,1)S(1)}, bf16[336,256]{1,0:T(8,128)(2,1)S(1)}, u32[]{:S(2)}, u32[]{:S(2)}) collective-permute-start(bf16[336,256]{1,0:T(8,128)(2,1)S(1)} %get-tuple-element.61.own_ref), channel_id=1, source_target_pairs={{0,4},{4,8},{8,12},{12,16},{16,20},{20,24},{24,28},{28,0},{1,5},{5... | collective-permute-start | bytes 516104 | tf_op jit(solution)/shard_map/ppermute | solution.py:407
  22.4 3.5 %collective-permute-start.6 = (bf16[320,256]{1,0:T(8,128)(2,1)S(1)}, bf16[320,256]{1,0:T(8,128)(2,1)S(1)}, u32[]{:S(2)}, u32[]{:S(2)}) collective-permute-start(bf16[320,256]{1,0:T(8,128)(2,1)S(1)} %get-tuple-element.62), channel_id=1, source_target_pairs={{0,4},{4,8},{8,12},{12,16},{16,20},{20,24},{24,28},{1,5},{5,9},{9,... | collective-permute-start | bytes 491528 | tf_op jit(solution)/shard_map/ppermute | solution.py:408
  25.9 2.9 %shard_map.87.now_ref = f32[2,320,256]{2,1,0:T(8,128)S(1)} custom-call(bf16[640,1536]{1,0:T(8,128)(2,1)S(1)} %get-tuple-element.59.wide_ref, bf16[320,512]{1,0:T(8,128)(2,1)S(1)} %get-tuple-element.60.mid_ref, bf16[3,3,1536,256]{3,2,1,0:T(8,128)(2,1)S(1)} %get-tuple-element.58.taps_ref, bf16[512,256]{1,0:T(8,128)(2,1)} %skip_hbm_ref.1), custom_call_target="tpu_custom_call" | custom-call | flops 30517 | bytes 1024 | tf_op jit(solution)/shard_map/pallas_call | solution.py:38
  28.9 1.6 %collective-permute-done.5.arrived_ref = bf16[336,256]{1,0:T(8,128)(2,1)S(1)} collective-permute-done((bf16[336,256]{1,0:T(8,128)(2,1)S(1)}, bf16[336,256]{1,0:T(8,128)(2,1)S(1)}, u32[]{:S(2)}, u32[]{:S(2)}) %collective-permute-start.5) | collective-permute-done | bytes 172064 | tf_op jit(solution)/shard_map/ppermute | solution.py:407
  30.4 0.6 %shard_map.88 = f32[2,320,256]{2,1,0:T(8,128)S(1)} custom-call(s32[3]{0:T(128)S(1)} %pad_add_fusion.place_ref, f32[2,320,256]{2,1,0:T(8,128)S(1)} %shard_map.87.now_ref, bf16[336,256]{1,0:T(8,128)(2,1)S(1)} %get-tuple-element.61.own_ref, bf16[336,256]{1,0:T(8,128)(2,1)S(1)} %collective-permute-done.5.arrived_ref), custom_call_target="tpu_custom_call" | custom-call | bytes 1024 | tf_op jit(solution)/shard_map/pallas_call | solution.py:38
  31.0 0.0 collective-permute-done.6
  31.1 0.9 %add_convert_fusion = bf16[2,320,256]{2,1,0:T(8,128)(2,1)} fusion(f32[2,320,256]{2,1,0:T(8,128)S(1)} %shard_map.88, f32[320,256]{1,0:T(8,128)S(1)} %select_convert_fusion, pred[2]{0:T(512)(128)(4,1)S(1)} %iota_compare_fusion), kind=kLoop, calls=%fused_computation | loop fusion | flops 491520 | bytes 1310722 | tf_op jit(solution)/shard_map/convert_element_type | solution.py:424
  (4 shorter events, 0.0 us)
Async XLA Ops:
  0.0 7.3 %collective-permute-start = (bf16[320,512]{1,0:T(8,128)(2,1)}, bf16[320,512]{1,0:T(8,128)(2,1)S(1)}, u32[]{:S(2)}, u32[]{:S(2)}) collective-permute-start(bf16[320,512]{1,0:T(8,128)(2,1)} %bitcast.8), channel_id=1, source_target_pairs={{0,1},{1,0},{2,3},{3,2},{4,5},{5,4},{6,7},{7,6},{8,9},{9,8},{10,11... | collective-permute-start | bytes 983048 | tf_op jit(solution)/shard_map/ppermute | solution.py:314
  1.5 4.2 %collective-permute-start.2 = (f32[8,512]{1,0:T(8,128)S(1)}, f32[8,512]{1,0:T(8,128)S(1)}, u32[]{:S(2)}, u32[]{:S(2)}) collective-permute-start(f32[8,512]{1,0:T(8,128)S(1)} %get-tuple-element.36), channel_id=1, source_target_pairs={{0,3},{1,2},{2,1},{3,0},{4,7},{5,6},{6,5},{7,4},{8,11},{9,10},{10,... | collective-permute-start | bytes 49160 | tf_op jit(solution)/shard_map/ppermute | solution.py:312
  4.2 9.8 %collective-permute-start.1 = (bf16[320,512]{1,0:T(8,128)(2,1)S(1)}, bf16[320,512]{1,0:T(8,128)(2,1)S(1)}, u32[]{:S(2)}, u32[]{:S(2)}) collective-permute-start(bf16[320,512]{1,0:T(8,128)(2,1)S(1)} %get-tuple-element.35.own_ref), channel_id=1, source_target_pairs={{0,3},{1,2},{2,1},{3,0},{4,7},{5,6},{6,5},{7,4},{8,11},{9,10},{10,... | collective-permute-start | bytes 983048 | tf_op jit(solution)/shard_map/ppermute | solution.py:312
  5.7 1.6 %collective-permute-start.3 = (f32[16,512]{1,0:T(8,128)S(1)}, f32[16,512]{1,0:T(8,128)S(1)}, u32[]{:S(2)}, u32[]{:S(2)}) collective-permute-start(f32[16,512]{1,0:T(8,128)S(1)} %constant_dynamic-update-slice_fusion.refs_0_), channel_id=1, source_target_pairs={{0,1},{1,0},{2,3},{3,2},{4,5},{5,4},{6,7},{7,6},{8,9},{9,8},{10,11... | collective-permute-start | bytes 98312 | tf_op jit(solution)/shard_map/ppermute | solution.py:326
  14.1 1.8 %collective-permute-start.4 = (bf16[320,512]{1,0:T(8,128)(2,1)S(1)}, bf16[320,512]{1,0:T(8,128)(2,1)S(1)}, u32[]{:S(2)}, u32[]{:S(2)}) collective-permute-start(bf16[320,512]{1,0:T(8,128)(2,1)S(1)} %collective-permute-done.1.refs_0_), channel_id=1, source_target_pairs={{0,1},{1,0},{2,3},{3,2},{4,5},{5,4},{6,7},{7,6},{8,9},{9,8},{10,11... | collective-permute-start | bytes 983048 | tf_op jit(solution)/shard_map/ppermute | solution.py:375
  20.9 9.5 %collective-permute-start.5 = (bf16[336,256]{1,0:T(8,128)(2,1)S(1)}, bf16[336,256]{1,0:T(8,128)(2,1)S(1)}, u32[]{:S(2)}, u32[]{:S(2)}) collective-permute-start(bf16[336,256]{1,0:T(8,128)(2,1)S(1)} %get-tuple-element.61.own_ref), channel_id=1, source_target_pairs={{0,4},{4,8},{8,12},{12,16},{16,20},{20,24},{24,28},{28,0},{1,5},{5... | collective-permute-start | bytes 516104 | tf_op jit(solution)/shard_map/ppermute | solution.py:407
  22.4 8.6 %collective-permute-start.6 = (bf16[320,256]{1,0:T(8,128)(2,1)S(1)}, bf16[320,256]{1,0:T(8,128)(2,1)S(1)}, u32[]{:S(2)}, u32[]{:S(2)}) collective-permute-start(bf16[320,256]{1,0:T(8,128)(2,1)S(1)} %get-tuple-element.62), channel_id=1, source_target_pairs={{0,4},{4,8},{8,12},{12,16},{16,20},{20,24},{24,28},{1,5},{5,9},{9,... | collective-permute-start | bytes 491528 | tf_op jit(solution)/shard_map/ppermute | solution.py:408

commit v6 on v5

--- a/solution.py
+++ b/solution.py
@@ -14,7 +14,10 @@
 LIMIT = 12 * 1024 * 1024
 PIECES = 4
 PAD = 16
-SHARE = 1 << 16
+STATS_COST = 1 << 6
+STAGE_COST = 1 << 4
+EARLY_COST = 2 * 10**9
+JOIN_COST = LATE_COST = NOW_COST = 1 << 15
 
 
 def dot(left, right):
@@ -42,8 +45,19 @@
         out_specs=jax.tree.map(lambda _: spec(), outs),
         scratch_shapes=scratch,
         compiler_params=pltpu.CompilerParams(vmem_limit_bytes=LIMIT),
-        cost_estimate=pl.CostEstimate(flops=cost // SHARE, bytes_accessed=1 << 10, transcendentals=0),
+        cost_estimate=pl.CostEstimate(flops=cost, bytes_accessed=1 << 10, transcendentals=0),
     )(*args)
+
+
+def core_index():
+    return lax.axis_index("tile") % 2
+
+
+def far_is_inside():
+    me = lax.axis_index("tile")
+    core = me % 2
+    last = lax.axis_size("tile") - 1
+    return me != core * last
 
 
 def stats_body(features_ref, sums_ref, own_ref, sems):
@@ -138,7 +152,7 @@
 
 def early_body(
     cells_all, cols, exponent, n_sums,
-    place_ref, own_ref, sib_ref, *refs,
+    own_ref, sib_ref, *refs,
 ):
     sum_refs, refs = refs[:n_sums], refs[n_sums:]
     gain_ref, wq_ref, wk_ref, wv_ref, wo_hbm_ref, taps_hbm_ref, refs = *refs[:6], refs[6:]
@@ -146,7 +160,7 @@
     wo_ref, taps_ref, sems = refs[7:]
     copies = [
         pltpu.make_async_copy(wo_hbm_ref, wo_ref, sems.at[0]),
-        pltpu.make_async_copy(taps_hbm_ref, taps_ref, sems.at[1]),
+        pltpu.make_async_copy(taps_hbm_ref.at[pl.ds(0, 2)], taps_ref, sems.at[1]),
     ]
     for copy in copies:
         copy.start()
@@ -156,7 +170,7 @@
         [mean, inverse, gain, jnp.zeros((5, mean.shape[1]), F32)], axis=0
     )
     cells = own_ref.shape[0]
-    core = place_ref[0]
+    core = core_index()
     own = normalise(own_ref[...], mean, inverse, gain)
     sib = normalise(sib_ref[...], mean, inverse, gain)
     near = pl.multiple_of(core * (cells - cols), 16)
@@ -174,8 +188,8 @@
     return norm_ref[0:1], norm_ref[1:2], norm_ref[2:3]
 
 
-def far_rows(place_ref, first_ref, last_ref, cols):
-    core = place_ref[0]
+def far_rows(first_ref, last_ref, cols):
+    core = core_index()
     far = pl.multiple_of((1 - core) * (first_ref.shape[0] - cols), 16)
     first = first_ref[pl.ds(far, cols), :]
     if last_ref is None:
@@ -189,13 +203,13 @@
     v_ref[...] = dot(normed, wv_ref[...]).astype(BF)
 
 
-def join_body(cols, exponent, single, place_ref, *refs):
+def join_body(cols, exponent, single, *refs):
     first_ref, refs = refs[0], refs[1:]
     last_ref, refs = (None, refs) if single else (refs[0], refs[1:])
     (norm_ref, wq_ref, wk_ref, wv_ref, q_ref, k_ref, v_ref, peak_ref, sum_ref, mix_ref,
      far_ref, all_q_ref, all_peak_ref, all_sum_ref, all_mix_ref, new_k_ref, new_v_ref) = refs
     near = q_ref.shape[0]
-    far = far_rows(place_ref, first_ref, last_ref, cols)
+    far = far_rows(first_ref, last_ref, cols)
     far_ref[...] = far
     far_q = dot(normalise(far, *normal_of(norm_ref)), wq_ref[...]).astype(BF)
     project(first_ref, norm_ref, wk_ref, wv_ref, new_k_ref, new_v_ref)
@@ -235,13 +249,13 @@
 
 def late_body(
     cols, exponent,
-    place_ref, own_ref, sib_ref, far_ref, block_ref, norm_ref, q_ref, peak_ref, sum_ref, mix_ref,
+    own_ref, sib_ref, far_ref, block_ref, norm_ref, q_ref, peak_ref, sum_ref, mix_ref,
     k_ref, v_ref, wk_ref, wv_ref, wo_ref, taps_ref,
-    even_ref, odd_ref, wide_ref, mid_ref,
+    even_ref, odd_ref, second_ref, wide_ref, mid_ref,
     keys_ref, values_ref, new_peak_ref, new_sum_ref, new_mix_ref, attended_ref,
 ):
     cells = own_ref.shape[0]
-    core = place_ref[0]
+    core = core_index()
     keys_ref[:cells] = k_ref[...]
     values_ref[:cells] = v_ref[...]
     rest = pl.ds(cells, cells)
@@ -255,7 +269,7 @@
     mid = (base.astype(F32) + change).astype(BF)
     mid_ref[...] = mid[:cells]
     act = jax.nn.silu(mid.astype(F32)).astype(BF).astype(F32)
-    far_act = jnp.where(place_ref[1] != 0, act[cells + cols :], 0.0)
+    far_act = jnp.where(far_is_inside(), act[cells + cols :], 0.0)
     above = pl.multiple_of(core * (cells + cols), 16)
     below = pl.multiple_of((1 - core) * (cells + cols), 16)
     wide_ref[cols : cols + cells] = spread(act[:cells], cols)
@@ -263,26 +277,33 @@
     wide_ref[pl.ds(above, cols), :] = spread(far_act, cols)
     first_tap = conv(wide_ref, lambda row: taps_ref[0, row], cells, cols)
     second_tap = conv(wide_ref, lambda row: taps_ref[1, row], cells, cols)
+    second_ref[...] = second_tap
     even_ref[...] = (first_tap + second_tap).astype(BF)
     odd_ref[:cells] = first_tap.astype(BF)
     odd_ref[cells:] = jnp.zeros((PAD, odd_ref.shape[1]), BF)
 
 
-def now_body(cols, wide_ref, mid_ref, taps_ref, skip_hbm_ref, out_ref, skip_ref, sem):
-    copy = pltpu.make_async_copy(skip_hbm_ref, skip_ref, sem)
-    copy.start()
+def now_body(
+    cols, wide_ref, mid_ref, second_ref, taps_ref, skip_hbm_ref, out_ref, tap_ref, skip_ref, sems
+):
+    copies = [
+        pltpu.make_async_copy(skip_hbm_ref, skip_ref, sems.at[0]),
+        pltpu.make_async_copy(taps_ref.at[2], tap_ref, sems.at[1]),
+    ]
+    for copy in copies:
+        copy.start()
     cells = mid_ref.shape[0]
-    second_tap = conv(wide_ref, lambda row: taps_ref[1, row], cells, cols)
-    last_tap = conv(wide_ref, lambda row: taps_ref[2, row], cells, cols)
-    copy.wait()
-    last_tap = last_tap + dot(mid_ref[...], skip_ref[...])
+    copies[0].wait()
+    skip = dot(mid_ref[...], skip_ref[...])
+    copies[1].wait()
+    last_tap = conv(wide_ref, lambda row: tap_ref[row], cells, cols) + skip
     out_ref[0] = last_tap
-    out_ref[1] = last_tap + second_tap
-
-
-def odd_body(place_ref, now_ref, own_ref, arrived_ref, sum_ref):
+    out_ref[1] = last_tap + second_ref[...]
+
+
+def odd_body(now_ref, own_ref, arrived_ref, sum_ref):
     cells = now_ref.shape[1]
-    before = jnp.where(place_ref[2] != 0, own_ref[:cells], arrived_ref[:cells])
+    before = jnp.where(lax.axis_index("tm") == 0, own_ref[:cells], arrived_ref[:cells])
     sum_ref[0] = now_ref[0]
     sum_ref[1] = now_ref[1] + before.astype(F32)
 
@@ -302,8 +323,6 @@
     cells = tile_rows * cols
     devices = lax.axis_size("tile")
     chips = devices // 2
-    me = lax.axis_index("tile")
-    core = me % 2
     swap = [(i, i ^ 1) for i in range(devices)]
     own = features.reshape(cells, channels)
 
@@ -316,7 +335,7 @@
         stats_body,
         [jax.ShapeDtypeStruct((8, channels), F32), jax.ShapeDtypeStruct(own.shape, BF)],
         [pltpu.SemaphoreType.DMA((PIECES,))],
-        1 << 22,
+        STATS_COST,
         hbm(own),
         spaces=[pltpu.HBM],
     )
@@ -326,19 +345,17 @@
     sums = [sums, lax.ppermute(sums, "tile", swap)]
 
     exponent = channels ** (-0.5) * 1.4426950408889634
-    outside = jnp.where(core == 0, me == 0, me == devices - 1)
     first_span = lax.axis_index("tm") == 0
-    place = jnp.stack([core, 1 - outside.astype(jnp.int32), first_span.astype(jnp.int32)])
-    place = place.astype(jnp.int32)
     near = cells + cols
     every = near + cols
     taps = conv_weight.reshape(3, 3, 3 * channels, out_channels)
+    first_taps = (2, *taps.shape[1:])
     weights = [norm_gain.reshape(1, channels), query_weight, key_weight, value_weight]
     held = call(
         stage_body,
         [jax.ShapeDtypeStruct(w.shape, w.dtype) for w in weights],
         [pltpu.SemaphoreType.DMA((len(weights),))],
-        1 << 20,
+        STAGE_COST,
         sums[0], *[hbm(w) for w in weights],
         spaces=[VMEM] + [pltpu.HBM] * len(weights),
     )
@@ -362,12 +379,13 @@
             rows_of(2 * cells),
             rows_of(2 * cells),
             *state_of(near),
-            *[jax.ShapeDtypeStruct(w.shape, w.dtype) for w in (out_weight, taps)],
+            jax.ShapeDtypeStruct(out_weight.shape, BF),
+            jax.ShapeDtypeStruct(first_taps, BF),
         ],
         [pltpu.SemaphoreType.DMA((2,))],
-        2 * 10**9,
-        place, own, sib, *sums, *held, hbm(out_weight), hbm(taps),
-        spaces=[pltpu.SMEM] + [VMEM] * (6 + n_sums) + [pltpu.HBM] * 2,
+        EARLY_COST,
+        own, sib, *sums, *held, hbm(out_weight), hbm(taps),
+        spaces=[VMEM] * (6 + n_sums) + [pltpu.HBM] * 2,
     )
     state, (wo, held_taps) = rest[:3], rest[3:]
 
@@ -378,9 +396,8 @@
         functools.partial(join_body, cols, exponent, chips == 2),
         [rows_of(cols), rows_of(every), *state_of(every), rows_of(cells), rows_of(cells)],
         [],
-        2 * 10**9,
-        place, *ends, norm, wq, wk, wv, q, k, v, *state,
-        spaces=[pltpu.SMEM] + [VMEM] * (10 + len(ends)),
+        JOIN_COST,
+        *ends, norm, wq, wk, wv, q, k, v, *state,
     )
     for block in recv[1:] + rsib[:-1]:
         state = call(
@@ -390,18 +407,18 @@
             10**9,
             block, norm, wk, wv, q, *state,
         )
-    even, odd, wide, mid = call(
+    even, odd, second, wide, mid = call(
         functools.partial(late_body, cols, exponent),
         [
             rows_of(cells, BF, out_channels),
             rows_of(cells + PAD, BF, out_channels),
+            rows_of(cells, F32, out_channels),
             rows_of(every, BF, 3 * channels),
             rows_of(cells),
         ],
         scratch_of([rows_of(2 * cells), rows_of(2 * cells), *state_of(every), rows_of(every)]),
-        4 * 10**9,
-        place, own, sib, far, rsib[-1], norm, q, *state, new_k, new_v, wk, wv, wo, held_taps,
-        spaces=[pltpu.SMEM] + [VMEM] * 15,
+        LATE_COST,
+        own, sib, far, rsib[-1], norm, q, *state, new_k, new_v, wk, wv, wo, held_taps,
     )
     spans = lax.axis_size("tm")
     arrived_odd = lax.ppermute(odd, "tm", [(i, (i + 1) % spans) for i in range(spans)])
@@ -410,13 +427,17 @@
     now = call(
         functools.partial(now_body, cols),
         both,
-        [VMEM(skip_weight.shape, BF), pltpu.SemaphoreType.DMA],
-        2 * 10**9,
-        wide, mid, held_taps, hbm(skip_weight),
-        spaces=[VMEM, VMEM, VMEM, pltpu.HBM],
+        [
+            VMEM(taps.shape[1:], BF),
+            VMEM(skip_weight.shape, BF),
+            pltpu.SemaphoreType.DMA((2,)),
+        ],
+        NOW_COST,
+        wide, mid, second, hbm(taps), hbm(skip_weight),
+        spaces=[VMEM] * 3 + [pltpu.HBM] * 2,
     )
     total = call(
-        odd_body, both, [], 1, place, now, odd, arrived_odd, spaces=[pltpu.SMEM] + [VMEM] * 3
+        odd_body, both, [], 1, now, odd, arrived_odd
     )
     total, arrived_even = lax.optimization_barrier((total, arrived_even))
     before = jnp.where(first_span, even, arrived_even).astype(F32)

time: 32.2 us -> 30.6 us (0.950)
  the two profiles are of different devices: /device:TPU:0 before, /device:TPU:24 now
where the time goes in v6:
time: 30.6 us; the launch traced here: 30.3 us
  Pallas kernels  15.3 us (50%)
  waiting for transfers between devices  7.9 us (26%)
  starting transfers between devices  6.1 us (20%)
  other arithmetic  0.89 us (3%)
    pallas_call x7, Pallas kernels, call(): pl.pallas_call(body, out_shape=outs, in_specs=[spec(s) for s in spaces],...  15.3 us
    ppermute x2, waiting for transfers between devices, turned(): return lax.ppermute(array, 'tile', pairs)  3.3 us
    ppermute x1, waiting for transfers between devices, per_device(): lax.ppermute(even, 'tm', [(i, i + 1) for i in range(spans - 1)])  2.9 us
    ppermute x1, starting transfers between devices, per_device(): lax.ppermute(even, 'tm', [(i, i + 1) for i in range(spans - 1)])  2.11 us
    ppermute x2, starting transfers between devices, turned(): return lax.ppermute(array, 'tile', pairs)  1.81 us
    ppermute x1, starting transfers between devices, per_device(): lax.ppermute(odd, 'tm', [(i, (i + 1) % spans) for i in range(spans)])  1.55 us
    ppermute x1, waiting for transfers between devices, per_device(): lax.ppermute(odd, 'tm', [(i, (i + 1) % spans) for i in range(spans)])  1.41 us
    convert_element_type x1, other arithmetic, per_device(): decoded = (total + jnp.where(is_even, before, 0.0)).astype(BF)  0.86 us
  transfers between devices with their start and end apart: 7, of which 5 were waited for; matrix products, arithmetic and copies ran while one was open for 0% of the time, Pallas kernels for 36%

profile of v6, /device:TPU:24, one launch (start us, length us, event | category | flops | bytes accessed | tf_op | source)
XLA Modules:
  0.0 30.3 jit_solution(885094055150947802)
XLA Ops:
  0.0 0.0 collective-permute-start
  0.0 1.1 %shard_map.82 = (f32[8,512]{1,0:T(8,128)S(1)}, bf16[320,512]{1,0:T(8,128)(2,1)S(1)}) custom-call(bf16[320,512]{1,0:T(8,128)(2,1)} %bitcast.7), custom_call_target="tpu_custom_call" | custom-call | flops 64 | bytes 1024 | tf_op jit(solution)/shard_map/pallas_call | solution.py:41
  1.1 1.7 %collective-permute-start.2 = (f32[8,512]{1,0:T(8,128)S(1)}, f32[8,512]{1,0:T(8,128)S(1)}, u32[]{:S(2)}, u32[]{:S(2)}) collective-permute-start(f32[8,512]{1,0:T(8,128)S(1)} %get-tuple-element.37), channel_id=1, source_target_pairs={{0,3},{1,2},{2,1},{3,0},{4,7},{5,6},{6,5},{7,4},{8,11},{9,10},{10,... | collective-permute-start | bytes 49160 | tf_op jit(solution)/shard_map/ppermute | solution.py:331
  2.8 0.1 collective-permute-start.1
  2.9 1.4 %collective-permute-done.2 = f32[8,512]{1,0:T(8,128)S(1)} collective-permute-done((f32[8,512]{1,0:T(8,128)S(1)}, f32[8,512]{1,0:T(8,128)S(1)}, u32[]{:S(2)}, u32[]{:S(2)}) %collective-permute-start.2) | collective-permute-done | bytes 16416 | tf_op jit(solution)/shard_map/ppermute | solution.py:331
  4.3 0.5 %collective-permute-start.3 = (f32[16,512]{1,0:T(8,128)S(1)}, f32[16,512]{1,0:T(8,128)S(1)}, u32[]{:S(2)}, u32[]{:S(2)}) collective-permute-start(f32[16,512]{1,0:T(8,128)S(1)} %constant_dynamic-update-slice_fusion.refs_0_), channel_id=1, source_target_pairs={{0,1},{1,0},{2,3},{3,2},{4,5},{5,4},{6,7},{7,6},{8,9},{9,8},{10,11... | collective-permute-start | bytes 98312 | tf_op jit(solution)/shard_map/ppermute | solution.py:345
  4.8 1.4 %shard_map.83 = (f32[1,512]{1,0:T(1,128)S(1)}, bf16[512,512]{1,0:T(8,128)(2,1)S(1)}, bf16[512,512]{1,0:T(8,128)(2,1)S(1)}, bf16[512,512]{1,0:T(8,128)(2,1)S(1)}) custom-call(f32[16,512]{1,0:T(8,128)S(1)} %constant_dynamic-update-slice_fusion.refs_0_, f32[1,512]{1,0:T(1,128)} %bitcast.8, bf16[512,512]{1,0:T(8,128)(2,1)} %refs_2_.1, bf16[512,512]{1,0:T(8,128)(2,1)} %refs_3_.1, ...), custom_call_target="tpu_custom_call" | custom-call | flops 16 | bytes 1024 | tf_op jit(solution)/shard_map/pallas_call | solution.py:41
  6.2 0.0 collective-permute-done.3.refs_1_
  6.2 0.0 collective-permute-done.sib_ref
  6.3 4.5 %shard_map.84 = (f32[8,512]{1,0:T(8,128)S(1)}, bf16[480,512]{1,0:T(8,128)(2,1)S(1)}, bf16[640,512]{1,0:T(8,128)(2,1)S(1)}, bf16[640,512]{1,0:T(8,128)(2,1)S(1)},...) custom-call(bf16[320,512]{1,0:T(8,128)(2,1)S(1)} %get-tuple-element., ...), custom_call_target="tpu_custom_call" | custom-call | flops 2000000000 | bytes 1024 | tf_op jit(solution)/shard_map/pallas_call | solution.py:41
  10.7 1.9 %collective-permute-done.1.refs_0_ = bf16[320,512]{1,0:T(8,128)(2,1)S(1)} collective-permute-done((bf16[320,512]{1,0:T(8,128)(2,1)S(1)}, bf16[320,512]{1,0:T(8,128)(2,1)S(1)}, u32[]{:S(2)}, u32[]{:S(2)}) %collective-permute-start.1) | collective-permute-done | bytes 327712 | tf_op jit(solution)/shard_map/ppermute | solution.py:331
  12.6 0.1 collective-permute-start.4
  12.7 1.2 %shard_map.85 = (bf16[160,512]{1,0:T(8,128)(2,1)S(1)}, bf16[640,512]{1,0:T(8,128)(2,1)S(1)}, f32[640,128]{1,0:T(8,128)S(1)}, f32[640,128]{1,0:T(8,128)S(1)}, f32...) custom-call(bf16[320,512]{1,0:T(8,128)(2,1)S(1)} %collective-permute-done.1.refs_0_, ...), custom_call_target="tpu_custom_call" | custom-call | flops 32768 | bytes 1024 | tf_op jit(solution)/shard_map/pallas_call | solution.py:41
  13.9 0.3 collective-permute-done.4.block_ref
  14.2 4.3 %shard_map.86 = (bf16[320,256]{1,0:T(8,128)(2,1)S(1)}, bf16[336,256]{1,0:T(8,128)(2,1)S(1)}, f32[320,256]{1,0:T(8,128)S(1)}, bf16[640,1536]{1,0:T(8,128)(2,1)S(1)}, bf16[320,512]{1,0:T(8,128)(2,1)S(1)}) custom-call(bf16[320,512]{1,0:T(8,128)(2,1)S(1)} %get-tuple-element.36.own_ref, bf16[320,512]{1,0:T(8,128)(2,1)S(1)} %collective-permute-done.sib_ref, ...), custom_call_target="tpu_custom_call" | custom-call | flops 32768 | bytes 1024 | tf_op jit(solution)/shard_map/pallas_call | solution.py:41
  18.5 1.6 %collective-permute-start.5 = (bf16[336,256]{1,0:T(8,128)(2,1)S(1)}, bf16[336,256]{1,0:T(8,128)(2,1)S(1)}, u32[]{:S(2)}, u32[]{:S(2)}) collective-permute-start(bf16[336,256]{1,0:T(8,128)(2,1)S(1)} %get-tuple-element.63.own_ref), channel_id=1, source_target_pairs={{0,4},{4,8},{8,12},{12,16},{16,20},{20,24},{24,28},{28,0},{1,5},{5... | collective-permute-start | bytes 516104 | tf_op jit(solution)/shard_map/ppermute | solution.py:424
  20.1 2.1 %collective-permute-start.6 = (bf16[320,256]{1,0:T(8,128)(2,1)S(1)}, bf16[320,256]{1,0:T(8,128)(2,1)S(1)}, u32[]{:S(2)}, u32[]{:S(2)}) collective-permute-start(bf16[320,256]{1,0:T(8,128)(2,1)S(1)} %get-tuple-element.64), channel_id=1, source_target_pairs={{0,4},{4,8},{8,12},{12,16},{16,20},{20,24},{24,28},{1,5},{5,9},{9,... | collective-permute-start | bytes 491528 | tf_op jit(solution)/shard_map/ppermute | solution.py:425
  22.2 2.8 %shard_map.87.now_ref = f32[2,320,256]{2,1,0:T(8,128)S(1)} custom-call(bf16[640,1536]{1,0:T(8,128)(2,1)S(1)} %get-tuple-element.60.wide_ref, bf16[320,512]{1,0:T(8,128)(2,1)S(1)} %get-tuple-element.61.mid_ref, f32[320,256]{1,0:T(8,128)S(1)} %get-tuple-element.62.second_ref, bf16[3,3,1536,256]{3,2,1,0:T(8,128)(2,1)} %bitcast.5, bf16[512,256]{1,0:T(8,128)(2,1)} %skip_hbm_ref.1), custom_call_target="tpu_custom_call" | custom-call | flops 32768 | bytes 1024 | tf_op jit(solution)/shard_map/pallas_call | solution.py:41
  25.0 1.4 %collective-permute-done.5.arrived_ref = bf16[336,256]{1,0:T(8,128)(2,1)S(1)} collective-permute-done((bf16[336,256]{1,0:T(8,128)(2,1)S(1)}, bf16[336,256]{1,0:T(8,128)(2,1)S(1)}, u32[]{:S(2)}, u32[]{:S(2)}) %collective-permute-start.5) | collective-permute-done | bytes 172064 | tf_op jit(solution)/shard_map/ppermute | solution.py:424
  26.5 0.1 shard_map.88
  26.5 2.9 %collective-permute-done.6 = bf16[320,256]{1,0:T(8,128)(2,1)S(1)} collective-permute-done((bf16[320,256]{1,0:T(8,128)(2,1)S(1)}, bf16[320,256]{1,0:T(8,128)(2,1)S(1)}, u32[]{:S(2)}, u32[]{:S(2)}) %collective-permute-start.6) | collective-permute-done | bytes 163872 | tf_op jit(solution)/shard_map/ppermute | solution.py:425
  29.5 0.9 %add_convert_fusion = bf16[2,320,256]{2,1,0:T(8,128)(2,1)} fusion(f32[2,320,256]{2,1,0:T(8,128)S(1)} %shard_map.88, f32[320,256]{1,0:T(8,128)S(1)} %select_convert_fusion, pred[2]{0:T(512)(128)(4,1)S(1)} %iota_compare_fusion), kind=kLoop, calls=%fused_computation | loop fusion | flops 491520 | bytes 1310722 | tf_op jit(solution)/shard_map/convert_element_type | solution.py:445
  (4 shorter events, 0.0 us)
Async XLA Ops:
  0.0 6.2 %collective-permute-start = (bf16[320,512]{1,0:T(8,128)(2,1)}, bf16[320,512]{1,0:T(8,128)(2,1)S(1)}, u32[]{:S(2)}, u32[]{:S(2)}) collective-permute-start(bf16[320,512]{1,0:T(8,128)(2,1)} %bitcast.6), channel_id=1, source_target_pairs={{0,1},{1,0},{2,3},{3,2},{4,5},{5,4},{6,7},{7,6},{8,9},{9,8},{10,11... | collective-permute-start | bytes 983048 | tf_op jit(solution)/shard_map/ppermute | solution.py:333
  1.1 3.2 %collective-permute-start.2 = (f32[8,512]{1,0:T(8,128)S(1)}, f32[8,512]{1,0:T(8,128)S(1)}, u32[]{:S(2)}, u32[]{:S(2)}) collective-permute-start(f32[8,512]{1,0:T(8,128)S(1)} %get-tuple-element.37), channel_id=1, source_target_pairs={{0,3},{1,2},{2,1},{3,0},{4,7},{5,6},{6,5},{7,4},{8,11},{9,10},{10,... | collective-permute-start | bytes 49160 | tf_op jit(solution)/shard_map/ppermute | solution.py:331
  2.8 9.8 %collective-permute-start.1 = (bf16[320,512]{1,0:T(8,128)(2,1)S(1)}, bf16[320,512]{1,0:T(8,128)(2,1)S(1)}, u32[]{:S(2)}, u32[]{:S(2)}) collective-permute-start(bf16[320,512]{1,0:T(8,128)(2,1)S(1)} %get-tuple-element.36.own_ref), channel_id=1, source_target_pairs={{0,3},{1,2},{2,1},{3,0},{4,7},{5,6},{6,5},{7,4},{8,11},{9,10},{10,... | collective-permute-start | bytes 983048 | tf_op jit(solution)/shard_map/ppermute | solution.py:331
  4.3 1.9 %collective-permute-start.3 = (f32[16,512]{1,0:T(8,128)S(1)}, f32[16,512]{1,0:T(8,128)S(1)}, u32[]{:S(2)}, u32[]{:S(2)}) collective-permute-start(f32[16,512]{1,0:T(8,128)S(1)} %constant_dynamic-update-slice_fusion.refs_0_), channel_id=1, source_target_pairs={{0,1},{1,0},{2,3},{3,2},{4,5},{5,4},{6,7},{7,6},{8,9},{9,8},{10,11... | collective-permute-start | bytes 98312 | tf_op jit(solution)/shard_map/ppermute | solution.py:345
  12.6 1.6 %collective-permute-start.4 = (bf16[320,512]{1,0:T(8,128)(2,1)S(1)}, bf16[320,512]{1,0:T(8,128)(2,1)S(1)}, u32[]{:S(2)}, u32[]{:S(2)}) collective-permute-start(bf16[320,512]{1,0:T(8,128)(2,1)S(1)} %collective-permute-done.1.refs_0_), channel_id=1, source_target_pairs={{0,1},{1,0},{2,3},{3,2},{4,5},{5,4},{6,7},{7,6},{8,9},{9,8},{10,11... | collective-permute-start | bytes 983048 | tf_op jit(solution)/shard_map/ppermute | solution.py:393
  18.5 7.9 %collective-permute-start.5 = (bf16[336,256]{1,0:T(8,128)(2,1)S(1)}, bf16[336,256]{1,0:T(8,128)(2,1)S(1)}, u32[]{:S(2)}, u32[]{:S(2)}) collective-permute-start(bf16[336,256]{1,0:T(8,128)(2,1)S(1)} %get-tuple-element.63.own_ref), channel_id=1, source_target_pairs={{0,4},{4,8},{8,12},{12,16},{16,20},{20,24},{24,28},{28,0},{1,5},{5... | collective-permute-start | bytes 516104 | tf_op jit(solution)/shard_map/ppermute | solution.py:424
  20.1 9.3 %collective-permute-start.6 = (bf16[320,256]{1,0:T(8,128)(2,1)S(1)}, bf16[320,256]{1,0:T(8,128)(2,1)S(1)}, u32[]{:S(2)}, u32[]{:S(2)}) collective-permute-start(bf16[320,256]{1,0:T(8,128)(2,1)S(1)} %get-tuple-element.64), channel_id=1, source_target_pairs={{0,4},{4,8},{8,12},{12,16},{16,20},{20,24},{24,28},{1,5},{5,9},{9,... | collective-permute-start | bytes 491528 | tf_op jit(solution)/shard_map/ppermute | solution.py:425

commit v7 on v6

--- a/solution.py
+++ b/solution.py
@@ -12,8 +12,7 @@
 F32 = jnp.float32
 VMEM = pltpu.VMEM
 LIMIT = 12 * 1024 * 1024
-PIECES = 4
-PAD = 16
+PIECES = 8
 STATS_COST = 1 << 6
 STAGE_COST = 1 << 4
 EARLY_COST = 2 * 10**9
@@ -279,8 +278,7 @@
     second_tap = conv(wide_ref, lambda row: taps_ref[1, row], cells, cols)
     second_ref[...] = second_tap
     even_ref[...] = (first_tap + second_tap).astype(BF)
-    odd_ref[:cells] = first_tap.astype(BF)
-    odd_ref[cells:] = jnp.zeros((PAD, odd_ref.shape[1]), BF)
+    odd_ref[...] = first_tap.astype(BF)
 
 
 def now_body(
@@ -302,10 +300,19 @@
 
 
 def odd_body(now_ref, own_ref, arrived_ref, sum_ref):
-    cells = now_ref.shape[1]
-    before = jnp.where(lax.axis_index("tm") == 0, own_ref[:cells], arrived_ref[:cells])
-    sum_ref[0] = now_ref[0]
-    sum_ref[1] = now_ref[1] + before.astype(F32)
+    before = jnp.where(lax.axis_index("tm") == 0, own_ref[...], arrived_ref[...])
+    sum_ref[...] = (now_ref[1] + before.astype(F32)).astype(BF)
+
+
+def last_body(odd_ref, now_ref, own_ref, arrived_ref, out_ref, even_ref, sems):
+    odd_copy = pltpu.make_async_copy(odd_ref, out_ref.at[1], sems.at[1])
+    odd_copy.start()
+    before = jnp.where(lax.axis_index("tm") == 0, own_ref[...], arrived_ref[...])
+    even_ref[...] = (now_ref[0] + before.astype(F32)).astype(BF)
+    even_copy = pltpu.make_async_copy(even_ref, out_ref.at[0], sems.at[0])
+    even_copy.start()
+    odd_copy.wait()
+    even_copy.wait()
 
 
 def per_device(
@@ -345,7 +352,6 @@
     sums = [sums, lax.ppermute(sums, "tile", swap)]
 
     exponent = channels ** (-0.5) * 1.4426950408889634
-    first_span = lax.axis_index("tm") == 0
     near = cells + cols
     every = near + cols
     taps = conv_weight.reshape(3, 3, 3 * channels, out_channels)
@@ -411,7 +417,7 @@
         functools.partial(late_body, cols, exponent),
         [
             rows_of(cells, BF, out_channels),
-            rows_of(cells + PAD, BF, out_channels),
+            rows_of(cells, BF, out_channels),
             rows_of(cells, F32, out_channels),
             rows_of(every, BF, 3 * channels),
             rows_of(cells),
@@ -436,13 +442,17 @@
         wide, mid, second, hbm(taps), hbm(skip_weight),
         spaces=[VMEM] * 3 + [pltpu.HBM] * 2,
     )
-    total = call(
-        odd_body, both, [], 1, now, odd, arrived_odd
-    )
-    total, arrived_even = lax.optimization_barrier((total, arrived_even))
-    before = jnp.where(first_span, even, arrived_even).astype(F32)
-    is_even = lax.broadcasted_iota(jnp.int32, both.shape, 0) == 0
-    decoded = (total + jnp.where(is_even, before, 0.0)).astype(BF)
+    share = rows_of(cells, BF, out_channels)
+    done_odd = call(odd_body, share, [], 1, now, odd, arrived_odd)
+    done_odd, arrived_even = lax.optimization_barrier((done_odd, arrived_even))
+    decoded = pl.pallas_call(
+        last_body,
+        out_shape=jax.ShapeDtypeStruct((2, cells, out_channels), BF),
+        in_specs=[spec()] * 4,
+        out_specs=spec(pltpu.HBM),
+        scratch_shapes=[VMEM((cells, out_channels), BF), pltpu.SemaphoreType.DMA((2,))],
+        compiler_params=pltpu.CompilerParams(vmem_limit_bytes=LIMIT),
+    )(done_odd, now, even, arrived_even)
     return decoded.reshape(2, tile_rows, cols, out_channels)
 
 

time: 30.6 us -> 30.2 us (0.987)
  other arithmetic: 0.89 us -> 0 us
  Pallas kernels: 15.3 us -> 15.9 us
    convert_element_type x2 -> x0, other arithmetic: 0.88 us -> none  [the longest x1 0.86 us: per_device(): decoded = (total + jnp.where(is_even, before, 0.0)).astype(BF)]
    pallas_call x0 -> x1, Pallas kernels: none -> 0.74 us  [per_device(): pl.pallas_call(last_body, out_shape=jax.ShapeDtypeStruct((2, cells, out_c...]
    ppermute x1, waiting for transfers between devices: 1.41 us -> 1.05 us  [per_device(): lax.ppermute(odd, 'tm', [(i, (i + 1) % spans) for i in range(spans)])]
  transfers between devices with their start and end apart: 7 -> 7, of which waited for: 5 -> 5; matrix products, arithmetic and copies ran while one was open for 0% -> 0% of each run, Pallas kernels for 36% -> 37%
where the time goes in v7:
time: 30.2 us; the launch traced here: 29.9 us
  Pallas kernels  15.9 us (53%)
  waiting for transfers between devices  7.77 us (26%)
  starting transfers between devices  6.1 us (20%)
    pallas_call x7, Pallas kernels, call(): pl.pallas_call(body, out_shape=outs, in_specs=[spec(s) for s in spaces],...  15.2 us
    ppermute x2, waiting for transfers between devices, turned(): return lax.ppermute(array, 'tile', pairs)  3.3 us
    ppermute x1, waiting for transfers between devices, per_device(): lax.ppermute(even, 'tm', [(i, i + 1) for i in range(spans - 1)])  3.12 us
    ppermute x1, starting transfers between devices, per_device(): lax.ppermute(even, 'tm', [(i, i + 1) for i in range(spans - 1)])  2.12 us
    ppermute x2, starting transfers between devices, turned(): return lax.ppermute(array, 'tile', pairs)  1.81 us
    ppermute x1, starting transfers between devices, per_device(): lax.ppermute(odd, 'tm', [(i, (i + 1) % spans) for i in range(spans)])  1.54 us
    ppermute x1, waiting for transfers between devices, per_device(): lax.ppermute(odd, 'tm', [(i, (i + 1) % spans) for i in range(spans)])  1.05 us
    pallas_call x1, Pallas kernels, per_device(): pl.pallas_call(last_body, out_shape=jax.ShapeDtypeStruct((2, cells, out_c...  0.74 us
  transfers between devices with their start and end apart: 7, of which 5 were waited for; matrix products, arithmetic and copies ran while one was open for 0% of the time, Pallas kernels for 37%

profile of v7, /device:TPU:24, one launch (start us, length us, event | category | flops | bytes accessed | tf_op | source)
XLA Modules:
  0.0 29.9 jit_solution(14111906420610976807)
XLA Ops:
  0.0 0.0 collective-permute-start
  0.0 1.0 %shard_map.82 = (f32[8,512]{1,0:T(8,128)S(1)}, bf16[320,512]{1,0:T(8,128)(2,1)S(1)}) custom-call(bf16[320,512]{1,0:T(8,128)(2,1)} %bitcast.7), custom_call_target="tpu_custom_call" | custom-call | flops 64 | bytes 1024 | tf_op jit(solution)/shard_map/pallas_call | solution.py:40
  1.0 1.7 %collective-permute-start.2 = (f32[8,512]{1,0:T(8,128)S(1)}, f32[8,512]{1,0:T(8,128)S(1)}, u32[]{:S(2)}, u32[]{:S(2)}) collective-permute-start(f32[8,512]{1,0:T(8,128)S(1)} %get-tuple-element.37), channel_id=1, source_target_pairs={{0,3},{1,2},{2,1},{3,0},{4,7},{5,6},{6,5},{7,4},{8,11},{9,10},{10,... | collective-permute-start | bytes 49160 | tf_op jit(solution)/shard_map/ppermute | solution.py:338
  2.7 0.1 collective-permute-start.1
  2.8 1.4 %collective-permute-done.2 = f32[8,512]{1,0:T(8,128)S(1)} collective-permute-done((f32[8,512]{1,0:T(8,128)S(1)}, f32[8,512]{1,0:T(8,128)S(1)}, u32[]{:S(2)}, u32[]{:S(2)}) %collective-permute-start.2) | collective-permute-done | bytes 16416 | tf_op jit(solution)/shard_map/ppermute | solution.py:338
  4.3 0.5 %collective-permute-start.3 = (f32[16,512]{1,0:T(8,128)S(1)}, f32[16,512]{1,0:T(8,128)S(1)}, u32[]{:S(2)}, u32[]{:S(2)}) collective-permute-start(f32[16,512]{1,0:T(8,128)S(1)} %constant_dynamic-update-slice_fusion.refs_0_), channel_id=1, source_target_pairs={{0,1},{1,0},{2,3},{3,2},{4,5},{5,4},{6,7},{7,6},{8,9},{9,8},{10,11... | collective-permute-start | bytes 98312 | tf_op jit(solution)/shard_map/ppermute | solution.py:352
  4.8 1.4 %shard_map.83 = (f32[1,512]{1,0:T(1,128)S(1)}, bf16[512,512]{1,0:T(8,128)(2,1)S(1)}, bf16[512,512]{1,0:T(8,128)(2,1)S(1)}, bf16[512,512]{1,0:T(8,128)(2,1)S(1)}) custom-call(f32[16,512]{1,0:T(8,128)S(1)} %constant_dynamic-update-slice_fusion.refs_0_, f32[1,512]{1,0:T(1,128)} %bitcast.8, bf16[512,512]{1,0:T(8,128)(2,1)} %refs_2_.1, bf16[512,512]{1,0:T(8,128)(2,1)} %refs_3_.1, ...), custom_call_target="tpu_custom_call" | custom-call | flops 16 | bytes 1024 | tf_op jit(solution)/shard_map/pallas_call | solution.py:40
  6.2 0.0 collective-permute-done.3.refs_1_
  6.2 0.0 collective-permute-done.sib_ref
  6.2 4.4 %shard_map.84 = (f32[8,512]{1,0:T(8,128)S(1)}, bf16[480,512]{1,0:T(8,128)(2,1)S(1)}, bf16[640,512]{1,0:T(8,128)(2,1)S(1)}, bf16[640,512]{1,0:T(8,128)(2,1)S(1)},...) custom-call(bf16[320,512]{1,0:T(8,128)(2,1)S(1)} %get-tuple-element., ...), custom_call_target="tpu_custom_call" | custom-call | flops 2000000000 | bytes 1024 | tf_op jit(solution)/shard_map/pallas_call | solution.py:40
  10.7 1.9 %collective-permute-done.1.refs_0_ = bf16[320,512]{1,0:T(8,128)(2,1)S(1)} collective-permute-done((bf16[320,512]{1,0:T(8,128)(2,1)S(1)}, bf16[320,512]{1,0:T(8,128)(2,1)S(1)}, u32[]{:S(2)}, u32[]{:S(2)}) %collective-permute-start.1) | collective-permute-done | bytes 327712 | tf_op jit(solution)/shard_map/ppermute | solution.py:338
  12.5 0.1 collective-permute-start.4
  12.7 1.2 %shard_map.85 = (bf16[160,512]{1,0:T(8,128)(2,1)S(1)}, bf16[640,512]{1,0:T(8,128)(2,1)S(1)}, f32[640,128]{1,0:T(8,128)S(1)}, f32[640,128]{1,0:T(8,128)S(1)}, f32...) custom-call(bf16[320,512]{1,0:T(8,128)(2,1)S(1)} %collective-permute-done.1.refs_0_, ...), custom_call_target="tpu_custom_call" | custom-call | flops 32768 | bytes 1024 | tf_op jit(solution)/shard_map/pallas_call | solution.py:40
  13.9 0.3 collective-permute-done.4.block_ref
  14.2 4.3 %shard_map.86 = (bf16[320,256]{1,0:T(8,128)(2,1)S(1)}, bf16[320,256]{1,0:T(8,128)(2,1)S(1)}, f32[320,256]{1,0:T(8,128)S(1)}, bf16[640,1536]{1,0:T(8,128)(2,1)S(1)}, bf16[320,512]{1,0:T(8,128)(2,1)S(1)}) custom-call(bf16[320,512]{1,0:T(8,128)(2,1)S(1)} %get-tuple-element.36.own_ref, bf16[320,512]{1,0:T(8,128)(2,1)S(1)} %collective-permute-done.sib_ref, ...), custom_call_target="tpu_custom_call" | custom-call | flops 32768 | bytes 1024 | tf_op jit(solution)/shard_map/pallas_call | solution.py:40
  18.5 1.5 %collective-permute-start.5 = (bf16[320,256]{1,0:T(8,128)(2,1)S(1)}, bf16[320,256]{1,0:T(8,128)(2,1)S(1)}, u32[]{:S(2)}, u32[]{:S(2)}) collective-permute-start(bf16[320,256]{1,0:T(8,128)(2,1)S(1)} %get-tuple-element.63.own_ref), channel_id=1, source_target_pairs={{0,4},{4,8},{8,12},{12,16},{16,20},{20,24},{24,28},{28,0},{1,5},{5... | collective-permute-start | bytes 491528 | tf_op jit(solution)/shard_map/ppermute | solution.py:430
  20.0 2.1 %collective-permute-start.6 = (bf16[320,256]{1,0:T(8,128)(2,1)S(1)}, bf16[320,256]{1,0:T(8,128)(2,1)S(1)}, u32[]{:S(2)}, u32[]{:S(2)}) collective-permute-start(bf16[320,256]{1,0:T(8,128)(2,1)S(1)} %get-tuple-element.64.own_ref), channel_id=1, source_target_pairs={{0,4},{4,8},{8,12},{12,16},{16,20},{20,24},{24,28},{1,5},{5,9},{9,... | collective-permute-start | bytes 491528 | tf_op jit(solution)/shard_map/ppermute | solution.py:431
  22.1 2.8 %shard_map.87.now_ref = f32[2,320,256]{2,1,0:T(8,128)S(1)} custom-call(bf16[640,1536]{1,0:T(8,128)(2,1)S(1)} %get-tuple-element.60.wide_ref, bf16[320,512]{1,0:T(8,128)(2,1)S(1)} %get-tuple-element.61.mid_ref, f32[320,256]{1,0:T(8,128)S(1)} %get-tuple-element.62.second_ref, bf16[3,3,1536,256]{3,2,1,0:T(8,128)(2,1)} %bitcast.5, bf16[512,256]{1,0:T(8,128)(2,1)} %skip_hbm_ref.1), custom_call_target="tpu_custom_call" | custom-call | flops 32768 | bytes 1024 | tf_op jit(solution)/shard_map/pallas_call | solution.py:40
  24.9 1.1 %collective-permute-done.5.arrived_ref = bf16[320,256]{1,0:T(8,128)(2,1)S(1)} collective-permute-done((bf16[320,256]{1,0:T(8,128)(2,1)S(1)}, bf16[320,256]{1,0:T(8,128)(2,1)S(1)}, u32[]{:S(2)}, u32[]{:S(2)}) %collective-permute-start.5) | collective-permute-done | bytes 163872 | tf_op jit(solution)/shard_map/ppermute | solution.py:430
  26.0 3.1 %collective-permute-done.6.arrived_ref = bf16[320,256]{1,0:T(8,128)(2,1)S(1)} collective-permute-done((bf16[320,256]{1,0:T(8,128)(2,1)S(1)}, bf16[320,256]{1,0:T(8,128)(2,1)S(1)}, u32[]{:S(2)}, u32[]{:S(2)}) %collective-permute-start.6) | collective-permute-done | bytes 163872 | tf_op jit(solution)/shard_map/ppermute | solution.py:431
  29.2 0.7 %shard_map.89 = bf16[2,320,256]{2,1,0:T(8,128)(2,1)} custom-call(bf16[320,256]{1,0:T(8,128)(2,1)S(1)} %shard_map.88.odd_ref, f32[2,320,256]{2,1,0:T(8,128)S(1)} %shard_map.87.now_ref, bf16[320,256]{1,0:T(8,128)(2,1)S(1)} %get-tuple-element.64.own_ref, bf16[320,256]{1,0:T(8,128)(2,1)S(1)} %collective-permute-done.6.arrived_ref), custom_call_target="tpu_custom_call" | custom-call | tf_op jit(solution)/shard_map/pallas_call | solution.py:448
  (3 shorter events, 0.0 us)
Async XLA Ops:
  0.0 6.2 %collective-permute-start = (bf16[320,512]{1,0:T(8,128)(2,1)}, bf16[320,512]{1,0:T(8,128)(2,1)S(1)}, u32[]{:S(2)}, u32[]{:S(2)}) collective-permute-start(bf16[320,512]{1,0:T(8,128)(2,1)} %bitcast.6), channel_id=1, source_target_pairs={{0,1},{1,0},{2,3},{3,2},{4,5},{5,4},{6,7},{7,6},{8,9},{9,8},{10,11... | collective-permute-start | bytes 983048 | tf_op jit(solution)/shard_map/ppermute | solution.py:340
  1.0 3.2 %collective-permute-start.2 = (f32[8,512]{1,0:T(8,128)S(1)}, f32[8,512]{1,0:T(8,128)S(1)}, u32[]{:S(2)}, u32[]{:S(2)}) collective-permute-start(f32[8,512]{1,0:T(8,128)S(1)} %get-tuple-element.37), channel_id=1, source_target_pairs={{0,3},{1,2},{2,1},{3,0},{4,7},{5,6},{6,5},{7,4},{8,11},{9,10},{10,... | collective-permute-start | bytes 49160 | tf_op jit(solution)/shard_map/ppermute | solution.py:338
  2.7 9.8 %collective-permute-start.1 = (bf16[320,512]{1,0:T(8,128)(2,1)S(1)}, bf16[320,512]{1,0:T(8,128)(2,1)S(1)}, u32[]{:S(2)}, u32[]{:S(2)}) collective-permute-start(bf16[320,512]{1,0:T(8,128)(2,1)S(1)} %get-tuple-element.36.own_ref), channel_id=1, source_target_pairs={{0,3},{1,2},{2,1},{3,0},{4,7},{5,6},{6,5},{7,4},{8,11},{9,10},{10,... | collective-permute-start | bytes 983048 | tf_op jit(solution)/shard_map/ppermute | solution.py:338
  4.3 1.9 %collective-permute-start.3 = (f32[16,512]{1,0:T(8,128)S(1)}, f32[16,512]{1,0:T(8,128)S(1)}, u32[]{:S(2)}, u32[]{:S(2)}) collective-permute-start(f32[16,512]{1,0:T(8,128)S(1)} %constant_dynamic-update-slice_fusion.refs_0_), channel_id=1, source_target_pairs={{0,1},{1,0},{2,3},{3,2},{4,5},{5,4},{6,7},{7,6},{8,9},{9,8},{10,11... | collective-permute-start | bytes 98312 | tf_op jit(solution)/shard_map/ppermute | solution.py:352
  12.5 1.6 %collective-permute-start.4 = (bf16[320,512]{1,0:T(8,128)(2,1)S(1)}, bf16[320,512]{1,0:T(8,128)(2,1)S(1)}, u32[]{:S(2)}, u32[]{:S(2)}) collective-permute-start(bf16[320,512]{1,0:T(8,128)(2,1)S(1)} %collective-permute-done.1.refs_0_), channel_id=1, source_target_pairs={{0,1},{1,0},{2,3},{3,2},{4,5},{5,4},{6,7},{7,6},{8,9},{9,8},{10,11... | collective-permute-start | bytes 983048 | tf_op jit(solution)/shard_map/ppermute | solution.py:399
  18.5 7.5 %collective-permute-start.5 = (bf16[320,256]{1,0:T(8,128)(2,1)S(1)}, bf16[320,256]{1,0:T(8,128)(2,1)S(1)}, u32[]{:S(2)}, u32[]{:S(2)}) collective-permute-start(bf16[320,256]{1,0:T(8,128)(2,1)S(1)} %get-tuple-element.63.own_ref), channel_id=1, source_target_pairs={{0,4},{4,8},{8,12},{12,16},{16,20},{20,24},{24,28},{28,0},{1,5},{5... | collective-permute-start | bytes 491528 | tf_op jit(solution)/shard_map/ppermute | solution.py:430
  20.0 9.2 %collective-permute-start.6 = (bf16[320,256]{1,0:T(8,128)(2,1)S(1)}, bf16[320,256]{1,0:T(8,128)(2,1)S(1)}, u32[]{:S(2)}, u32[]{:S(2)}) collective-permute-start(bf16[320,256]{1,0:T(8,128)(2,1)S(1)} %get-tuple-element.64.own_ref), channel_id=1, source_target_pairs={{0,4},{4,8},{8,12},{12,16},{16,20},{20,24},{24,28},{1,5},{5,9},{9,... | collective-permute-start | bytes 491528 | tf_op jit(solution)/shard_map/ppermute | solution.py:431

commit v8 on v7

--- a/solution.py
+++ b/solution.py
@@ -15,7 +15,7 @@
 PIECES = 8
 STATS_COST = 1 << 6
 STAGE_COST = 1 << 4
-EARLY_COST = 2 * 10**9
+EARLY_COST = 7 * 10**8
 JOIN_COST = LATE_COST = NOW_COST = 1 << 15
 
 
@@ -59,7 +59,7 @@
     return me != core * last
 
 
-def stats_body(features_ref, sums_ref, own_ref, sems):
+def stats_body(features_ref, sums_ref, own_ref, first_ref, second_ref, sems):
     rows = own_ref.shape[0] // PIECES
     copies = []
     for i in range(PIECES):
@@ -78,6 +78,13 @@
     sums_ref[...] = jnp.concatenate(
         [total, squared, jnp.zeros((6, own_ref.shape[1]), F32)], axis=0
     )
+    first = first_ref.shape[0]
+    first_ref[...] = own_ref[:first]
+    second_ref[...] = own_ref[first:]
+
+
+def near_rows(first_ref, second_ref, cols):
+    return jnp.where(core_index() == 0, first_ref[:cols], second_ref[second_ref.shape[0] - cols :])
 
 
 def group_sums(sums, width):
@@ -151,7 +158,7 @@
 
 def early_body(
     cells_all, cols, exponent, n_sums,
-    own_ref, sib_ref, *refs,
+    own_ref, sib_first_ref, sib_second_ref, *refs,
 ):
     sum_refs, refs = refs[:n_sums], refs[n_sums:]
     gain_ref, wq_ref, wk_ref, wv_ref, wo_hbm_ref, taps_hbm_ref, refs = *refs[:6], refs[6:]
@@ -168,12 +175,10 @@
     norm_ref[...] = jnp.concatenate(
         [mean, inverse, gain, jnp.zeros((5, mean.shape[1]), F32)], axis=0
     )
-    cells = own_ref.shape[0]
-    core = core_index()
     own = normalise(own_ref[...], mean, inverse, gain)
-    sib = normalise(sib_ref[...], mean, inverse, gain)
-    near = pl.multiple_of(core * (cells - cols), 16)
-    halo = normalise(sib_ref[pl.ds(near, cols), :], mean, inverse, gain)
+    sib = jnp.concatenate([sib_first_ref[...], sib_second_ref[...]], axis=0)
+    sib = normalise(sib, mean, inverse, gain)
+    halo = normalise(near_rows(sib_first_ref, sib_second_ref, cols), mean, inverse, gain)
     both = jnp.concatenate([own, sib], axis=0)
     q_ref[...] = dot(jnp.concatenate([own, halo], axis=0), wq_ref[...]).astype(BF)
     k_ref[...] = dot(both, wk_ref[...]).astype(BF)
@@ -248,7 +253,7 @@
 
 def late_body(
     cols, exponent,
-    own_ref, sib_ref, far_ref, block_ref, norm_ref, q_ref, peak_ref, sum_ref, mix_ref,
+    own_ref, sib_first_ref, sib_second_ref, far_ref, block_ref, norm_ref, q_ref, peak_ref, sum_ref, mix_ref,
     k_ref, v_ref, wk_ref, wv_ref, wo_ref, taps_ref,
     even_ref, odd_ref, second_ref, wide_ref, mid_ref,
     keys_ref, values_ref, new_peak_ref, new_sum_ref, new_mix_ref, attended_ref,
@@ -263,8 +268,8 @@
     attend(q_ref[...], keys_ref[...], values_ref[...], exponent, *new)
     merge((peak_ref, sum_ref, mix_ref), new, (attended_ref,), exponent, True)
     change = dot(attended_ref[...], wo_ref[...])
-    near = pl.multiple_of(core * (cells - cols), 16)
-    base = jnp.concatenate([own_ref[...], sib_ref[pl.ds(near, cols), :], far_ref[...]], axis=0)
+    near = near_rows(sib_first_ref, sib_second_ref, cols)
+    base = jnp.concatenate([own_ref[...], near, far_ref[...]], axis=0)
     mid = (base.astype(F32) + change).astype(BF)
     mid_ref[...] = mid[:cells]
     act = jax.nn.silu(mid.astype(F32)).astype(BF).astype(F32)
@@ -337,10 +342,12 @@
         pairs = [(i, ((i + 2 * by) % devices) ^ flip) for i in range(devices)]
         return lax.ppermute(array, "tile", pairs)
 
-    sib = lax.ppermute(own, "tile", swap)
-    sums, own = call(
+    sums, own, first, second = call(
         stats_body,
-        [jax.ShapeDtypeStruct((8, channels), F32), jax.ShapeDtypeStruct(own.shape, BF)],
+        [
+            jax.ShapeDtypeStruct((8, channels), F32),
+            *[jax.ShapeDtypeStruct((n, channels), BF) for n in (cells, cols, cells - cols)],
+        ],
         [pltpu.SemaphoreType.DMA((PIECES,))],
         STATS_COST,
         hbm(own),
@@ -349,6 +356,8 @@
     sums = [sums] + [turned(sums, by, 1) for by in range(1, chips)]
     recv = [turned(own, by, 1) for by in range(1, chips)]
     sums = jnp.concatenate(sums, axis=0)
+    first, second, sums = lax.optimization_barrier((first, second, sums))
+    sib = [lax.ppermute(part, "tile", swap) for part in (first, second)]
     sums = [sums, lax.ppermute(sums, "tile", swap)]
 
     exponent = channels ** (-0.5) * 1.4426950408889634
@@ -390,8 +399,8 @@
         ],
         [pltpu.SemaphoreType.DMA((2,))],
         EARLY_COST,
-        own, sib, *sums, *held, hbm(out_weight), hbm(taps),
-        spaces=[VMEM] * (6 + n_sums) + [pltpu.HBM] * 2,
+        own, *sib, *sums, *held, hbm(out_weight), hbm(taps),
+        spaces=[VMEM] * (7 + n_sums) + [pltpu.HBM] * 2,
     )
     state, (wo, held_taps) = rest[:3], rest[3:]
 
@@ -424,7 +433,7 @@
         ],
         scratch_of([rows_of(2 * cells), rows_of(2 * cells), *state_of(every), rows_of(every)]),
         LATE_COST,
-        own, sib, far, rsib[-1], norm, q, *state, new_k, new_v, wk, wv, wo, held_taps,
+        own, *sib, far, rsib[-1], norm, q, *state, new_k, new_v, wk, wv, wo, held_taps,
     )
     spans = lax.axis_size("tm")
     arrived_odd = lax.ppermute(odd, "tm", [(i, (i + 1) % spans) for i in range(spans)])

time: 30.2 us -> 29.4 us (0.974)
  waiting for transfers between devices: 7.77 us -> 6.31 us
  starting transfers between devices: 6.1 us -> 6.72 us
    ppermute x2, waiting for transfers between devices: 3.3 us -> 1.85 us  [turned(): return lax.ppermute(array, 'tile', pairs)]
    ppermute x1, starting transfers between devices: 0.12 us -> 0.65 us  [per_device(): rsib = [lax.ppermute(block, 'tile', swap) for block in recv]]
    ppermute x1 -> x2, starting transfers between devices: 0.01 us -> 0.51 us  [per_device(): sib = [lax.ppermute(part, 'tile', swap) for part in (first, second)]]
    ppermute x1, starting transfers between devices: 0.51 us -> 0.12 us  [per_device(): sums = [sums, lax.ppermute(sums, 'tile', swap)]]
  transfers between devices with their start and end apart: 7 -> 8, of which waited for: 5 -> 4; matrix products, arithmetic and copies ran while one was open for 0% -> 0% of each run, Pallas kernels for 37% -> 34%
where the time goes in v8:
time: 29.4 us; the launch traced here: 29.1 us
  Pallas kernels  16 us (54%)
  starting transfers between devices  6.72 us (23%)
  waiting for transfers between devices  6.31 us (21%)
    pallas_call x7, Pallas kernels, call(): pl.pallas_call(body, out_shape=outs, in_specs=[spec(s) for s in spaces],...  15.3 us
    ppermute x1, waiting for transfers between devices, per_device(): lax.ppermute(even, 'tm', [(i, i + 1) for i in range(spans - 1)])  3.12 us
    ppermute x1, starting transfers between devices, per_device(): lax.ppermute(even, 'tm', [(i, i + 1) for i in range(spans - 1)])  2.09 us
    ppermute x2, waiting for transfers between devices, turned(): return lax.ppermute(array, 'tile', pairs)  1.85 us
    ppermute x2, starting transfers between devices, turned(): return lax.ppermute(array, 'tile', pairs)  1.81 us
    ppermute x1, starting transfers between devices, per_device(): lax.ppermute(odd, 'tm', [(i, (i + 1) % spans) for i in range(spans)])  1.55 us
    ppermute x1, waiting for transfers between devices, per_device(): lax.ppermute(odd, 'tm', [(i, (i + 1) % spans) for i in range(spans)])  1.31 us
    pallas_call x1, Pallas kernels, per_device(): pl.pallas_call(last_body, out_shape=jax.ShapeDtypeStruct((2, cells, out_c...  0.74 us
  transfers between devices with their start and end apart: 8, of which 4 were waited for; matrix products, arithmetic and copies ran while one was open for 0% of the time, Pallas kernels for 34%

profile of v8, /device:TPU:24, one launch (start us, length us, event | category | flops | bytes accessed | tf_op | source)
XLA Modules:
  0.0 29.1 jit_solution(10829136613554127054)
XLA Ops:
  0.0 1.0 %shard_map.82 = (f32[8,512]{1,0:T(8,128)S(1)}, bf16[320,512]{1,0:T(8,128)(2,1)S(1)}, bf16[160,512]{1,0:T(8,128)(2,1)S(1)}, bf16[160,512]{1,0:T(8,128)(2,1)S(1)}) custom-call(bf16[320,512]{1,0:T(8,128)(2,1)} %bitcast.6), custom_call_target="tpu_custom_call" | custom-call | flops 64 | bytes 1024 | tf_op jit(solution)/shard_map/pallas_call | solution.py:40
  1.0 1.0 %collective-permute-start = (f32[8,512]{1,0:T(8,128)S(1)}, f32[8,512]{1,0:T(8,128)S(1)}, u32[]{:S(2)}, u32[]{:S(2)}) collective-permute-start(f32[8,512]{1,0:T(8,128)S(1)} %get-tuple-element.44), channel_id=1, source_target_pairs={{0,3},{1,2},{2,1},{3,0},{4,7},{5,6},{6,5},{7,4},{8,11},{9,10},{10,... | collective-permute-start | bytes 49160 | tf_op jit(solution)/shard_map/ppermute | solution.py:343
  2.1 0.8 %collective-permute-start.3 = (bf16[320,512]{1,0:T(8,128)(2,1)S(1)}, bf16[320,512]{1,0:T(8,128)(2,1)S(1)}, u32[]{:S(2)}, u32[]{:S(2)}) collective-permute-start(bf16[320,512]{1,0:T(8,128)(2,1)S(1)} %get-tuple-element.41.own_ref), channel_id=1, source_target_pairs={{0,3},{1,2},{2,1},{3,0},{4,7},{5,6},{6,5},{7,4},{8,11},{9,10},{10,... | collective-permute-start | bytes 983048 | tf_op jit(solution)/shard_map/ppermute | solution.py:343
  2.8 1.5 %collective-permute-done = f32[8,512]{1,0:T(8,128)S(1)} collective-permute-done((f32[8,512]{1,0:T(8,128)S(1)}, f32[8,512]{1,0:T(8,128)S(1)}, u32[]{:S(2)}, u32[]{:S(2)}) %collective-permute-start) | collective-permute-done | bytes 16416 | tf_op jit(solution)/shard_map/ppermute | solution.py:343
  4.4 0.1 collective-permute-start.1
  4.5 0.4 %collective-permute-start.2 = (bf16[160,512]{1,0:T(8,128)(2,1)S(1)}, bf16[160,512]{1,0:T(8,128)(2,1)S(1)}, u32[]{:S(2)}, u32[]{:S(2)}) collective-permute-start(bf16[160,512]{1,0:T(8,128)(2,1)S(1)} %get-tuple-element.46), channel_id=1, source_target_pairs={{0,1},{1,0},{2,3},{3,2},{4,5},{5,4},{6,7},{7,6},{8,9},{9,8},{10,11... | collective-permute-start | bytes 491528 | tf_op jit(solution)/shard_map/ppermute | solution.py:360
  4.9 0.1 collective-permute-start.4
  5.0 1.4 %shard_map.83 = (f32[1,512]{1,0:T(1,128)S(1)}, bf16[512,512]{1,0:T(8,128)(2,1)S(1)}, bf16[512,512]{1,0:T(8,128)(2,1)S(1)}, bf16[512,512]{1,0:T(8,128)(2,1)S(1)}) custom-call(f32[16,512]{1,0:T(8,128)S(1)} %pad_maximum_fusion.refs_0_, f32[1,512]{1,0:T(1,128)} %bitcast.7, bf16[512,512]{1,0:T(8,128)(2,1)} %refs_2_.1, bf16[512,512]{1,0:T(8,128)(2,1)} %refs_3_.1, ...), custom_call_target="tpu_custom_call" | custom-call | flops 16 | bytes 1024 | tf_op jit(solution)/shard_map/pallas_call | solution.py:40
  6.4 0.0 collective-permute-done.4.refs_1_
  6.4 0.0 collective-permute-done.1.sib_first_ref
  6.4 0.0 collective-permute-done.2.sib_second_ref
  6.4 4.5 %shard_map.84 = (f32[8,512]{1,0:T(8,128)S(1)}, bf16[480,512]{1,0:T(8,128)(2,1)S(1)}, bf16[640,512]{1,0:T(8,128)(2,1)S(1)}, bf16[640,512]{1,0:T(8,128)(2,1)S(1)},...) custom-call(bf16[320,512]{1,0:T(8,128)(2,1)S(1)} %get-tuple-element., ...), custom_call_target="tpu_custom_call" | custom-call | flops 700000000 | bytes 1024 | tf_op jit(solution)/shard_map/pallas_call | solution.py:40
  10.9 0.3 %collective-permute-done.3.refs_0_ = bf16[320,512]{1,0:T(8,128)(2,1)S(1)} collective-permute-done((bf16[320,512]{1,0:T(8,128)(2,1)S(1)}, bf16[320,512]{1,0:T(8,128)(2,1)S(1)}, u32[]{:S(2)}, u32[]{:S(2)}) %collective-permute-start.3) | collective-permute-done | bytes 327712 | tf_op jit(solution)/shard_map/ppermute | solution.py:343
  11.2 0.7 %collective-permute-start.5 = (bf16[320,512]{1,0:T(8,128)(2,1)S(1)}, bf16[320,512]{1,0:T(8,128)(2,1)S(1)}, u32[]{:S(2)}, u32[]{:S(2)}) collective-permute-start(bf16[320,512]{1,0:T(8,128)(2,1)S(1)} %collective-permute-done.3.refs_0_), channel_id=1, source_target_pairs={{0,1},{1,0},{2,3},{3,2},{4,5},{5,4},{6,7},{7,6},{8,9},{9,8},{10,11... | collective-permute-start | bytes 983048 | tf_op jit(solution)/shard_map/ppermute | solution.py:408
  11.9 1.2 %shard_map.85 = (bf16[160,512]{1,0:T(8,128)(2,1)S(1)}, bf16[640,512]{1,0:T(8,128)(2,1)S(1)}, f32[640,128]{1,0:T(8,128)S(1)}, f32[640,128]{1,0:T(8,128)S(1)}, f32...) custom-call(bf16[320,512]{1,0:T(8,128)(2,1)S(1)} %collective-permute-done.3.refs_0_, ...), custom_call_target="tpu_custom_call" | custom-call | flops 32768 | bytes 1024 | tf_op jit(solution)/shard_map/pallas_call | solution.py:40
  13.1 0.0 collective-permute-done.5.block_ref
  13.1 4.3 %shard_map.86 = (bf16[320,256]{1,0:T(8,128)(2,1)S(1)}, bf16[320,256]{1,0:T(8,128)(2,1)S(1)}, f32[320,256]{1,0:T(8,128)S(1)}, bf16[640,1536]{1,0:T(8,128)(2,1)S(1)}, bf16[320,512]{1,0:T(8,128)(2,1)S(1)}) custom-call(bf16[320,512]{1,0:T(8,128)(2,1)S(1)} %get-tuple-element.41.own_ref, bf16[160,512]{1,0:T(8,128)(2,1)S(1)} %collective-permute-done.1.sib_first_ref, ...), custom_call_target="tpu_custom_call" | custom-call | flops 32768 | bytes 1024 | tf_op jit(solution)/shard_map/pallas_call | solution.py:40
  17.5 1.5 %collective-permute-start.6 = (bf16[320,256]{1,0:T(8,128)(2,1)S(1)}, bf16[320,256]{1,0:T(8,128)(2,1)S(1)}, u32[]{:S(2)}, u32[]{:S(2)}) collective-permute-start(bf16[320,256]{1,0:T(8,128)(2,1)S(1)} %get-tuple-element.73.own_ref), channel_id=1, source_target_pairs={{0,4},{4,8},{8,12},{12,16},{16,20},{20,24},{24,28},{28,0},{1,5},{5... | collective-permute-start | bytes 491528 | tf_op jit(solution)/shard_map/ppermute | solution.py:439
  19.0 2.1 %collective-permute-start.7 = (bf16[320,256]{1,0:T(8,128)(2,1)S(1)}, bf16[320,256]{1,0:T(8,128)(2,1)S(1)}, u32[]{:S(2)}, u32[]{:S(2)}) collective-permute-start(bf16[320,256]{1,0:T(8,128)(2,1)S(1)} %get-tuple-element.74.own_ref), channel_id=1, source_target_pairs={{0,4},{4,8},{8,12},{12,16},{16,20},{20,24},{24,28},{1,5},{5,9},{9,... | collective-permute-start | bytes 491528 | tf_op jit(solution)/shard_map/ppermute | solution.py:440
  21.1 2.8 %shard_map.87.now_ref = f32[2,320,256]{2,1,0:T(8,128)S(1)} custom-call(bf16[640,1536]{1,0:T(8,128)(2,1)S(1)} %get-tuple-element.70.wide_ref, bf16[320,512]{1,0:T(8,128)(2,1)S(1)} %get-tuple-element.71.mid_ref, f32[320,256]{1,0:T(8,128)S(1)} %get-tuple-element.72.second_ref, bf16[3,3,1536,256]{3,2,1,0:T(8,128)(2,1)} %bitcast.5, bf16[512,256]{1,0:T(8,128)(2,1)} %skip_hbm_ref.1), custom_call_target="tpu_custom_call" | custom-call | flops 32768 | bytes 1024 | tf_op jit(solution)/shard_map/pallas_call | solution.py:40
  23.9 1.3 %collective-permute-done.6.arrived_ref = bf16[320,256]{1,0:T(8,128)(2,1)S(1)} collective-permute-done((bf16[320,256]{1,0:T(8,128)(2,1)S(1)}, bf16[320,256]{1,0:T(8,128)(2,1)S(1)}, u32[]{:S(2)}, u32[]{:S(2)}) %collective-permute-start.6) | collective-permute-done | bytes 163872 | tf_op jit(solution)/shard_map/ppermute | solution.py:439
  25.3 3.1 %collective-permute-done.7.arrived_ref = bf16[320,256]{1,0:T(8,128)(2,1)S(1)} collective-permute-done((bf16[320,256]{1,0:T(8,128)(2,1)S(1)}, bf16[320,256]{1,0:T(8,128)(2,1)S(1)}, u32[]{:S(2)}, u32[]{:S(2)}) %collective-permute-start.7) | collective-permute-done | bytes 163872 | tf_op jit(solution)/shard_map/ppermute | solution.py:440
  28.4 0.7 %shard_map.89 = bf16[2,320,256]{2,1,0:T(8,128)(2,1)} custom-call(bf16[320,256]{1,0:T(8,128)(2,1)S(1)} %shard_map.88.odd_ref, f32[2,320,256]{2,1,0:T(8,128)S(1)} %shard_map.87.now_ref, bf16[320,256]{1,0:T(8,128)(2,1)S(1)} %get-tuple-element.74.own_ref, bf16[320,256]{1,0:T(8,128)(2,1)S(1)} %collective-permute-done.7.arrived_ref), custom_call_target="tpu_custom_call" | custom-call | tf_op jit(solution)/shard_map/pallas_call | solution.py:457
  (2 shorter events, 0.0 us)
Async XLA Ops:
  1.0 3.3 %collective-permute-start = (f32[8,512]{1,0:T(8,128)S(1)}, f32[8,512]{1,0:T(8,128)S(1)}, u32[]{:S(2)}, u32[]{:S(2)}) collective-permute-start(f32[8,512]{1,0:T(8,128)S(1)} %get-tuple-element.44), channel_id=1, source_target_pairs={{0,3},{1,2},{2,1},{3,0},{4,7},{5,6},{6,5},{7,4},{8,11},{9,10},{10,... | collective-permute-start | bytes 49160 | tf_op jit(solution)/shard_map/ppermute | solution.py:343
  2.1 9.2 %collective-permute-start.3 = (bf16[320,512]{1,0:T(8,128)(2,1)S(1)}, bf16[320,512]{1,0:T(8,128)(2,1)S(1)}, u32[]{:S(2)}, u32[]{:S(2)}) collective-permute-start(bf16[320,512]{1,0:T(8,128)(2,1)S(1)} %get-tuple-element.41.own_ref), channel_id=1, source_target_pairs={{0,3},{1,2},{2,1},{3,0},{4,7},{5,6},{6,5},{7,4},{8,11},{9,10},{10,... | collective-permute-start | bytes 983048 | tf_op jit(solution)/shard_map/ppermute | solution.py:343
  4.4 2.1 %collective-permute-start.1 = (bf16[160,512]{1,0:T(8,128)(2,1)S(1)}, bf16[160,512]{1,0:T(8,128)(2,1)S(1)}, u32[]{:S(2)}, u32[]{:S(2)}) collective-permute-start(bf16[160,512]{1,0:T(8,128)(2,1)S(1)} %get-tuple-element.45), channel_id=1, source_target_pairs={{0,1},{1,0},{2,3},{3,2},{4,5},{5,4},{6,7},{7,6},{8,9},{9,8},{10,11... | collective-permute-start | bytes 491528 | tf_op jit(solution)/shard_map/ppermute | solution.py:360
  4.5 1.9 %collective-permute-start.2 = (bf16[160,512]{1,0:T(8,128)(2,1)S(1)}, bf16[160,512]{1,0:T(8,128)(2,1)S(1)}, u32[]{:S(2)}, u32[]{:S(2)}) collective-permute-start(bf16[160,512]{1,0:T(8,128)(2,1)S(1)} %get-tuple-element.46), channel_id=1, source_target_pairs={{0,1},{1,0},{2,3},{3,2},{4,5},{5,4},{6,7},{7,6},{8,9},{9,8},{10,11... | collective-permute-start | bytes 491528 | tf_op jit(solution)/shard_map/ppermute | solution.py:360
  4.9 1.5 %collective-permute-start.4 = (f32[16,512]{1,0:T(8,128)S(1)}, f32[16,512]{1,0:T(8,128)S(1)}, u32[]{:S(2)}, u32[]{:S(2)}) collective-permute-start(f32[16,512]{1,0:T(8,128)S(1)} %pad_maximum_fusion.refs_0_), channel_id=1, source_target_pairs={{0,1},{1,0},{2,3},{3,2},{4,5},{5,4},{6,7},{7,6},{8,9},{9,8},{10,11... | collective-permute-start | bytes 98312 | tf_op jit(solution)/shard_map/ppermute | solution.py:361
  11.2 1.9 %collective-permute-start.5 = (bf16[320,512]{1,0:T(8,128)(2,1)S(1)}, bf16[320,512]{1,0:T(8,128)(2,1)S(1)}, u32[]{:S(2)}, u32[]{:S(2)}) collective-permute-start(bf16[320,512]{1,0:T(8,128)(2,1)S(1)} %collective-permute-done.3.refs_0_), channel_id=1, source_target_pairs={{0,1},{1,0},{2,3},{3,2},{4,5},{5,4},{6,7},{7,6},{8,9},{9,8},{10,11... | collective-permute-start | bytes 983048 | tf_op jit(solution)/shard_map/ppermute | solution.py:408
  17.5 7.8 %collective-permute-start.6 = (bf16[320,256]{1,0:T(8,128)(2,1)S(1)}, bf16[320,256]{1,0:T(8,128)(2,1)S(1)}, u32[]{:S(2)}, u32[]{:S(2)}) collective-permute-start(bf16[320,256]{1,0:T(8,128)(2,1)S(1)} %get-tuple-element.73.own_ref), channel_id=1, source_target_pairs={{0,4},{4,8},{8,12},{12,16},{16,20},{20,24},{24,28},{28,0},{1,5},{5... | collective-permute-start | bytes 491528 | tf_op jit(solution)/shard_map/ppermute | solution.py:439
  19.0 9.4 %collective-permute-start.7 = (bf16[320,256]{1,0:T(8,128)(2,1)S(1)}, bf16[320,256]{1,0:T(8,128)(2,1)S(1)}, u32[]{:S(2)}, u32[]{:S(2)}) collective-permute-start(bf16[320,256]{1,0:T(8,128)(2,1)S(1)} %get-tuple-element.74.own_ref), channel_id=1, source_target_pairs={{0,4},{4,8},{8,12},{12,16},{16,20},{20,24},{24,28},{1,5},{5,9},{9,... | collective-permute-start | bytes 491528 | tf_op jit(solution)/shard_map/ppermute | solution.py:440

commit v9 on v8

--- a/solution.py
+++ b/solution.py
@@ -118,6 +118,8 @@
 
 def attend(queries, keys, values, exponent, peak_ref, sum_ref, mix_ref):
     scores = dot_t(queries, keys)
+    if callable(values):
+        values = values()
     peak = jnp.max(scores, axis=1, keepdims=True)
     unnormed = jnp.exp2((scores - peak) * exponent)
     peak_ref[...] = jnp.broadcast_to(peak, peak_ref.shape)
@@ -182,8 +184,12 @@
     both = jnp.concatenate([own, sib], axis=0)
     q_ref[...] = dot(jnp.concatenate([own, halo], axis=0), wq_ref[...]).astype(BF)
     k_ref[...] = dot(both, wk_ref[...]).astype(BF)
-    v_ref[...] = dot(both, wv_ref[...]).astype(BF)
-    attend(q_ref[...], k_ref[...], v_ref[...], exponent, *state_refs)
+
+    def values():
+        v_ref[...] = dot(both, wv_ref[...]).astype(BF)
+        return v_ref[...]
+
+    attend(q_ref[...], k_ref[...], values, exponent, *state_refs)
     for copy in copies:
         copy.wait()
 
@@ -216,15 +222,17 @@
     far = far_rows(first_ref, last_ref, cols)
     far_ref[...] = far
     far_q = dot(normalise(far, *normal_of(norm_ref)), wq_ref[...]).astype(BF)
-    project(first_ref, norm_ref, wk_ref, wv_ref, new_k_ref, new_v_ref)
     all_q_ref[:near] = q_ref[...]
     all_q_ref[near:] = far_q
     every = (all_peak_ref, all_sum_ref, all_mix_ref)
     for old, new in zip((peak_ref, sum_ref, mix_ref), every, strict=True):
         new[:near] = old[...]
-    attend(
-        far_q, k_ref[...], v_ref[...], exponent, *[ref.at[pl.ds(near, cols)] for ref in every]
-    )
+
+    def values():
+        project(first_ref, norm_ref, wk_ref, wv_ref, new_k_ref, new_v_ref)
+        return v_ref[...]
+
+    attend(far_q, k_ref[...], values, exponent, *[ref.at[pl.ds(near, cols)] for ref in every])
 
 
 def more_body(exponent, block_ref, norm_ref, wk_ref, wv_ref, q_ref, *refs):
@@ -260,12 +268,17 @@
 ):
     cells = own_ref.shape[0]
     core = core_index()
+    normed = normalise(block_ref[...], *normal_of(norm_ref))
     keys_ref[:cells] = k_ref[...]
-    values_ref[:cells] = v_ref[...]
-    rest = pl.ds(cells, cells)
-    project(block_ref, norm_ref, wk_ref, wv_ref, keys_ref.at[rest], values_ref.at[rest])
+    keys_ref[cells:] = dot(normed, wk_ref[...]).astype(BF)
+
+    def values():
+        values_ref[:cells] = v_ref[...]
+        values_ref[cells:] = dot(normed, wv_ref[...]).astype(BF)
+        return values_ref[...]
+
     new = (new_peak_ref, new_sum_ref, new_mix_ref)
-    attend(q_ref[...], keys_ref[...], values_ref[...], exponent, *new)
+    attend(q_ref[...], keys_ref[...], values, exponent, *new)
     merge((peak_ref, sum_ref, mix_ref), new, (attended_ref,), exponent, True)
     change = dot(attended_ref[...], wo_ref[...])
     near = near_rows(sib_first_ref, sib_second_ref, cols)
@@ -276,7 +289,8 @@
     far_act = jnp.where(far_is_inside(), act[cells + cols :], 0.0)
     above = pl.multiple_of(core * (cells + cols), 16)
     below = pl.multiple_of((1 - core) * (cells + cols), 16)
-    wide_ref[cols : cols + cells] = spread(act[:cells], cols)
+    for row in range(0, cells, cols):
+        wide_ref[cols + row : 2 * cols + row] = spread(act[row : row + cols], cols)
     wide_ref[pl.ds(below, cols), :] = spread(act[cells : cells + cols], cols)
     wide_ref[pl.ds(above, cols), :] = spread(far_act, cols)
     first_tap = conv(wide_ref, lambda row: taps_ref[0, row], cells, cols)

time: 29.4 us -> 29.2 us (level)
  Pallas kernels: 16 us -> 13.8 us
  waiting for transfers between devices: 6.31 us -> 8.28 us
    pallas_call x7, Pallas kernels: 15.3 us -> 13.1 us  [call(): pl.pallas_call(body, out_shape=outs, in_specs=[spec(s) for s in spaces],...]
    ppermute x2, waiting for transfers between devices: 1.85 us -> 3.69 us  [turned(): return lax.ppermute(array, 'tile', pairs)]
  transfers between devices with their start and end apart: 8 -> 8, of which waited for: 4 -> 5; matrix products, arithmetic and copies ran while one was open for 0% -> 0% of each run, Pallas kernels for 34% -> 28%
where the time goes in v9:
time: 29.2 us; the launch traced here: 28.9 us
  Pallas kernels  13.8 us (47%)
  waiting for transfers between devices  8.28 us (28%)
  starting transfers between devices  6.74 us (23%)
    pallas_call x7, Pallas kernels, call(): pl.pallas_call(body, out_shape=outs, in_specs=[spec(s) for s in spaces],...  13.1 us
    ppermute x2, waiting for transfers between devices, turned(): return lax.ppermute(array, 'tile', pairs)  3.69 us
    ppermute x1, waiting for transfers between devices, per_device(): lax.ppermute(even, 'tm', [(i, i + 1) for i in range(spans - 1)])  3.12 us
    ppermute x1, starting transfers between devices, per_device(): lax.ppermute(even, 'tm', [(i, i + 1) for i in range(spans - 1)])  2.09 us
    ppermute x2, starting transfers between devices, turned(): return lax.ppermute(array, 'tile', pairs)  1.81 us
    ppermute x1, starting transfers between devices, per_device(): lax.ppermute(odd, 'tm', [(i, (i + 1) % spans) for i in range(spans)])  1.56 us
    ppermute x1, waiting for transfers between devices, per_device(): lax.ppermute(odd, 'tm', [(i, (i + 1) % spans) for i in range(spans)])  1.31 us
    pallas_call x1, Pallas kernels, per_device(): pl.pallas_call(last_body, out_shape=jax.ShapeDtypeStruct((2, cells, out_c...  0.74 us
  transfers between devices with their start and end apart: 8, of which 5 were waited for; matrix products, arithmetic and copies ran while one was open for 0% of the time, Pallas kernels for 28%

profile of v9, /device:TPU:24, one launch (start us, length us, event | category | flops | bytes accessed | tf_op | source)
XLA Modules:
  0.0 28.9 jit_solution(733101424963901310)
XLA Ops:
  0.0 1.0 %shard_map.82 = (f32[8,512]{1,0:T(8,128)S(1)}, bf16[320,512]{1,0:T(8,128)(2,1)S(1)}, bf16[160,512]{1,0:T(8,128)(2,1)S(1)}, bf16[160,512]{1,0:T(8,128)(2,1)S(1)}) custom-call(bf16[320,512]{1,0:T(8,128)(2,1)} %bitcast.6), custom_call_target="tpu_custom_call" | custom-call | flops 64 | bytes 1024 | tf_op jit(solution)/shard_map/pallas_call | solution.py:40
  1.0 1.0 %collective-permute-start = (f32[8,512]{1,0:T(8,128)S(1)}, f32[8,512]{1,0:T(8,128)S(1)}, u32[]{:S(2)}, u32[]{:S(2)}) collective-permute-start(f32[8,512]{1,0:T(8,128)S(1)} %get-tuple-element.44), channel_id=1, source_target_pairs={{0,3},{1,2},{2,1},{3,0},{4,7},{5,6},{6,5},{7,4},{8,11},{9,10},{10,... | collective-permute-start | bytes 49160 | tf_op jit(solution)/shard_map/ppermute | solution.py:357
  2.1 0.8 %collective-permute-start.3 = (bf16[320,512]{1,0:T(8,128)(2,1)S(1)}, bf16[320,512]{1,0:T(8,128)(2,1)S(1)}, u32[]{:S(2)}, u32[]{:S(2)}) collective-permute-start(bf16[320,512]{1,0:T(8,128)(2,1)S(1)} %get-tuple-element.41.own_ref), channel_id=1, source_target_pairs={{0,3},{1,2},{2,1},{3,0},{4,7},{5,6},{6,5},{7,4},{8,11},{9,10},{10,... | collective-permute-start | bytes 983048 | tf_op jit(solution)/shard_map/ppermute | solution.py:357
  2.8 1.5 %collective-permute-done = f32[8,512]{1,0:T(8,128)S(1)} collective-permute-done((f32[8,512]{1,0:T(8,128)S(1)}, f32[8,512]{1,0:T(8,128)S(1)}, u32[]{:S(2)}, u32[]{:S(2)}) %collective-permute-start) | collective-permute-done | bytes 16416 | tf_op jit(solution)/shard_map/ppermute | solution.py:357
  4.4 0.1 collective-permute-start.1
  4.5 0.4 %collective-permute-start.2 = (bf16[160,512]{1,0:T(8,128)(2,1)S(1)}, bf16[160,512]{1,0:T(8,128)(2,1)S(1)}, u32[]{:S(2)}, u32[]{:S(2)}) collective-permute-start(bf16[160,512]{1,0:T(8,128)(2,1)S(1)} %get-tuple-element.46), channel_id=1, source_target_pairs={{0,1},{1,0},{2,3},{3,2},{4,5},{5,4},{6,7},{7,6},{8,9},{9,8},{10,11... | collective-permute-start | bytes 491528 | tf_op jit(solution)/shard_map/ppermute | solution.py:374
  4.9 0.1 collective-permute-start.4
  5.0 1.4 %shard_map.83 = (f32[1,512]{1,0:T(1,128)S(1)}, bf16[512,512]{1,0:T(8,128)(2,1)S(1)}, bf16[512,512]{1,0:T(8,128)(2,1)S(1)}, bf16[512,512]{1,0:T(8,128)(2,1)S(1)}) custom-call(f32[16,512]{1,0:T(8,128)S(1)} %pad_maximum_fusion.refs_0_, f32[1,512]{1,0:T(1,128)} %bitcast.7, bf16[512,512]{1,0:T(8,128)(2,1)} %refs_2_.1, bf16[512,512]{1,0:T(8,128)(2,1)} %refs_3_.1, ...), custom_call_target="tpu_custom_call" | custom-call | flops 16 | bytes 1024 | tf_op jit(solution)/shard_map/pallas_call | solution.py:40
  6.4 0.0 collective-permute-done.4.refs_1_
  6.4 0.0 collective-permute-done.1.sib_first_ref
  6.4 0.0 collective-permute-done.2.sib_second_ref
  6.4 2.6 %shard_map.84 = (f32[8,512]{1,0:T(8,128)S(1)}, bf16[480,512]{1,0:T(8,128)(2,1)S(1)}, bf16[640,512]{1,0:T(8,128)(2,1)S(1)}, bf16[640,512]{1,0:T(8,128)(2,1)S(1)},...) custom-call(bf16[320,512]{1,0:T(8,128)(2,1)S(1)} %get-tuple-element., ...), custom_call_target="tpu_custom_call" | custom-call | flops 700000000 | bytes 1024 | tf_op jit(solution)/shard_map/pallas_call | solution.py:40
  9.1 2.2 %collective-permute-done.3.refs_0_ = bf16[320,512]{1,0:T(8,128)(2,1)S(1)} collective-permute-done((bf16[320,512]{1,0:T(8,128)(2,1)S(1)}, bf16[320,512]{1,0:T(8,128)(2,1)S(1)}, u32[]{:S(2)}, u32[]{:S(2)}) %collective-permute-start.3) | collective-permute-done | bytes 327712 | tf_op jit(solution)/shard_map/ppermute | solution.py:357
  11.2 0.7 %collective-permute-start.5 = (bf16[320,512]{1,0:T(8,128)(2,1)S(1)}, bf16[320,512]{1,0:T(8,128)(2,1)S(1)}, u32[]{:S(2)}, u32[]{:S(2)}) collective-permute-start(bf16[320,512]{1,0:T(8,128)(2,1)S(1)} %collective-permute-done.3.refs_0_), channel_id=1, source_target_pairs={{0,1},{1,0},{2,3},{3,2},{4,5},{5,4},{6,7},{7,6},{8,9},{9,8},{10,11... | collective-permute-start | bytes 983048 | tf_op jit(solution)/shard_map/ppermute | solution.py:422
  11.9 1.1 %shard_map.85 = (bf16[160,512]{1,0:T(8,128)(2,1)S(1)}, bf16[640,512]{1,0:T(8,128)(2,1)S(1)}, f32[640,128]{1,0:T(8,128)S(1)}, f32[640,128]{1,0:T(8,128)S(1)}, f32...) custom-call(bf16[320,512]{1,0:T(8,128)(2,1)S(1)} %collective-permute-done.3.refs_0_, ...), custom_call_target="tpu_custom_call" | custom-call | flops 32768 | bytes 1024 | tf_op jit(solution)/shard_map/pallas_call | solution.py:40
  13.0 0.2 collective-permute-done.5.block_ref
  13.1 4.1 %shard_map.86 = (bf16[320,256]{1,0:T(8,128)(2,1)S(1)}, bf16[320,256]{1,0:T(8,128)(2,1)S(1)}, f32[320,256]{1,0:T(8,128)S(1)}, bf16[640,1536]{1,0:T(8,128)(2,1)S(1)}, bf16[320,512]{1,0:T(8,128)(2,1)S(1)}) custom-call(bf16[320,512]{1,0:T(8,128)(2,1)S(1)} %get-tuple-element.41.own_ref, bf16[160,512]{1,0:T(8,128)(2,1)S(1)} %collective-permute-done.1.sib_first_ref, ...), custom_call_target="tpu_custom_call" | custom-call | flops 32768 | bytes 1024 | tf_op jit(solution)/shard_map/pallas_call | solution.py:40
  17.3 1.6 %collective-permute-start.6 = (bf16[320,256]{1,0:T(8,128)(2,1)S(1)}, bf16[320,256]{1,0:T(8,128)(2,1)S(1)}, u32[]{:S(2)}, u32[]{:S(2)}) collective-permute-start(bf16[320,256]{1,0:T(8,128)(2,1)S(1)} %get-tuple-element.73.own_ref), channel_id=1, source_target_pairs={{0,4},{4,8},{8,12},{12,16},{16,20},{20,24},{24,28},{28,0},{1,5},{5... | collective-permute-start | bytes 491528 | tf_op jit(solution)/shard_map/ppermute | solution.py:453
  18.8 2.1 %collective-permute-start.7 = (bf16[320,256]{1,0:T(8,128)(2,1)S(1)}, bf16[320,256]{1,0:T(8,128)(2,1)S(1)}, u32[]{:S(2)}, u32[]{:S(2)}) collective-permute-start(bf16[320,256]{1,0:T(8,128)(2,1)S(1)} %get-tuple-element.74.own_ref), channel_id=1, source_target_pairs={{0,4},{4,8},{8,12},{12,16},{16,20},{20,24},{24,28},{1,5},{5,9},{9,... | collective-permute-start | bytes 491528 | tf_op jit(solution)/shard_map/ppermute | solution.py:454
  20.9 2.8 %shard_map.87.now_ref = f32[2,320,256]{2,1,0:T(8,128)S(1)} custom-call(bf16[640,1536]{1,0:T(8,128)(2,1)S(1)} %get-tuple-element.70.wide_ref, bf16[320,512]{1,0:T(8,128)(2,1)S(1)} %get-tuple-element.71.mid_ref, f32[320,256]{1,0:T(8,128)S(1)} %get-tuple-element.72.second_ref, bf16[3,3,1536,256]{3,2,1,0:T(8,128)(2,1)} %bitcast.5, bf16[512,256]{1,0:T(8,128)(2,1)} %skip_hbm_ref.1), custom_call_target="tpu_custom_call" | custom-call | flops 32768 | bytes 1024 | tf_op jit(solution)/shard_map/pallas_call | solution.py:40
  23.7 1.3 %collective-permute-done.6.arrived_ref = bf16[320,256]{1,0:T(8,128)(2,1)S(1)} collective-permute-done((bf16[320,256]{1,0:T(8,128)(2,1)S(1)}, bf16[320,256]{1,0:T(8,128)(2,1)S(1)}, u32[]{:S(2)}, u32[]{:S(2)}) %collective-permute-start.6) | collective-permute-done | bytes 163872 | tf_op jit(solution)/shard_map/ppermute | solution.py:453
  25.1 3.1 %collective-permute-done.7.arrived_ref = bf16[320,256]{1,0:T(8,128)(2,1)S(1)} collective-permute-done((bf16[320,256]{1,0:T(8,128)(2,1)S(1)}, bf16[320,256]{1,0:T(8,128)(2,1)S(1)}, u32[]{:S(2)}, u32[]{:S(2)}) %collective-permute-start.7) | collective-permute-done | bytes 163872 | tf_op jit(solution)/shard_map/ppermute | solution.py:454
  28.2 0.7 %shard_map.89 = bf16[2,320,256]{2,1,0:T(8,128)(2,1)} custom-call(bf16[320,256]{1,0:T(8,128)(2,1)S(1)} %shard_map.88.odd_ref, f32[2,320,256]{2,1,0:T(8,128)S(1)} %shard_map.87.now_ref, bf16[320,256]{1,0:T(8,128)(2,1)S(1)} %get-tuple-element.74.own_ref, bf16[320,256]{1,0:T(8,128)(2,1)S(1)} %collective-permute-done.7.arrived_ref), custom_call_target="tpu_custom_call" | custom-call | tf_op jit(solution)/shard_map/pallas_call | solution.py:471
  (2 shorter events, 0.0 us)
Async XLA Ops:
  1.0 3.3 %collective-permute-start = (f32[8,512]{1,0:T(8,128)S(1)}, f32[8,512]{1,0:T(8,128)S(1)}, u32[]{:S(2)}, u32[]{:S(2)}) collective-permute-start(f32[8,512]{1,0:T(8,128)S(1)} %get-tuple-element.44), channel_id=1, source_target_pairs={{0,3},{1,2},{2,1},{3,0},{4,7},{5,6},{6,5},{7,4},{8,11},{9,10},{10,... | collective-permute-start | bytes 49160 | tf_op jit(solution)/shard_map/ppermute | solution.py:357
  2.1 9.2 %collective-permute-start.3 = (bf16[320,512]{1,0:T(8,128)(2,1)S(1)}, bf16[320,512]{1,0:T(8,128)(2,1)S(1)}, u32[]{:S(2)}, u32[]{:S(2)}) collective-permute-start(bf16[320,512]{1,0:T(8,128)(2,1)S(1)} %get-tuple-element.41.own_ref), channel_id=1, source_target_pairs={{0,3},{1,2},{2,1},{3,0},{4,7},{5,6},{6,5},{7,4},{8,11},{9,10},{10,... | collective-permute-start | bytes 983048 | tf_op jit(solution)/shard_map/ppermute | solution.py:357
  4.4 2.1 %collective-permute-start.1 = (bf16[160,512]{1,0:T(8,128)(2,1)S(1)}, bf16[160,512]{1,0:T(8,128)(2,1)S(1)}, u32[]{:S(2)}, u32[]{:S(2)}) collective-permute-start(bf16[160,512]{1,0:T(8,128)(2,1)S(1)} %get-tuple-element.45), channel_id=1, source_target_pairs={{0,1},{1,0},{2,3},{3,2},{4,5},{5,4},{6,7},{7,6},{8,9},{9,8},{10,11... | collective-permute-start | bytes 491528 | tf_op jit(solution)/shard_map/ppermute | solution.py:374
  4.5 1.9 %collective-permute-start.2 = (bf16[160,512]{1,0:T(8,128)(2,1)S(1)}, bf16[160,512]{1,0:T(8,128)(2,1)S(1)}, u32[]{:S(2)}, u32[]{:S(2)}) collective-permute-start(bf16[160,512]{1,0:T(8,128)(2,1)S(1)} %get-tuple-element.46), channel_id=1, source_target_pairs={{0,1},{1,0},{2,3},{3,2},{4,5},{5,4},{6,7},{7,6},{8,9},{9,8},{10,11... | collective-permute-start | bytes 491528 | tf_op jit(solution)/shard_map/ppermute | solution.py:374
  4.9 1.5 %collective-permute-start.4 = (f32[16,512]{1,0:T(8,128)S(1)}, f32[16,512]{1,0:T(8,128)S(1)}, u32[]{:S(2)}, u32[]{:S(2)}) collective-permute-start(f32[16,512]{1,0:T(8,128)S(1)} %pad_maximum_fusion.refs_0_), channel_id=1, source_target_pairs={{0,1},{1,0},{2,3},{3,2},{4,5},{5,4},{6,7},{7,6},{8,9},{9,8},{10,11... | collective-permute-start | bytes 98312 | tf_op jit(solution)/shard_map/ppermute | solution.py:375
  11.2 1.9 %collective-permute-start.5 = (bf16[320,512]{1,0:T(8,128)(2,1)S(1)}, bf16[320,512]{1,0:T(8,128)(2,1)S(1)}, u32[]{:S(2)}, u32[]{:S(2)}) collective-permute-start(bf16[320,512]{1,0:T(8,128)(2,1)S(1)} %collective-permute-done.3.refs_0_), channel_id=1, source_target_pairs={{0,1},{1,0},{2,3},{3,2},{4,5},{5,4},{6,7},{7,6},{8,9},{9,8},{10,11... | collective-permute-start | bytes 983048 | tf_op jit(solution)/shard_map/ppermute | solution.py:422
  17.3 7.8 %collective-permute-start.6 = (bf16[320,256]{1,0:T(8,128)(2,1)S(1)}, bf16[320,256]{1,0:T(8,128)(2,1)S(1)}, u32[]{:S(2)}, u32[]{:S(2)}) collective-permute-start(bf16[320,256]{1,0:T(8,128)(2,1)S(1)} %get-tuple-element.73.own_ref), channel_id=1, source_target_pairs={{0,4},{4,8},{8,12},{12,16},{16,20},{20,24},{24,28},{28,0},{1,5},{5... | collective-permute-start | bytes 491528 | tf_op jit(solution)/shard_map/ppermute | solution.py:453
  18.8 9.4 %collective-permute-start.7 = (bf16[320,256]{1,0:T(8,128)(2,1)S(1)}, bf16[320,256]{1,0:T(8,128)(2,1)S(1)}, u32[]{:S(2)}, u32[]{:S(2)}) collective-permute-start(bf16[320,256]{1,0:T(8,128)(2,1)S(1)} %get-tuple-element.74.own_ref), channel_id=1, source_target_pairs={{0,4},{4,8},{8,12},{12,16},{16,20},{20,24},{24,28},{1,5},{5,9},{9,... | collective-permute-start | bytes 491528 | tf_op jit(solution)/shard_map/ppermute | solution.py:454

commit v10 on v9

--- a/solution.py
+++ b/solution.py
@@ -12,7 +12,7 @@
 F32 = jnp.float32
 VMEM = pltpu.VMEM
 LIMIT = 12 * 1024 * 1024
-PIECES = 8
+PIECES = 5
 STATS_COST = 1 << 6
 STAGE_COST = 1 << 4
 EARLY_COST = 7 * 10**8

time: 29.2 us -> 29.2 us (level)
  transfers between devices with their start and end apart: 8 -> 8, of which waited for: 5 -> 5; matrix products, arithmetic and copies ran while one was open for 0% -> 0% of each run, Pallas kernels for 28% -> 27%
where the time goes in v10:
time: 29.2 us; the launch traced here: 29 us
  Pallas kernels  13.9 us (48%)
  waiting for transfers between devices  8.28 us (28%)
  starting transfers between devices  6.75 us (23%)
    pallas_call x7, Pallas kernels, call(): pl.pallas_call(body, out_shape=outs, in_specs=[spec(s) for s in spaces],...  13.1 us
    ppermute x2, waiting for transfers between devices, turned(): return lax.ppermute(array, 'tile', pairs)  3.69 us
    ppermute x1, waiting for transfers between devices, per_device(): lax.ppermute(even, 'tm', [(i, i + 1) for i in range(spans - 1)])  3.11 us
    ppermute x1, starting transfers between devices, per_device(): lax.ppermute(even, 'tm', [(i, i + 1) for i in range(spans - 1)])  2.1 us
    ppermute x2, starting transfers between devices, turned(): return lax.ppermute(array, 'tile', pairs)  1.81 us
    ppermute x1, starting transfers between devices, per_device(): lax.ppermute(odd, 'tm', [(i, (i + 1) % spans) for i in range(spans)])  1.56 us
    ppermute x1, waiting for transfers between devices, per_device(): lax.ppermute(odd, 'tm', [(i, (i + 1) % spans) for i in range(spans)])  1.32 us
    pallas_call x1, Pallas kernels, per_device(): pl.pallas_call(last_body, out_shape=jax.ShapeDtypeStruct((2, cells, out_c...  0.74 us
  transfers between devices with their start and end apart: 8, of which 5 were waited for; matrix products, arithmetic and copies ran while one was open for 0% of the time, Pallas kernels for 27%

profile of v10, /device:TPU:24, one launch (start us, length us, event | category | flops | bytes accessed | tf_op | source)
XLA Modules:
  0.0 29.0 jit_solution(10969187843197487962)
XLA Ops:
  0.0 1.0 %shard_map.82 = (f32[8,512]{1,0:T(8,128)S(1)}, bf16[320,512]{1,0:T(8,128)(2,1)S(1)}, bf16[160,512]{1,0:T(8,128)(2,1)S(1)}, bf16[160,512]{1,0:T(8,128)(2,1)S(1)}) custom-call(bf16[320,512]{1,0:T(8,128)(2,1)} %bitcast.6), custom_call_target="tpu_custom_call" | custom-call | flops 64 | bytes 1024 | tf_op jit(solution)/shard_map/pallas_call | solution.py:40
  1.1 1.0 %collective-permute-start = (f32[8,512]{1,0:T(8,128)S(1)}, f32[8,512]{1,0:T(8,128)S(1)}, u32[]{:S(2)}, u32[]{:S(2)}) collective-permute-start(f32[8,512]{1,0:T(8,128)S(1)} %get-tuple-element.44), channel_id=1, source_target_pairs={{0,3},{1,2},{2,1},{3,0},{4,7},{5,6},{6,5},{7,4},{8,11},{9,10},{10,... | collective-permute-start | bytes 49160 | tf_op jit(solution)/shard_map/ppermute | solution.py:357
  2.1 0.8 %collective-permute-start.3 = (bf16[320,512]{1,0:T(8,128)(2,1)S(1)}, bf16[320,512]{1,0:T(8,128)(2,1)S(1)}, u32[]{:S(2)}, u32[]{:S(2)}) collective-permute-start(bf16[320,512]{1,0:T(8,128)(2,1)S(1)} %get-tuple-element.41.own_ref), channel_id=1, source_target_pairs={{0,3},{1,2},{2,1},{3,0},{4,7},{5,6},{6,5},{7,4},{8,11},{9,10},{10,... | collective-permute-start | bytes 983048 | tf_op jit(solution)/shard_map/ppermute | solution.py:357
  2.9 1.5 %collective-permute-done = f32[8,512]{1,0:T(8,128)S(1)} collective-permute-done((f32[8,512]{1,0:T(8,128)S(1)}, f32[8,512]{1,0:T(8,128)S(1)}, u32[]{:S(2)}, u32[]{:S(2)}) %collective-permute-start) | collective-permute-done | bytes 16416 | tf_op jit(solution)/shard_map/ppermute | solution.py:357
  4.4 0.1 collective-permute-start.1
  4.5 0.4 %collective-permute-start.2 = (bf16[160,512]{1,0:T(8,128)(2,1)S(1)}, bf16[160,512]{1,0:T(8,128)(2,1)S(1)}, u32[]{:S(2)}, u32[]{:S(2)}) collective-permute-start(bf16[160,512]{1,0:T(8,128)(2,1)S(1)} %get-tuple-element.46), channel_id=1, source_target_pairs={{0,1},{1,0},{2,3},{3,2},{4,5},{5,4},{6,7},{7,6},{8,9},{9,8},{10,11... | collective-permute-start | bytes 491528 | tf_op jit(solution)/shard_map/ppermute | solution.py:374
  4.9 0.1 collective-permute-start.4
  5.0 1.4 %shard_map.83 = (f32[1,512]{1,0:T(1,128)S(1)}, bf16[512,512]{1,0:T(8,128)(2,1)S(1)}, bf16[512,512]{1,0:T(8,128)(2,1)S(1)}, bf16[512,512]{1,0:T(8,128)(2,1)S(1)}) custom-call(f32[16,512]{1,0:T(8,128)S(1)} %pad_maximum_fusion.refs_0_, f32[1,512]{1,0:T(1,128)} %bitcast.7, bf16[512,512]{1,0:T(8,128)(2,1)} %refs_2_.1, bf16[512,512]{1,0:T(8,128)(2,1)} %refs_3_.1, ...), custom_call_target="tpu_custom_call" | custom-call | flops 16 | bytes 1024 | tf_op jit(solution)/shard_map/pallas_call | solution.py:40
  6.4 0.0 collective-permute-done.4.refs_1_
  6.4 0.0 collective-permute-done.1.sib_first_ref
  6.5 0.0 collective-permute-done.2.sib_second_ref
  6.5 2.6 %shard_map.84 = (f32[8,512]{1,0:T(8,128)S(1)}, bf16[480,512]{1,0:T(8,128)(2,1)S(1)}, bf16[640,512]{1,0:T(8,128)(2,1)S(1)}, bf16[640,512]{1,0:T(8,128)(2,1)S(1)},...) custom-call(bf16[320,512]{1,0:T(8,128)(2,1)S(1)} %get-tuple-element., ...), custom_call_target="tpu_custom_call" | custom-call | flops 700000000 | bytes 1024 | tf_op jit(solution)/shard_map/pallas_call | solution.py:40
  9.1 2.2 %collective-permute-done.3.refs_0_ = bf16[320,512]{1,0:T(8,128)(2,1)S(1)} collective-permute-done((bf16[320,512]{1,0:T(8,128)(2,1)S(1)}, bf16[320,512]{1,0:T(8,128)(2,1)S(1)}, u32[]{:S(2)}, u32[]{:S(2)}) %collective-permute-start.3) | collective-permute-done | bytes 327712 | tf_op jit(solution)/shard_map/ppermute | solution.py:357
  11.3 0.7 %collective-permute-start.5 = (bf16[320,512]{1,0:T(8,128)(2,1)S(1)}, bf16[320,512]{1,0:T(8,128)(2,1)S(1)}, u32[]{:S(2)}, u32[]{:S(2)}) collective-permute-start(bf16[320,512]{1,0:T(8,128)(2,1)S(1)} %collective-permute-done.3.refs_0_), channel_id=1, source_target_pairs={{0,1},{1,0},{2,3},{3,2},{4,5},{5,4},{6,7},{7,6},{8,9},{9,8},{10,11... | collective-permute-start | bytes 983048 | tf_op jit(solution)/shard_map/ppermute | solution.py:422
  11.9 1.1 %shard_map.85 = (bf16[160,512]{1,0:T(8,128)(2,1)S(1)}, bf16[640,512]{1,0:T(8,128)(2,1)S(1)}, f32[640,128]{1,0:T(8,128)S(1)}, f32[640,128]{1,0:T(8,128)S(1)}, f32...) custom-call(bf16[320,512]{1,0:T(8,128)(2,1)S(1)} %collective-permute-done.3.refs_0_, ...), custom_call_target="tpu_custom_call" | custom-call | flops 32768 | bytes 1024 | tf_op jit(solution)/shard_map/pallas_call | solution.py:40
  13.0 0.2 collective-permute-done.5.block_ref
  13.2 4.1 %shard_map.86 = (bf16[320,256]{1,0:T(8,128)(2,1)S(1)}, bf16[320,256]{1,0:T(8,128)(2,1)S(1)}, f32[320,256]{1,0:T(8,128)S(1)}, bf16[640,1536]{1,0:T(8,128)(2,1)S(1)}, bf16[320,512]{1,0:T(8,128)(2,1)S(1)}) custom-call(bf16[320,512]{1,0:T(8,128)(2,1)S(1)} %get-tuple-element.41.own_ref, bf16[160,512]{1,0:T(8,128)(2,1)S(1)} %collective-permute-done.1.sib_first_ref, ...), custom_call_target="tpu_custom_call" | custom-call | flops 32768 | bytes 1024 | tf_op jit(solution)/shard_map/pallas_call | solution.py:40
  17.3 1.6 %collective-permute-start.6 = (bf16[320,256]{1,0:T(8,128)(2,1)S(1)}, bf16[320,256]{1,0:T(8,128)(2,1)S(1)}, u32[]{:S(2)}, u32[]{:S(2)}) collective-permute-start(bf16[320,256]{1,0:T(8,128)(2,1)S(1)} %get-tuple-element.73.own_ref), channel_id=1, source_target_pairs={{0,4},{4,8},{8,12},{12,16},{16,20},{20,24},{24,28},{28,0},{1,5},{5... | collective-permute-start | bytes 491528 | tf_op jit(solution)/shard_map/ppermute | solution.py:453
  18.8 2.1 %collective-permute-start.7 = (bf16[320,256]{1,0:T(8,128)(2,1)S(1)}, bf16[320,256]{1,0:T(8,128)(2,1)S(1)}, u32[]{:S(2)}, u32[]{:S(2)}) collective-permute-start(bf16[320,256]{1,0:T(8,128)(2,1)S(1)} %get-tuple-element.74.own_ref), channel_id=1, source_target_pairs={{0,4},{4,8},{8,12},{12,16},{16,20},{20,24},{24,28},{1,5},{5,9},{9,... | collective-permute-start | bytes 491528 | tf_op jit(solution)/shard_map/ppermute | solution.py:454
  21.0 2.8 %shard_map.87.now_ref = f32[2,320,256]{2,1,0:T(8,128)S(1)} custom-call(bf16[640,1536]{1,0:T(8,128)(2,1)S(1)} %get-tuple-element.70.wide_ref, bf16[320,512]{1,0:T(8,128)(2,1)S(1)} %get-tuple-element.71.mid_ref, f32[320,256]{1,0:T(8,128)S(1)} %get-tuple-element.72.second_ref, bf16[3,3,1536,256]{3,2,1,0:T(8,128)(2,1)} %bitcast.5, bf16[512,256]{1,0:T(8,128)(2,1)} %skip_hbm_ref.1), custom_call_target="tpu_custom_call" | custom-call | flops 32768 | bytes 1024 | tf_op jit(solution)/shard_map/pallas_call | solution.py:40
  23.8 1.3 %collective-permute-done.6.arrived_ref = bf16[320,256]{1,0:T(8,128)(2,1)S(1)} collective-permute-done((bf16[320,256]{1,0:T(8,128)(2,1)S(1)}, bf16[320,256]{1,0:T(8,128)(2,1)S(1)}, u32[]{:S(2)}, u32[]{:S(2)}) %collective-permute-start.6) | collective-permute-done | bytes 163872 | tf_op jit(solution)/shard_map/ppermute | solution.py:453
  25.1 3.1 %collective-permute-done.7.arrived_ref = bf16[320,256]{1,0:T(8,128)(2,1)S(1)} collective-permute-done((bf16[320,256]{1,0:T(8,128)(2,1)S(1)}, bf16[320,256]{1,0:T(8,128)(2,1)S(1)}, u32[]{:S(2)}, u32[]{:S(2)}) %collective-permute-start.7) | collective-permute-done | bytes 163872 | tf_op jit(solution)/shard_map/ppermute | solution.py:454
  28.2 0.7 %shard_map.89 = bf16[2,320,256]{2,1,0:T(8,128)(2,1)} custom-call(bf16[320,256]{1,0:T(8,128)(2,1)S(1)} %shard_map.88.odd_ref, f32[2,320,256]{2,1,0:T(8,128)S(1)} %shard_map.87.now_ref, bf16[320,256]{1,0:T(8,128)(2,1)S(1)} %get-tuple-element.74.own_ref, bf16[320,256]{1,0:T(8,128)(2,1)S(1)} %collective-permute-done.7.arrived_ref), custom_call_target="tpu_custom_call" | custom-call | tf_op jit(solution)/shard_map/pallas_call | solution.py:471
  (2 shorter events, 0.0 us)
Async XLA Ops:
  1.1 3.3 %collective-permute-start = (f32[8,512]{1,0:T(8,128)S(1)}, f32[8,512]{1,0:T(8,128)S(1)}, u32[]{:S(2)}, u32[]{:S(2)}) collective-permute-start(f32[8,512]{1,0:T(8,128)S(1)} %get-tuple-element.44), channel_id=1, source_target_pairs={{0,3},{1,2},{2,1},{3,0},{4,7},{5,6},{6,5},{7,4},{8,11},{9,10},{10,... | collective-permute-start | bytes 49160 | tf_op jit(solution)/shard_map/ppermute | solution.py:357
  2.1 9.2 %collective-permute-start.3 = (bf16[320,512]{1,0:T(8,128)(2,1)S(1)}, bf16[320,512]{1,0:T(8,128)(2,1)S(1)}, u32[]{:S(2)}, u32[]{:S(2)}) collective-permute-start(bf16[320,512]{1,0:T(8,128)(2,1)S(1)} %get-tuple-element.41.own_ref), channel_id=1, source_target_pairs={{0,3},{1,2},{2,1},{3,0},{4,7},{5,6},{6,5},{7,4},{8,11},{9,10},{10,... | collective-permute-start | bytes 983048 | tf_op jit(solution)/shard_map/ppermute | solution.py:357
  4.4 2.1 %collective-permute-start.1 = (bf16[160,512]{1,0:T(8,128)(2,1)S(1)}, bf16[160,512]{1,0:T(8,128)(2,1)S(1)}, u32[]{:S(2)}, u32[]{:S(2)}) collective-permute-start(bf16[160,512]{1,0:T(8,128)(2,1)S(1)} %get-tuple-element.45), channel_id=1, source_target_pairs={{0,1},{1,0},{2,3},{3,2},{4,5},{5,4},{6,7},{7,6},{8,9},{9,8},{10,11... | collective-permute-start | bytes 491528 | tf_op jit(solution)/shard_map/ppermute | solution.py:374
  4.5 1.9 %collective-permute-start.2 = (bf16[160,512]{1,0:T(8,128)(2,1)S(1)}, bf16[160,512]{1,0:T(8,128)(2,1)S(1)}, u32[]{:S(2)}, u32[]{:S(2)}) collective-permute-start(bf16[160,512]{1,0:T(8,128)(2,1)S(1)} %get-tuple-element.46), channel_id=1, source_target_pairs={{0,1},{1,0},{2,3},{3,2},{4,5},{5,4},{6,7},{7,6},{8,9},{9,8},{10,11... | collective-permute-start | bytes 491528 | tf_op jit(solution)/shard_map/ppermute | solution.py:374
  4.9 1.5 %collective-permute-start.4 = (f32[16,512]{1,0:T(8,128)S(1)}, f32[16,512]{1,0:T(8,128)S(1)}, u32[]{:S(2)}, u32[]{:S(2)}) collective-permute-start(f32[16,512]{1,0:T(8,128)S(1)} %pad_maximum_fusion.refs_0_), channel_id=1, source_target_pairs={{0,1},{1,0},{2,3},{3,2},{4,5},{5,4},{6,7},{7,6},{8,9},{9,8},{10,11... | collective-permute-start | bytes 98312 | tf_op jit(solution)/shard_map/ppermute | solution.py:375
  11.3 1.9 %collective-permute-start.5 = (bf16[320,512]{1,0:T(8,128)(2,1)S(1)}, bf16[320,512]{1,0:T(8,128)(2,1)S(1)}, u32[]{:S(2)}, u32[]{:S(2)}) collective-permute-start(bf16[320,512]{1,0:T(8,128)(2,1)S(1)} %collective-permute-done.3.refs_0_), channel_id=1, source_target_pairs={{0,1},{1,0},{2,3},{3,2},{4,5},{5,4},{6,7},{7,6},{8,9},{9,8},{10,11... | collective-permute-start | bytes 983048 | tf_op jit(solution)/shard_map/ppermute | solution.py:422
  17.3 7.8 %collective-permute-start.6 = (bf16[320,256]{1,0:T(8,128)(2,1)S(1)}, bf16[320,256]{1,0:T(8,128)(2,1)S(1)}, u32[]{:S(2)}, u32[]{:S(2)}) collective-permute-start(bf16[320,256]{1,0:T(8,128)(2,1)S(1)} %get-tuple-element.73.own_ref), channel_id=1, source_target_pairs={{0,4},{4,8},{8,12},{12,16},{16,20},{20,24},{24,28},{28,0},{1,5},{5... | collective-permute-start | bytes 491528 | tf_op jit(solution)/shard_map/ppermute | solution.py:453
  18.8 9.4 %collective-permute-start.7 = (bf16[320,256]{1,0:T(8,128)(2,1)S(1)}, bf16[320,256]{1,0:T(8,128)(2,1)S(1)}, u32[]{:S(2)}, u32[]{:S(2)}) collective-permute-start(bf16[320,256]{1,0:T(8,128)(2,1)S(1)} %get-tuple-element.74.own_ref), channel_id=1, source_target_pairs={{0,4},{4,8},{8,12},{12,16},{16,20},{20,24},{24,28},{1,5},{5,9},{9,... | collective-permute-start | bytes 491528 | tf_op jit(solution)/shard_map/ppermute | solution.py:454

commit v11 on v10

--- a/solution.py
+++ b/solution.py
@@ -13,6 +13,7 @@
 VMEM = pltpu.VMEM
 LIMIT = 12 * 1024 * 1024
 PIECES = 5
+MOVED = 16
 STATS_COST = 1 << 6
 STAGE_COST = 1 << 4
 EARLY_COST = 7 * 10**8
@@ -296,8 +297,10 @@
     first_tap = conv(wide_ref, lambda row: taps_ref[0, row], cells, cols)
     second_tap = conv(wide_ref, lambda row: taps_ref[1, row], cells, cols)
     second_ref[...] = second_tap
-    even_ref[...] = (first_tap + second_tap).astype(BF)
-    odd_ref[...] = first_tap.astype(BF)
+    even = (first_tap + second_tap).astype(BF)
+    even_ref[...] = even[: cells - MOVED]
+    odd_ref[:cells] = first_tap.astype(BF)
+    odd_ref[cells:] = even[cells - MOVED :]
 
 
 def now_body(
@@ -319,15 +322,20 @@
 
 
 def odd_body(now_ref, own_ref, arrived_ref, sum_ref):
-    before = jnp.where(lax.axis_index("tm") == 0, own_ref[...], arrived_ref[...])
-    sum_ref[...] = (now_ref[1] + before.astype(F32)).astype(BF)
+    cells = now_ref.shape[1]
+    before = jnp.where(lax.axis_index("tm") == 0, own_ref[...], arrived_ref[...]).astype(F32)
+    sum_ref[:cells] = (now_ref[1] + before[:cells]).astype(BF)
+    sum_ref[cells:] = (now_ref[0, cells - MOVED :, :] + before[cells:]).astype(BF)
 
 
 def last_body(odd_ref, now_ref, own_ref, arrived_ref, out_ref, even_ref, sems):
-    odd_copy = pltpu.make_async_copy(odd_ref, out_ref.at[1], sems.at[1])
+    cells = now_ref.shape[1]
+    odd_copy = pltpu.make_async_copy(odd_ref.at[pl.ds(0, cells)], out_ref.at[1], sems.at[1])
     odd_copy.start()
     before = jnp.where(lax.axis_index("tm") == 0, own_ref[...], arrived_ref[...])
-    even_ref[...] = (now_ref[0] + before.astype(F32)).astype(BF)
+    kept = cells - MOVED
+    even_ref[:kept] = (now_ref[0, :kept, :] + before.astype(F32)).astype(BF)
+    even_ref[kept:] = odd_ref[cells:]
     even_copy = pltpu.make_async_copy(even_ref, out_ref.at[0], sems.at[0])
     even_copy.start()
     odd_copy.wait()
@@ -439,8 +447,8 @@
     even, odd, second, wide, mid = call(
         functools.partial(late_body, cols, exponent),
         [
-            rows_of(cells, BF, out_channels),
-            rows_of(cells, BF, out_channels),
+            rows_of(cells - MOVED, BF, out_channels),
+            rows_of(cells + MOVED, BF, out_channels),
             rows_of(cells, F32, out_channels),
             rows_of(every, BF, 3 * channels),
             rows_of(cells),
@@ -450,7 +458,12 @@
         own, *sib, far, rsib[-1], norm, q, *state, new_k, new_v, wk, wv, wo, held_taps,
     )
     spans = lax.axis_size("tm")
-    arrived_odd = lax.ppermute(odd, "tm", [(i, (i + 1) % spans) for i in range(spans)])
+    ring = [
+        (i * devices + j, (i + 1) * devices + j if i + 1 < spans else j ^ 1)
+        for i in range(spans)
+        for j in range(devices)
+    ]
+    arrived_odd = lax.ppermute(odd, ("tm", "tile"), ring)
     arrived_even = lax.ppermute(even, "tm", [(i, i + 1) for i in range(spans - 1)])
     both = jax.ShapeDtypeStruct((2, cells, out_channels), F32)
     now = call(
@@ -465,8 +478,7 @@
         wide, mid, second, hbm(taps), hbm(skip_weight),
         spaces=[VMEM] * 3 + [pltpu.HBM] * 2,
     )
-    share = rows_of(cells, BF, out_channels)
-    done_odd = call(odd_body, share, [], 1, now, odd, arrived_odd)
+    done_odd = call(odd_body, rows_of(cells + MOVED, BF, out_channels), [], 1, now, odd, arrived_odd)
     done_odd, arrived_even = lax.optimization_barrier((done_odd, arrived_even))
     decoded = pl.pallas_call(
         last_body,

time: 29.2 us -> 29.2 us (level)
    ppermute x1, waiting for transfers between devices: 1.32 us -> 1.74 us  [per_device(): arrived_odd = lax.ppermute(odd, ('tm', 'tile'), ring)]
    ppermute x1, waiting for transfers between devices: 3.11 us -> 2.72 us  [per_device(): lax.ppermute(even, 'tm', [(i, i + 1) for i in range(spans - 1)])]
  transfers between devices with their start and end apart: 8 -> 8, of which waited for: 5 -> 5; matrix products, arithmetic and copies ran while one was open for 0% -> 0% of each run, Pallas kernels for 27% -> 28%
where the time goes in v11:
time: 29.2 us; the launch traced here: 29 us
  Pallas kernels  13.9 us (48%)
  waiting for transfers between devices  8.31 us (28%)
  starting transfers between devices  6.7 us (23%)
    pallas_call x7, Pallas kernels, call(): pl.pallas_call(body, out_shape=outs, in_specs=[spec(s) for s in spaces],...  13.1 us
    ppermute x2, waiting for transfers between devices, turned(): return lax.ppermute(array, 'tile', pairs)  3.69 us
    ppermute x1, waiting for transfers between devices, per_device(): lax.ppermute(even, 'tm', [(i, i + 1) for i in range(spans - 1)])  2.72 us
    ppermute x1, starting transfers between devices, per_device(): lax.ppermute(even, 'tm', [(i, i + 1) for i in range(spans - 1)])  2.05 us
    ppermute x2, starting transfers between devices, turned(): return lax.ppermute(array, 'tile', pairs)  1.81 us
    ppermute x1, waiting for transfers between devices, per_device(): arrived_odd = lax.ppermute(odd, ('tm', 'tile'), ring)  1.74 us
    ppermute x1, starting transfers between devices, per_device(): arrived_odd = lax.ppermute(odd, ('tm', 'tile'), ring)  1.56 us
    pallas_call x1, Pallas kernels, per_device(): pl.pallas_call(last_body, out_shape=jax.ShapeDtypeStruct((2, cells, out_c...  0.74 us
  transfers between devices with their start and end apart: 8, of which 5 were waited for; matrix products, arithmetic and copies ran while one was open for 0% of the time, Pallas kernels for 28%

profile of v11, /device:TPU:24, one launch (start us, length us, event | category | flops | bytes accessed | tf_op | source)
XLA Modules:
  0.0 29.0 jit_solution(5564909316567532440)
XLA Ops:
  0.0 1.0 %shard_map.82 = (f32[8,512]{1,0:T(8,128)S(1)}, bf16[320,512]{1,0:T(8,128)(2,1)S(1)}, bf16[160,512]{1,0:T(8,128)(2,1)S(1)}, bf16[160,512]{1,0:T(8,128)(2,1)S(1)}) custom-call(bf16[320,512]{1,0:T(8,128)(2,1)} %bitcast.6), custom_call_target="tpu_custom_call" | custom-call | flops 64 | bytes 1024 | tf_op jit(solution)/shard_map/pallas_call | solution.py:41
  1.1 1.0 %collective-permute-start = (f32[8,512]{1,0:T(8,128)S(1)}, f32[8,512]{1,0:T(8,128)S(1)}, u32[]{:S(2)}, u32[]{:S(2)}) collective-permute-start(f32[8,512]{1,0:T(8,128)S(1)} %get-tuple-element.44), channel_id=1, source_target_pairs={{0,3},{1,2},{2,1},{3,0},{4,7},{5,6},{6,5},{7,4},{8,11},{9,10},{10,... | collective-permute-start | bytes 49160 | tf_op jit(solution)/shard_map/ppermute | solution.py:365
  2.1 0.8 %collective-permute-start.3 = (bf16[320,512]{1,0:T(8,128)(2,1)S(1)}, bf16[320,512]{1,0:T(8,128)(2,1)S(1)}, u32[]{:S(2)}, u32[]{:S(2)}) collective-permute-start(bf16[320,512]{1,0:T(8,128)(2,1)S(1)} %get-tuple-element.41.own_ref), channel_id=1, source_target_pairs={{0,3},{1,2},{2,1},{3,0},{4,7},{5,6},{6,5},{7,4},{8,11},{9,10},{10,... | collective-permute-start | bytes 983048 | tf_op jit(solution)/shard_map/ppermute | solution.py:365
  2.9 1.5 %collective-permute-done = f32[8,512]{1,0:T(8,128)S(1)} collective-permute-done((f32[8,512]{1,0:T(8,128)S(1)}, f32[8,512]{1,0:T(8,128)S(1)}, u32[]{:S(2)}, u32[]{:S(2)}) %collective-permute-start) | collective-permute-done | bytes 16416 | tf_op jit(solution)/shard_map/ppermute | solution.py:365
  4.4 0.1 collective-permute-start.1
  4.5 0.4 %collective-permute-start.2 = (bf16[160,512]{1,0:T(8,128)(2,1)S(1)}, bf16[160,512]{1,0:T(8,128)(2,1)S(1)}, u32[]{:S(2)}, u32[]{:S(2)}) collective-permute-start(bf16[160,512]{1,0:T(8,128)(2,1)S(1)} %get-tuple-element.46), channel_id=1, source_target_pairs={{0,1},{1,0},{2,3},{3,2},{4,5},{5,4},{6,7},{7,6},{8,9},{9,8},{10,11... | collective-permute-start | bytes 491528 | tf_op jit(solution)/shard_map/ppermute | solution.py:382
  4.9 0.1 collective-permute-start.4
  5.0 1.4 %shard_map.83 = (f32[1,512]{1,0:T(1,128)S(1)}, bf16[512,512]{1,0:T(8,128)(2,1)S(1)}, bf16[512,512]{1,0:T(8,128)(2,1)S(1)}, bf16[512,512]{1,0:T(8,128)(2,1)S(1)}) custom-call(f32[16,512]{1,0:T(8,128)S(1)} %pad_maximum_fusion.refs_0_, f32[1,512]{1,0:T(1,128)} %bitcast.7, bf16[512,512]{1,0:T(8,128)(2,1)} %refs_2_.1, bf16[512,512]{1,0:T(8,128)(2,1)} %refs_3_.1, ...), custom_call_target="tpu_custom_call" | custom-call | flops 16 | bytes 1024 | tf_op jit(solution)/shard_map/pallas_call | solution.py:41
  6.4 0.0 collective-permute-done.4.refs_1_
  6.4 0.0 collective-permute-done.1.sib_first_ref
  6.5 0.0 collective-permute-done.2.sib_second_ref
  6.5 2.6 %shard_map.84 = (f32[8,512]{1,0:T(8,128)S(1)}, bf16[480,512]{1,0:T(8,128)(2,1)S(1)}, bf16[640,512]{1,0:T(8,128)(2,1)S(1)}, bf16[640,512]{1,0:T(8,128)(2,1)S(1)},...) custom-call(bf16[320,512]{1,0:T(8,128)(2,1)S(1)} %get-tuple-element., ...), custom_call_target="tpu_custom_call" | custom-call | flops 700000000 | bytes 1024 | tf_op jit(solution)/shard_map/pallas_call | solution.py:41
  9.1 2.2 %collective-permute-done.3.refs_0_ = bf16[320,512]{1,0:T(8,128)(2,1)S(1)} collective-permute-done((bf16[320,512]{1,0:T(8,128)(2,1)S(1)}, bf16[320,512]{1,0:T(8,128)(2,1)S(1)}, u32[]{:S(2)}, u32[]{:S(2)}) %collective-permute-start.3) | collective-permute-done | bytes 327712 | tf_op jit(solution)/shard_map/ppermute | solution.py:365
  11.3 0.7 %collective-permute-start.5 = (bf16[320,512]{1,0:T(8,128)(2,1)S(1)}, bf16[320,512]{1,0:T(8,128)(2,1)S(1)}, u32[]{:S(2)}, u32[]{:S(2)}) collective-permute-start(bf16[320,512]{1,0:T(8,128)(2,1)S(1)} %collective-permute-done.3.refs_0_), channel_id=1, source_target_pairs={{0,1},{1,0},{2,3},{3,2},{4,5},{5,4},{6,7},{7,6},{8,9},{9,8},{10,11... | collective-permute-start | bytes 983048 | tf_op jit(solution)/shard_map/ppermute | solution.py:430
  11.9 1.1 %shard_map.85 = (bf16[160,512]{1,0:T(8,128)(2,1)S(1)}, bf16[640,512]{1,0:T(8,128)(2,1)S(1)}, f32[640,128]{1,0:T(8,128)S(1)}, f32[640,128]{1,0:T(8,128)S(1)}, f32...) custom-call(bf16[320,512]{1,0:T(8,128)(2,1)S(1)} %collective-permute-done.3.refs_0_, ...), custom_call_target="tpu_custom_call" | custom-call | flops 32768 | bytes 1024 | tf_op jit(solution)/shard_map/pallas_call | solution.py:41
  13.0 0.2 collective-permute-done.5.block_ref
  13.2 4.1 %shard_map.86 = (bf16[304,256]{1,0:T(8,128)(2,1)S(1)}, bf16[336,256]{1,0:T(8,128)(2,1)S(1)}, f32[320,256]{1,0:T(8,128)S(1)}, bf16[640,1536]{1,0:T(8,128)(2,1)S(1)}, bf16[320,512]{1,0:T(8,128)(2,1)S(1)}) custom-call(bf16[320,512]{1,0:T(8,128)(2,1)S(1)} %get-tuple-element.41.own_ref, bf16[160,512]{1,0:T(8,128)(2,1)S(1)} %collective-permute-done.1.sib_first_ref, ...), custom_call_target="tpu_custom_call" | custom-call | flops 32768 | bytes 1024 | tf_op jit(solution)/shard_map/pallas_call | solution.py:41
  17.3 1.6 %collective-permute-start.6 = (bf16[336,256]{1,0:T(8,128)(2,1)S(1)}, bf16[336,256]{1,0:T(8,128)(2,1)S(1)}, u32[]{:S(2)}, u32[]{:S(2)}) collective-permute-start(bf16[336,256]{1,0:T(8,128)(2,1)S(1)} %get-tuple-element.73.own_ref), channel_id=1, source_target_pairs={{0,4},{1,5},{2,6},{3,7},{4,8},{5,9},{6,10},{7,11},{8,12},{9,13},{1... | collective-permute-start | bytes 516104 | tf_op jit(solution)/shard_map/ppermute | solution.py:466
  18.9 2.1 %collective-permute-start.7 = (bf16[304,256]{1,0:T(8,128)(2,1)S(1)}, bf16[304,256]{1,0:T(8,128)(2,1)S(1)}, u32[]{:S(2)}, u32[]{:S(2)}) collective-permute-start(bf16[304,256]{1,0:T(8,128)(2,1)S(1)} %get-tuple-element.74.own_ref), channel_id=1, source_target_pairs={{0,4},{4,8},{8,12},{12,16},{16,20},{20,24},{24,28},{1,5},{5,9},{9,... | collective-permute-start | bytes 466952 | tf_op jit(solution)/shard_map/ppermute | solution.py:467
  20.9 2.8 %shard_map.87.now_ref = f32[2,320,256]{2,1,0:T(8,128)S(1)} custom-call(bf16[640,1536]{1,0:T(8,128)(2,1)S(1)} %get-tuple-element.70.wide_ref, bf16[320,512]{1,0:T(8,128)(2,1)S(1)} %get-tuple-element.71.mid_ref, f32[320,256]{1,0:T(8,128)S(1)} %get-tuple-element.72.second_ref, bf16[3,3,1536,256]{3,2,1,0:T(8,128)(2,1)} %bitcast.5, bf16[512,256]{1,0:T(8,128)(2,1)} %skip_hbm_ref.1), custom_call_target="tpu_custom_call" | custom-call | flops 32768 | bytes 1024 | tf_op jit(solution)/shard_map/pallas_call | solution.py:41
  23.7 1.7 %collective-permute-done.6.arrived_ref = bf16[336,256]{1,0:T(8,128)(2,1)S(1)} collective-permute-done((bf16[336,256]{1,0:T(8,128)(2,1)S(1)}, bf16[336,256]{1,0:T(8,128)(2,1)S(1)}, u32[]{:S(2)}, u32[]{:S(2)}) %collective-permute-start.6) | collective-permute-done | bytes 172064 | tf_op jit(solution)/shard_map/ppermute | solution.py:466
  25.5 0.1 shard_map.88.odd_ref
  25.5 2.7 %collective-permute-done.7.arrived_ref = bf16[304,256]{1,0:T(8,128)(2,1)S(1)} collective-permute-done((bf16[304,256]{1,0:T(8,128)(2,1)S(1)}, bf16[304,256]{1,0:T(8,128)(2,1)S(1)}, u32[]{:S(2)}, u32[]{:S(2)}) %collective-permute-start.7) | collective-permute-done | bytes 155680 | tf_op jit(solution)/shard_map/ppermute | solution.py:467
  28.2 0.7 %shard_map.89 = bf16[2,320,256]{2,1,0:T(8,128)(2,1)} custom-call(bf16[336,256]{1,0:T(8,128)(2,1)S(1)} %shard_map.88.odd_ref, f32[2,320,256]{2,1,0:T(8,128)S(1)} %shard_map.87.now_ref, bf16[304,256]{1,0:T(8,128)(2,1)S(1)} %get-tuple-element.74.own_ref, bf16[304,256]{1,0:T(8,128)(2,1)S(1)} %collective-permute-done.7.arrived_ref), custom_call_target="tpu_custom_call" | custom-call | tf_op jit(solution)/shard_map/pallas_call | solution.py:483
  (1 shorter events, 0.0 us)
Async XLA Ops:
  1.1 3.3 %collective-permute-start = (f32[8,512]{1,0:T(8,128)S(1)}, f32[8,512]{1,0:T(8,128)S(1)}, u32[]{:S(2)}, u32[]{:S(2)}) collective-permute-start(f32[8,512]{1,0:T(8,128)S(1)} %get-tuple-element.44), channel_id=1, source_target_pairs={{0,3},{1,2},{2,1},{3,0},{4,7},{5,6},{6,5},{7,4},{8,11},{9,10},{10,... | collective-permute-start | bytes 49160 | tf_op jit(solution)/shard_map/ppermute | solution.py:365
  2.1 9.2 %collective-permute-start.3 = (bf16[320,512]{1,0:T(8,128)(2,1)S(1)}, bf16[320,512]{1,0:T(8,128)(2,1)S(1)}, u32[]{:S(2)}, u32[]{:S(2)}) collective-permute-start(bf16[320,512]{1,0:T(8,128)(2,1)S(1)} %get-tuple-element.41.own_ref), channel_id=1, source_target_pairs={{0,3},{1,2},{2,1},{3,0},{4,7},{5,6},{6,5},{7,4},{8,11},{9,10},{10,... | collective-permute-start | bytes 983048 | tf_op jit(solution)/shard_map/ppermute | solution.py:365
  4.4 2.1 %collective-permute-start.1 = (bf16[160,512]{1,0:T(8,128)(2,1)S(1)}, bf16[160,512]{1,0:T(8,128)(2,1)S(1)}, u32[]{:S(2)}, u32[]{:S(2)}) collective-permute-start(bf16[160,512]{1,0:T(8,128)(2,1)S(1)} %get-tuple-element.45), channel_id=1, source_target_pairs={{0,1},{1,0},{2,3},{3,2},{4,5},{5,4},{6,7},{7,6},{8,9},{9,8},{10,11... | collective-permute-start | bytes 491528 | tf_op jit(solution)/shard_map/ppermute | solution.py:382
  4.5 1.9 %collective-permute-start.2 = (bf16[160,512]{1,0:T(8,128)(2,1)S(1)}, bf16[160,512]{1,0:T(8,128)(2,1)S(1)}, u32[]{:S(2)}, u32[]{:S(2)}) collective-permute-start(bf16[160,512]{1,0:T(8,128)(2,1)S(1)} %get-tuple-element.46), channel_id=1, source_target_pairs={{0,1},{1,0},{2,3},{3,2},{4,5},{5,4},{6,7},{7,6},{8,9},{9,8},{10,11... | collective-permute-start | bytes 491528 | tf_op jit(solution)/shard_map/ppermute | solution.py:382
  4.9 1.5 %collective-permute-start.4 = (f32[16,512]{1,0:T(8,128)S(1)}, f32[16,512]{1,0:T(8,128)S(1)}, u32[]{:S(2)}, u32[]{:S(2)}) collective-permute-start(f32[16,512]{1,0:T(8,128)S(1)} %pad_maximum_fusion.refs_0_), channel_id=1, source_target_pairs={{0,1},{1,0},{2,3},{3,2},{4,5},{5,4},{6,7},{7,6},{8,9},{9,8},{10,11... | collective-permute-start | bytes 98312 | tf_op jit(solution)/shard_map/ppermute | solution.py:383
  11.3 1.9 %collective-permute-start.5 = (bf16[320,512]{1,0:T(8,128)(2,1)S(1)}, bf16[320,512]{1,0:T(8,128)(2,1)S(1)}, u32[]{:S(2)}, u32[]{:S(2)}) collective-permute-start(bf16[320,512]{1,0:T(8,128)(2,1)S(1)} %collective-permute-done.3.refs_0_), channel_id=1, source_target_pairs={{0,1},{1,0},{2,3},{3,2},{4,5},{5,4},{6,7},{7,6},{8,9},{9,8},{10,11... | collective-permute-start | bytes 983048 | tf_op jit(solution)/shard_map/ppermute | solution.py:430
  17.3 8.2 %collective-permute-start.6 = (bf16[336,256]{1,0:T(8,128)(2,1)S(1)}, bf16[336,256]{1,0:T(8,128)(2,1)S(1)}, u32[]{:S(2)}, u32[]{:S(2)}) collective-permute-start(bf16[336,256]{1,0:T(8,128)(2,1)S(1)} %get-tuple-element.73.own_ref), channel_id=1, source_target_pairs={{0,4},{1,5},{2,6},{3,7},{4,8},{5,9},{6,10},{7,11},{8,12},{9,13},{1... | collective-permute-start | bytes 516104 | tf_op jit(solution)/shard_map/ppermute | solution.py:466
  18.9 9.4 %collective-permute-start.7 = (bf16[304,256]{1,0:T(8,128)(2,1)S(1)}, bf16[304,256]{1,0:T(8,128)(2,1)S(1)}, u32[]{:S(2)}, u32[]{:S(2)}) collective-permute-start(bf16[304,256]{1,0:T(8,128)(2,1)S(1)} %get-tuple-element.74.own_ref), channel_id=1, source_target_pairs={{0,4},{4,8},{8,12},{12,16},{16,20},{20,24},{24,28},{1,5},{5,9},{9,... | collective-permute-start | bytes 466952 | tf_op jit(solution)/shard_map/ppermute | solution.py:467

commit v12 on v11

--- a/solution.py
+++ b/solution.py
@@ -13,7 +13,7 @@
 VMEM = pltpu.VMEM
 LIMIT = 12 * 1024 * 1024
 PIECES = 5
-MOVED = 16
+MOVED = 48
 STATS_COST = 1 << 6
 STAGE_COST = 1 << 4
 EARLY_COST = 7 * 10**8

time: 29.2 us -> 29.2 us (level)
    ppermute x1, waiting for transfers between devices: 2.72 us -> 2.36 us  [per_device(): lax.ppermute(even, 'tm', [(i, i + 1) for i in range(spans - 1)])]
    ppermute x1, waiting for transfers between devices: 1.74 us -> 2.09 us  [per_device(): arrived_odd = lax.ppermute(odd, ('tm', 'tile'), ring)]
where the time goes in v12:
time: 29.2 us; the launch traced here: 29 us
  Pallas kernels  13.9 us (48%)
  waiting for transfers between devices  8.3 us (28%)
  starting transfers between devices  6.7 us (23%)
    pallas_call x7, Pallas kernels, call(): pl.pallas_call(body, out_shape=outs, in_specs=[spec(s) for s in spaces],...  13.1 us
    ppermute x2, waiting for transfers between devices, turned(): return lax.ppermute(array, 'tile', pairs)  3.69 us
    ppermute x1, waiting for transfers between devices, per_device(): lax.ppermute(even, 'tm', [(i, i + 1) for i in range(spans - 1)])  2.36 us
    ppermute x1, waiting for transfers between devices, per_device(): arrived_odd = lax.ppermute(odd, ('tm', 'tile'), ring)  2.09 us
    ppermute x1, starting transfers between devices, per_device(): lax.ppermute(even, 'tm', [(i, i + 1) for i in range(spans - 1)])  2.05 us
    ppermute x2, starting transfers between devices, turned(): return lax.ppermute(array, 'tile', pairs)  1.81 us
    ppermute x1, starting transfers between devices, per_device(): arrived_odd = lax.ppermute(odd, ('tm', 'tile'), ring)  1.56 us
    pallas_call x1, Pallas kernels, per_device(): pl.pallas_call(last_body, out_shape=jax.ShapeDtypeStruct((2, cells, out_c...  0.74 us
  transfers between devices with their start and end apart: 8, of which 5 were waited for; matrix products, arithmetic and copies ran while one was open for 0% of the time, Pallas kernels for 28%

profile of v12, /device:TPU:24, one launch (start us, length us, event | category | flops | bytes accessed | tf_op | source)
XLA Modules:
  0.0 29.0 jit_solution(9445518855682466248)
XLA Ops:
  0.0 1.0 %shard_map.82 = (f32[8,512]{1,0:T(8,128)S(1)}, bf16[320,512]{1,0:T(8,128)(2,1)S(1)}, bf16[160,512]{1,0:T(8,128)(2,1)S(1)}, bf16[160,512]{1,0:T(8,128)(2,1)S(1)}) custom-call(bf16[320,512]{1,0:T(8,128)(2,1)} %bitcast.6), custom_call_target="tpu_custom_call" | custom-call | flops 64 | bytes 1024 | tf_op jit(solution)/shard_map/pallas_call | solution.py:41
  1.1 1.0 %collective-permute-start = (f32[8,512]{1,0:T(8,128)S(1)}, f32[8,512]{1,0:T(8,128)S(1)}, u32[]{:S(2)}, u32[]{:S(2)}) collective-permute-start(f32[8,512]{1,0:T(8,128)S(1)} %get-tuple-element.44), channel_id=1, source_target_pairs={{0,3},{1,2},{2,1},{3,0},{4,7},{5,6},{6,5},{7,4},{8,11},{9,10},{10,... | collective-permute-start | bytes 49160 | tf_op jit(solution)/shard_map/ppermute | solution.py:365
  2.1 0.8 %collective-permute-start.3 = (bf16[320,512]{1,0:T(8,128)(2,1)S(1)}, bf16[320,512]{1,0:T(8,128)(2,1)S(1)}, u32[]{:S(2)}, u32[]{:S(2)}) collective-permute-start(bf16[320,512]{1,0:T(8,128)(2,1)S(1)} %get-tuple-element.41.own_ref), channel_id=1, source_target_pairs={{0,3},{1,2},{2,1},{3,0},{4,7},{5,6},{6,5},{7,4},{8,11},{9,10},{10,... | collective-permute-start | bytes 983048 | tf_op jit(solution)/shard_map/ppermute | solution.py:365
  2.9 1.5 %collective-permute-done = f32[8,512]{1,0:T(8,128)S(1)} collective-permute-done((f32[8,512]{1,0:T(8,128)S(1)}, f32[8,512]{1,0:T(8,128)S(1)}, u32[]{:S(2)}, u32[]{:S(2)}) %collective-permute-start) | collective-permute-done | bytes 16416 | tf_op jit(solution)/shard_map/ppermute | solution.py:365
  4.4 0.1 collective-permute-start.1
  4.5 0.4 %collective-permute-start.2 = (bf16[160,512]{1,0:T(8,128)(2,1)S(1)}, bf16[160,512]{1,0:T(8,128)(2,1)S(1)}, u32[]{:S(2)}, u32[]{:S(2)}) collective-permute-start(bf16[160,512]{1,0:T(8,128)(2,1)S(1)} %get-tuple-element.46), channel_id=1, source_target_pairs={{0,1},{1,0},{2,3},{3,2},{4,5},{5,4},{6,7},{7,6},{8,9},{9,8},{10,11... | collective-permute-start | bytes 491528 | tf_op jit(solution)/shard_map/ppermute | solution.py:382
  4.9 0.1 collective-permute-start.4
  5.0 1.4 %shard_map.83 = (f32[1,512]{1,0:T(1,128)S(1)}, bf16[512,512]{1,0:T(8,128)(2,1)S(1)}, bf16[512,512]{1,0:T(8,128)(2,1)S(1)}, bf16[512,512]{1,0:T(8,128)(2,1)S(1)}) custom-call(f32[16,512]{1,0:T(8,128)S(1)} %pad_maximum_fusion.refs_0_, f32[1,512]{1,0:T(1,128)} %bitcast.7, bf16[512,512]{1,0:T(8,128)(2,1)} %refs_2_.1, bf16[512,512]{1,0:T(8,128)(2,1)} %refs_3_.1, ...), custom_call_target="tpu_custom_call" | custom-call | flops 16 | bytes 1024 | tf_op jit(solution)/shard_map/pallas_call | solution.py:41
  6.4 0.0 collective-permute-done.4.refs_1_
  6.4 0.0 collective-permute-done.1.sib_first_ref
  6.5 0.0 collective-permute-done.2.sib_second_ref
  6.5 2.6 %shard_map.84 = (f32[8,512]{1,0:T(8,128)S(1)}, bf16[480,512]{1,0:T(8,128)(2,1)S(1)}, bf16[640,512]{1,0:T(8,128)(2,1)S(1)}, bf16[640,512]{1,0:T(8,128)(2,1)S(1)},...) custom-call(bf16[320,512]{1,0:T(8,128)(2,1)S(1)} %get-tuple-element., ...), custom_call_target="tpu_custom_call" | custom-call | flops 700000000 | bytes 1024 | tf_op jit(solution)/shard_map/pallas_call | solution.py:41
  9.1 2.2 %collective-permute-done.3.refs_0_ = bf16[320,512]{1,0:T(8,128)(2,1)S(1)} collective-permute-done((bf16[320,512]{1,0:T(8,128)(2,1)S(1)}, bf16[320,512]{1,0:T(8,128)(2,1)S(1)}, u32[]{:S(2)}, u32[]{:S(2)}) %collective-permute-start.3) | collective-permute-done | bytes 327712 | tf_op jit(solution)/shard_map/ppermute | solution.py:365
  11.3 0.7 %collective-permute-start.5 = (bf16[320,512]{1,0:T(8,128)(2,1)S(1)}, bf16[320,512]{1,0:T(8,128)(2,1)S(1)}, u32[]{:S(2)}, u32[]{:S(2)}) collective-permute-start(bf16[320,512]{1,0:T(8,128)(2,1)S(1)} %collective-permute-done.3.refs_0_), channel_id=1, source_target_pairs={{0,1},{1,0},{2,3},{3,2},{4,5},{5,4},{6,7},{7,6},{8,9},{9,8},{10,11... | collective-permute-start | bytes 983048 | tf_op jit(solution)/shard_map/ppermute | solution.py:430
  11.9 1.1 %shard_map.85 = (bf16[160,512]{1,0:T(8,128)(2,1)S(1)}, bf16[640,512]{1,0:T(8,128)(2,1)S(1)}, f32[640,128]{1,0:T(8,128)S(1)}, f32[640,128]{1,0:T(8,128)S(1)}, f32...) custom-call(bf16[320,512]{1,0:T(8,128)(2,1)S(1)} %collective-permute-done.3.refs_0_, ...), custom_call_target="tpu_custom_call" | custom-call | flops 32768 | bytes 1024 | tf_op jit(solution)/shard_map/pallas_call | solution.py:41
  13.0 0.2 collective-permute-done.5.block_ref
  13.2 4.1 %shard_map.86 = (bf16[272,256]{1,0:T(8,128)(2,1)S(1)}, bf16[368,256]{1,0:T(8,128)(2,1)S(1)}, f32[320,256]{1,0:T(8,128)S(1)}, bf16[640,1536]{1,0:T(8,128)(2,1)S(1)}, bf16[320,512]{1,0:T(8,128)(2,1)S(1)}) custom-call(bf16[320,512]{1,0:T(8,128)(2,1)S(1)} %get-tuple-element.41.own_ref, bf16[160,512]{1,0:T(8,128)(2,1)S(1)} %collective-permute-done.1.sib_first_ref, ...), custom_call_target="tpu_custom_call" | custom-call | flops 32768 | bytes 1024 | tf_op jit(solution)/shard_map/pallas_call | solution.py:41
  17.3 1.6 %collective-permute-start.6 = (bf16[368,256]{1,0:T(8,128)(2,1)S(1)}, bf16[368,256]{1,0:T(8,128)(2,1)S(1)}, u32[]{:S(2)}, u32[]{:S(2)}) collective-permute-start(bf16[368,256]{1,0:T(8,128)(2,1)S(1)} %get-tuple-element.73.own_ref), channel_id=1, source_target_pairs={{0,4},{1,5},{2,6},{3,7},{4,8},{5,9},{6,10},{7,11},{8,12},{9,13},{1... | collective-permute-start | bytes 565256 | tf_op jit(solution)/shard_map/ppermute | solution.py:466
  18.9 2.1 %collective-permute-start.7 = (bf16[272,256]{1,0:T(8,128)(2,1)S(1)}, bf16[272,256]{1,0:T(8,128)(2,1)S(1)}, u32[]{:S(2)}, u32[]{:S(2)}) collective-permute-start(bf16[272,256]{1,0:T(8,128)(2,1)S(1)} %get-tuple-element.74.own_ref), channel_id=1, source_target_pairs={{0,4},{4,8},{8,12},{12,16},{16,20},{20,24},{24,28},{1,5},{5,9},{9,... | collective-permute-start | bytes 417800 | tf_op jit(solution)/shard_map/ppermute | solution.py:467
  20.9 2.8 %shard_map.87.now_ref = f32[2,320,256]{2,1,0:T(8,128)S(1)} custom-call(bf16[640,1536]{1,0:T(8,128)(2,1)S(1)} %get-tuple-element.70.wide_ref, bf16[320,512]{1,0:T(8,128)(2,1)S(1)} %get-tuple-element.71.mid_ref, f32[320,256]{1,0:T(8,128)S(1)} %get-tuple-element.72.second_ref, bf16[3,3,1536,256]{3,2,1,0:T(8,128)(2,1)} %bitcast.5, bf16[512,256]{1,0:T(8,128)(2,1)} %skip_hbm_ref.1), custom_call_target="tpu_custom_call" | custom-call | flops 32768 | bytes 1024 | tf_op jit(solution)/shard_map/pallas_call | solution.py:41
  23.7 2.1 %collective-permute-done.6.arrived_ref = bf16[368,256]{1,0:T(8,128)(2,1)S(1)} collective-permute-done((bf16[368,256]{1,0:T(8,128)(2,1)S(1)}, bf16[368,256]{1,0:T(8,128)(2,1)S(1)}, u32[]{:S(2)}, u32[]{:S(2)}) %collective-permute-start.6) | collective-permute-done | bytes 188448 | tf_op jit(solution)/shard_map/ppermute | solution.py:466
  25.8 0.1 shard_map.88.odd_ref
  25.9 2.4 %collective-permute-done.7.arrived_ref = bf16[272,256]{1,0:T(8,128)(2,1)S(1)} collective-permute-done((bf16[272,256]{1,0:T(8,128)(2,1)S(1)}, bf16[272,256]{1,0:T(8,128)(2,1)S(1)}, u32[]{:S(2)}, u32[]{:S(2)}) %collective-permute-start.7) | collective-permute-done | bytes 139296 | tf_op jit(solution)/shard_map/ppermute | solution.py:467
  28.2 0.7 %shard_map.89 = bf16[2,320,256]{2,1,0:T(8,128)(2,1)} custom-call(bf16[368,256]{1,0:T(8,128)(2,1)S(1)} %shard_map.88.odd_ref, f32[2,320,256]{2,1,0:T(8,128)S(1)} %shard_map.87.now_ref, bf16[272,256]{1,0:T(8,128)(2,1)S(1)} %get-tuple-element.74.own_ref, bf16[272,256]{1,0:T(8,128)(2,1)S(1)} %collective-permute-done.7.arrived_ref), custom_call_target="tpu_custom_call" | custom-call | tf_op jit(solution)/shard_map/pallas_call | solution.py:483
  (1 shorter events, 0.0 us)
Async XLA Ops:
  1.1 3.3 %collective-permute-start = (f32[8,512]{1,0:T(8,128)S(1)}, f32[8,512]{1,0:T(8,128)S(1)}, u32[]{:S(2)}, u32[]{:S(2)}) collective-permute-start(f32[8,512]{1,0:T(8,128)S(1)} %get-tuple-element.44), channel_id=1, source_target_pairs={{0,3},{1,2},{2,1},{3,0},{4,7},{5,6},{6,5},{7,4},{8,11},{9,10},{10,... | collective-permute-start | bytes 49160 | tf_op jit(solution)/shard_map/ppermute | solution.py:365
  2.1 9.2 %collective-permute-start.3 = (bf16[320,512]{1,0:T(8,128)(2,1)S(1)}, bf16[320,512]{1,0:T(8,128)(2,1)S(1)}, u32[]{:S(2)}, u32[]{:S(2)}) collective-permute-start(bf16[320,512]{1,0:T(8,128)(2,1)S(1)} %get-tuple-element.41.own_ref), channel_id=1, source_target_pairs={{0,3},{1,2},{2,1},{3,0},{4,7},{5,6},{6,5},{7,4},{8,11},{9,10},{10,... | collective-permute-start | bytes 983048 | tf_op jit(solution)/shard_map/ppermute | solution.py:365
  4.4 2.1 %collective-permute-start.1 = (bf16[160,512]{1,0:T(8,128)(2,1)S(1)}, bf16[160,512]{1,0:T(8,128)(2,1)S(1)}, u32[]{:S(2)}, u32[]{:S(2)}) collective-permute-start(bf16[160,512]{1,0:T(8,128)(2,1)S(1)} %get-tuple-element.45), channel_id=1, source_target_pairs={{0,1},{1,0},{2,3},{3,2},{4,5},{5,4},{6,7},{7,6},{8,9},{9,8},{10,11... | collective-permute-start | bytes 491528 | tf_op jit(solution)/shard_map/ppermute | solution.py:382
  4.5 1.9 %collective-permute-start.2 = (bf16[160,512]{1,0:T(8,128)(2,1)S(1)}, bf16[160,512]{1,0:T(8,128)(2,1)S(1)}, u32[]{:S(2)}, u32[]{:S(2)}) collective-permute-start(bf16[160,512]{1,0:T(8,128)(2,1)S(1)} %get-tuple-element.46), channel_id=1, source_target_pairs={{0,1},{1,0},{2,3},{3,2},{4,5},{5,4},{6,7},{7,6},{8,9},{9,8},{10,11... | collective-permute-start | bytes 491528 | tf_op jit(solution)/shard_map/ppermute | solution.py:382
  4.9 1.5 %collective-permute-start.4 = (f32[16,512]{1,0:T(8,128)S(1)}, f32[16,512]{1,0:T(8,128)S(1)}, u32[]{:S(2)}, u32[]{:S(2)}) collective-permute-start(f32[16,512]{1,0:T(8,128)S(1)} %pad_maximum_fusion.refs_0_), channel_id=1, source_target_pairs={{0,1},{1,0},{2,3},{3,2},{4,5},{5,4},{6,7},{7,6},{8,9},{9,8},{10,11... | collective-permute-start | bytes 98312 | tf_op jit(solution)/shard_map/ppermute | solution.py:383
  11.3 1.9 %collective-permute-start.5 = (bf16[320,512]{1,0:T(8,128)(2,1)S(1)}, bf16[320,512]{1,0:T(8,128)(2,1)S(1)}, u32[]{:S(2)}, u32[]{:S(2)}) collective-permute-start(bf16[320,512]{1,0:T(8,128)(2,1)S(1)} %collective-permute-done.3.refs_0_), channel_id=1, source_target_pairs={{0,1},{1,0},{2,3},{3,2},{4,5},{5,4},{6,7},{7,6},{8,9},{9,8},{10,11... | collective-permute-start | bytes 983048 | tf_op jit(solution)/shard_map/ppermute | solution.py:430
  17.3 8.5 %collective-permute-start.6 = (bf16[368,256]{1,0:T(8,128)(2,1)S(1)}, bf16[368,256]{1,0:T(8,128)(2,1)S(1)}, u32[]{:S(2)}, u32[]{:S(2)}) collective-permute-start(bf16[368,256]{1,0:T(8,128)(2,1)S(1)} %get-tuple-element.73.own_ref), channel_id=1, source_target_pairs={{0,4},{1,5},{2,6},{3,7},{4,8},{5,9},{6,10},{7,11},{8,12},{9,13},{1... | collective-permute-start | bytes 565256 | tf_op jit(solution)/shard_map/ppermute | solution.py:466
  18.9 9.4 %collective-permute-start.7 = (bf16[272,256]{1,0:T(8,128)(2,1)S(1)}, bf16[272,256]{1,0:T(8,128)(2,1)S(1)}, u32[]{:S(2)}, u32[]{:S(2)}) collective-permute-start(bf16[272,256]{1,0:T(8,128)(2,1)S(1)} %get-tuple-element.74.own_ref), channel_id=1, source_target_pairs={{0,4},{4,8},{8,12},{12,16},{16,20},{20,24},{24,28},{1,5},{5,9},{9,... | collective-permute-start | bytes 417800 | tf_op jit(solution)/shard_map/ppermute | solution.py:467

commit v13 on v10

--- a/solution.py
+++ b/solution.py
@@ -12,7 +12,7 @@
 F32 = jnp.float32
 VMEM = pltpu.VMEM
 LIMIT = 12 * 1024 * 1024
-PIECES = 5
+PIECES = 10
 STATS_COST = 1 << 6
 STAGE_COST = 1 << 4
 EARLY_COST = 7 * 10**8

time: 29.2 us -> 29.2 us (level)
  no operation moved by 1% of the time
where the time goes in v13:
time: 29.2 us; the launch traced here: 29 us
  Pallas kernels  13.9 us (48%)
  waiting for transfers between devices  8.28 us (28%)
  starting transfers between devices  6.74 us (23%)
    pallas_call x7, Pallas kernels, call(): pl.pallas_call(body, out_shape=outs, in_specs=[spec(s) for s in spaces],...  13.1 us
    ppermute x2, waiting for transfers between devices, turned(): return lax.ppermute(array, 'tile', pairs)  3.69 us
    ppermute x1, waiting for transfers between devices, per_device(): lax.ppermute(even, 'tm', [(i, i + 1) for i in range(spans - 1)])  3.12 us
    ppermute x1, starting transfers between devices, per_device(): lax.ppermute(even, 'tm', [(i, i + 1) for i in range(spans - 1)])  2.09 us
    ppermute x2, starting transfers between devices, turned(): return lax.ppermute(array, 'tile', pairs)  1.81 us
    ppermute x1, starting transfers between devices, per_device(): lax.ppermute(odd, 'tm', [(i, (i + 1) % spans) for i in range(spans)])  1.56 us
    ppermute x1, waiting for transfers between devices, per_device(): lax.ppermute(odd, 'tm', [(i, (i + 1) % spans) for i in range(spans)])  1.32 us
    pallas_call x1, Pallas kernels, per_device(): pl.pallas_call(last_body, out_shape=jax.ShapeDtypeStruct((2, cells, out_c...  0.74 us
  transfers between devices with their start and end apart: 8, of which 5 were waited for; matrix products, arithmetic and copies ran while one was open for 0% of the time, Pallas kernels for 27%

profile of v13, /device:TPU:24, one launch (start us, length us, event | category | flops | bytes accessed | tf_op | source)
XLA Modules:
  0.0 29.0 jit_solution(5609738264258611022)
XLA Ops:
  0.0 1.0 %shard_map.82 = (f32[8,512]{1,0:T(8,128)S(1)}, bf16[320,512]{1,0:T(8,128)(2,1)S(1)}, bf16[160,512]{1,0:T(8,128)(2,1)S(1)}, bf16[160,512]{1,0:T(8,128)(2,1)S(1)}) custom-call(bf16[320,512]{1,0:T(8,128)(2,1)} %bitcast.6), custom_call_target="tpu_custom_call" | custom-call | flops 64 | bytes 1024 | tf_op jit(solution)/shard_map/pallas_call | solution.py:40
  1.0 1.0 %collective-permute-start = (f32[8,512]{1,0:T(8,128)S(1)}, f32[8,512]{1,0:T(8,128)S(1)}, u32[]{:S(2)}, u32[]{:S(2)}) collective-permute-start(f32[8,512]{1,0:T(8,128)S(1)} %get-tuple-element.44), channel_id=1, source_target_pairs={{0,3},{1,2},{2,1},{3,0},{4,7},{5,6},{6,5},{7,4},{8,11},{9,10},{10,... | collective-permute-start | bytes 49160 | tf_op jit(solution)/shard_map/ppermute | solution.py:357
  2.1 0.8 %collective-permute-start.3 = (bf16[320,512]{1,0:T(8,128)(2,1)S(1)}, bf16[320,512]{1,0:T(8,128)(2,1)S(1)}, u32[]{:S(2)}, u32[]{:S(2)}) collective-permute-start(bf16[320,512]{1,0:T(8,128)(2,1)S(1)} %get-tuple-element.41.own_ref), channel_id=1, source_target_pairs={{0,3},{1,2},{2,1},{3,0},{4,7},{5,6},{6,5},{7,4},{8,11},{9,10},{10,... | collective-permute-start | bytes 983048 | tf_op jit(solution)/shard_map/ppermute | solution.py:357
  2.9 1.5 %collective-permute-done = f32[8,512]{1,0:T(8,128)S(1)} collective-permute-done((f32[8,512]{1,0:T(8,128)S(1)}, f32[8,512]{1,0:T(8,128)S(1)}, u32[]{:S(2)}, u32[]{:S(2)}) %collective-permute-start) | collective-permute-done | bytes 16416 | tf_op jit(solution)/shard_map/ppermute | solution.py:357
  4.4 0.1 collective-permute-start.1
  4.5 0.4 %collective-permute-start.2 = (bf16[160,512]{1,0:T(8,128)(2,1)S(1)}, bf16[160,512]{1,0:T(8,128)(2,1)S(1)}, u32[]{:S(2)}, u32[]{:S(2)}) collective-permute-start(bf16[160,512]{1,0:T(8,128)(2,1)S(1)} %get-tuple-element.46), channel_id=1, source_target_pairs={{0,1},{1,0},{2,3},{3,2},{4,5},{5,4},{6,7},{7,6},{8,9},{9,8},{10,11... | collective-permute-start | bytes 491528 | tf_op jit(solution)/shard_map/ppermute | solution.py:374
  4.9 0.1 collective-permute-start.4
  5.0 1.4 %shard_map.83 = (f32[1,512]{1,0:T(1,128)S(1)}, bf16[512,512]{1,0:T(8,128)(2,1)S(1)}, bf16[512,512]{1,0:T(8,128)(2,1)S(1)}, bf16[512,512]{1,0:T(8,128)(2,1)S(1)}) custom-call(f32[16,512]{1,0:T(8,128)S(1)} %pad_maximum_fusion.refs_0_, f32[1,512]{1,0:T(1,128)} %bitcast.7, bf16[512,512]{1,0:T(8,128)(2,1)} %refs_2_.1, bf16[512,512]{1,0:T(8,128)(2,1)} %refs_3_.1, ...), custom_call_target="tpu_custom_call" | custom-call | flops 16 | bytes 1024 | tf_op jit(solution)/shard_map/pallas_call | solution.py:40
  6.4 0.0 collective-permute-done.4.refs_1_
  6.4 0.0 collective-permute-done.1.sib_first_ref
  6.4 0.0 collective-permute-done.2.sib_second_ref
  6.5 2.6 %shard_map.84 = (f32[8,512]{1,0:T(8,128)S(1)}, bf16[480,512]{1,0:T(8,128)(2,1)S(1)}, bf16[640,512]{1,0:T(8,128)(2,1)S(1)}, bf16[640,512]{1,0:T(8,128)(2,1)S(1)},...) custom-call(bf16[320,512]{1,0:T(8,128)(2,1)S(1)} %get-tuple-element., ...), custom_call_target="tpu_custom_call" | custom-call | flops 700000000 | bytes 1024 | tf_op jit(solution)/shard_map/pallas_call | solution.py:40
  9.1 2.2 %collective-permute-done.3.refs_0_ = bf16[320,512]{1,0:T(8,128)(2,1)S(1)} collective-permute-done((bf16[320,512]{1,0:T(8,128)(2,1)S(1)}, bf16[320,512]{1,0:T(8,128)(2,1)S(1)}, u32[]{:S(2)}, u32[]{:S(2)}) %collective-permute-start.3) | collective-permute-done | bytes 327712 | tf_op jit(solution)/shard_map/ppermute | solution.py:357
  11.2 0.7 %collective-permute-start.5 = (bf16[320,512]{1,0:T(8,128)(2,1)S(1)}, bf16[320,512]{1,0:T(8,128)(2,1)S(1)}, u32[]{:S(2)}, u32[]{:S(2)}) collective-permute-start(bf16[320,512]{1,0:T(8,128)(2,1)S(1)} %collective-permute-done.3.refs_0_), channel_id=1, source_target_pairs={{0,1},{1,0},{2,3},{3,2},{4,5},{5,4},{6,7},{7,6},{8,9},{9,8},{10,11... | collective-permute-start | bytes 983048 | tf_op jit(solution)/shard_map/ppermute | solution.py:422
  11.9 1.1 %shard_map.85 = (bf16[160,512]{1,0:T(8,128)(2,1)S(1)}, bf16[640,512]{1,0:T(8,128)(2,1)S(1)}, f32[640,128]{1,0:T(8,128)S(1)}, f32[640,128]{1,0:T(8,128)S(1)}, f32...) custom-call(bf16[320,512]{1,0:T(8,128)(2,1)S(1)} %collective-permute-done.3.refs_0_, ...), custom_call_target="tpu_custom_call" | custom-call | flops 32768 | bytes 1024 | tf_op jit(solution)/shard_map/pallas_call | solution.py:40
  13.0 0.2 collective-permute-done.5.block_ref
  13.2 4.1 %shard_map.86 = (bf16[320,256]{1,0:T(8,128)(2,1)S(1)}, bf16[320,256]{1,0:T(8,128)(2,1)S(1)}, f32[320,256]{1,0:T(8,128)S(1)}, bf16[640,1536]{1,0:T(8,128)(2,1)S(1)}, bf16[320,512]{1,0:T(8,128)(2,1)S(1)}) custom-call(bf16[320,512]{1,0:T(8,128)(2,1)S(1)} %get-tuple-element.41.own_ref, bf16[160,512]{1,0:T(8,128)(2,1)S(1)} %collective-permute-done.1.sib_first_ref, ...), custom_call_target="tpu_custom_call" | custom-call | flops 32768 | bytes 1024 | tf_op jit(solution)/shard_map/pallas_call | solution.py:40
  17.3 1.6 %collective-permute-start.6 = (bf16[320,256]{1,0:T(8,128)(2,1)S(1)}, bf16[320,256]{1,0:T(8,128)(2,1)S(1)}, u32[]{:S(2)}, u32[]{:S(2)}) collective-permute-start(bf16[320,256]{1,0:T(8,128)(2,1)S(1)} %get-tuple-element.73.own_ref), channel_id=1, source_target_pairs={{0,4},{4,8},{8,12},{12,16},{16,20},{20,24},{24,28},{28,0},{1,5},{5... | collective-permute-start | bytes 491528 | tf_op jit(solution)/shard_map/ppermute | solution.py:453
  18.8 2.1 %collective-permute-start.7 = (bf16[320,256]{1,0:T(8,128)(2,1)S(1)}, bf16[320,256]{1,0:T(8,128)(2,1)S(1)}, u32[]{:S(2)}, u32[]{:S(2)}) collective-permute-start(bf16[320,256]{1,0:T(8,128)(2,1)S(1)} %get-tuple-element.74.own_ref), channel_id=1, source_target_pairs={{0,4},{4,8},{8,12},{12,16},{16,20},{20,24},{24,28},{1,5},{5,9},{9,... | collective-permute-start | bytes 491528 | tf_op jit(solution)/shard_map/ppermute | solution.py:454
  20.9 2.8 %shard_map.87.now_ref = f32[2,320,256]{2,1,0:T(8,128)S(1)} custom-call(bf16[640,1536]{1,0:T(8,128)(2,1)S(1)} %get-tuple-element.70.wide_ref, bf16[320,512]{1,0:T(8,128)(2,1)S(1)} %get-tuple-element.71.mid_ref, f32[320,256]{1,0:T(8,128)S(1)} %get-tuple-element.72.second_ref, bf16[3,3,1536,256]{3,2,1,0:T(8,128)(2,1)} %bitcast.5, bf16[512,256]{1,0:T(8,128)(2,1)} %skip_hbm_ref.1), custom_call_target="tpu_custom_call" | custom-call | flops 32768 | bytes 1024 | tf_op jit(solution)/shard_map/pallas_call | solution.py:40
  23.7 1.3 %collective-permute-done.6.arrived_ref = bf16[320,256]{1,0:T(8,128)(2,1)S(1)} collective-permute-done((bf16[320,256]{1,0:T(8,128)(2,1)S(1)}, bf16[320,256]{1,0:T(8,128)(2,1)S(1)}, u32[]{:S(2)}, u32[]{:S(2)}) %collective-permute-start.6) | collective-permute-done | bytes 163872 | tf_op jit(solution)/shard_map/ppermute | solution.py:453
  25.1 3.1 %collective-permute-done.7.arrived_ref = bf16[320,256]{1,0:T(8,128)(2,1)S(1)} collective-permute-done((bf16[320,256]{1,0:T(8,128)(2,1)S(1)}, bf16[320,256]{1,0:T(8,128)(2,1)S(1)}, u32[]{:S(2)}, u32[]{:S(2)}) %collective-permute-start.7) | collective-permute-done | bytes 163872 | tf_op jit(solution)/shard_map/ppermute | solution.py:454
  28.2 0.7 %shard_map.89 = bf16[2,320,256]{2,1,0:T(8,128)(2,1)} custom-call(bf16[320,256]{1,0:T(8,128)(2,1)S(1)} %shard_map.88.odd_ref, f32[2,320,256]{2,1,0:T(8,128)S(1)} %shard_map.87.now_ref, bf16[320,256]{1,0:T(8,128)(2,1)S(1)} %get-tuple-element.74.own_ref, bf16[320,256]{1,0:T(8,128)(2,1)S(1)} %collective-permute-done.7.arrived_ref), custom_call_target="tpu_custom_call" | custom-call | tf_op jit(solution)/shard_map/pallas_call | solution.py:471
  (2 shorter events, 0.0 us)
Async XLA Ops:
  1.0 3.3 %collective-permute-start = (f32[8,512]{1,0:T(8,128)S(1)}, f32[8,512]{1,0:T(8,128)S(1)}, u32[]{:S(2)}, u32[]{:S(2)}) collective-permute-start(f32[8,512]{1,0:T(8,128)S(1)} %get-tuple-element.44), channel_id=1, source_target_pairs={{0,3},{1,2},{2,1},{3,0},{4,7},{5,6},{6,5},{7,4},{8,11},{9,10},{10,... | collective-permute-start | bytes 49160 | tf_op jit(solution)/shard_map/ppermute | solution.py:357
  2.1 9.2 %collective-permute-start.3 = (bf16[320,512]{1,0:T(8,128)(2,1)S(1)}, bf16[320,512]{1,0:T(8,128)(2,1)S(1)}, u32[]{:S(2)}, u32[]{:S(2)}) collective-permute-start(bf16[320,512]{1,0:T(8,128)(2,1)S(1)} %get-tuple-element.41.own_ref), channel_id=1, source_target_pairs={{0,3},{1,2},{2,1},{3,0},{4,7},{5,6},{6,5},{7,4},{8,11},{9,10},{10,... | collective-permute-start | bytes 983048 | tf_op jit(solution)/shard_map/ppermute | solution.py:357
  4.4 2.1 %collective-permute-start.1 = (bf16[160,512]{1,0:T(8,128)(2,1)S(1)}, bf16[160,512]{1,0:T(8,128)(2,1)S(1)}, u32[]{:S(2)}, u32[]{:S(2)}) collective-permute-start(bf16[160,512]{1,0:T(8,128)(2,1)S(1)} %get-tuple-element.45), channel_id=1, source_target_pairs={{0,1},{1,0},{2,3},{3,2},{4,5},{5,4},{6,7},{7,6},{8,9},{9,8},{10,11... | collective-permute-start | bytes 491528 | tf_op jit(solution)/shard_map/ppermute | solution.py:374
  4.5 1.9 %collective-permute-start.2 = (bf16[160,512]{1,0:T(8,128)(2,1)S(1)}, bf16[160,512]{1,0:T(8,128)(2,1)S(1)}, u32[]{:S(2)}, u32[]{:S(2)}) collective-permute-start(bf16[160,512]{1,0:T(8,128)(2,1)S(1)} %get-tuple-element.46), channel_id=1, source_target_pairs={{0,1},{1,0},{2,3},{3,2},{4,5},{5,4},{6,7},{7,6},{8,9},{9,8},{10,11... | collective-permute-start | bytes 491528 | tf_op jit(solution)/shard_map/ppermute | solution.py:374
  4.9 1.5 %collective-permute-start.4 = (f32[16,512]{1,0:T(8,128)S(1)}, f32[16,512]{1,0:T(8,128)S(1)}, u32[]{:S(2)}, u32[]{:S(2)}) collective-permute-start(f32[16,512]{1,0:T(8,128)S(1)} %pad_maximum_fusion.refs_0_), channel_id=1, source_target_pairs={{0,1},{1,0},{2,3},{3,2},{4,5},{5,4},{6,7},{7,6},{8,9},{9,8},{10,11... | collective-permute-start | bytes 98312 | tf_op jit(solution)/shard_map/ppermute | solution.py:375
  11.2 1.9 %collective-permute-start.5 = (bf16[320,512]{1,0:T(8,128)(2,1)S(1)}, bf16[320,512]{1,0:T(8,128)(2,1)S(1)}, u32[]{:S(2)}, u32[]{:S(2)}) collective-permute-start(bf16[320,512]{1,0:T(8,128)(2,1)S(1)} %collective-permute-done.3.refs_0_), channel_id=1, source_target_pairs={{0,1},{1,0},{2,3},{3,2},{4,5},{5,4},{6,7},{7,6},{8,9},{9,8},{10,11... | collective-permute-start | bytes 983048 | tf_op jit(solution)/shard_map/ppermute | solution.py:422
  17.3 7.8 %collective-permute-start.6 = (bf16[320,256]{1,0:T(8,128)(2,1)S(1)}, bf16[320,256]{1,0:T(8,128)(2,1)S(1)}, u32[]{:S(2)}, u32[]{:S(2)}) collective-permute-start(bf16[320,256]{1,0:T(8,128)(2,1)S(1)} %get-tuple-element.73.own_ref), channel_id=1, source_target_pairs={{0,4},{4,8},{8,12},{12,16},{16,20},{20,24},{24,28},{28,0},{1,5},{5... | collective-permute-start | bytes 491528 | tf_op jit(solution)/shard_map/ppermute | solution.py:453
  18.8 9.4 %collective-permute-start.7 = (bf16[320,256]{1,0:T(8,128)(2,1)S(1)}, bf16[320,256]{1,0:T(8,128)(2,1)S(1)}, u32[]{:S(2)}, u32[]{:S(2)}) collective-permute-start(bf16[320,256]{1,0:T(8,128)(2,1)S(1)} %get-tuple-element.74.own_ref), channel_id=1, source_target_pairs={{0,4},{4,8},{8,12},{12,16},{16,20},{20,24},{24,28},{1,5},{5,9},{9,... | collective-permute-start | bytes 491528 | tf_op jit(solution)/shard_map/ppermute | solution.py:454
